TPU v7x, 128 devices: a whole 4x4x4 slice. The times are simulated.
128 devices in a mesh: seq: 16 (over z, y_lo, core), head: 8 (over x, y_hi).
Axes of the slice: x: 4, y: 4 (y_hi: 2, y_lo: 2; y = y_hi * 2 + y_lo), z: 4, core: 2. Of those that a mesh axis runs over, the one named last changes fastest.
Arguments:
- context_hidden: bfloat16 [32, 1024, 8192], P(None, ('seq', 'head')), may hold values from -25 to 25
- norm_gain: float32 [8192], replicated, may hold values from 0.25 to 1.75
- kv_weight: bfloat16 [2, 8192, 1024], P(None, 'seq', 'head'), may hold values from -0.0625 to 0.0625
- queries: bfloat16 [4, 32, 8192], P(None, None, 'head'), may hold values from -12 to 12
- new_kv: bfloat16 [2, 4, 32, 1024], P(None, None, None, 'head'), may hold values from -12 to 12
- lengths: int32 [32], replicated, may hold values from 1 to 1024, 16384 in all
- slab_start: int32 [32], replicated, may hold values from 0 to 130043
Outputs:
- k_cache: bfloat16 [32, 1024, 1024], P(None, 'seq', 'head')
- v_cache: bfloat16 [32, 1024, 1024], P(None, 'seq', 'head')
- attention: bfloat16 [4, 32, 8192], P(None, 'seq', 'head')
Inputs may be any that keep to these rules, and one draw needn't show every extreme that they name: `lengths`: they sum to 16384, and some session reaches 1024.
All inputs are finite; a program needn't handle non-finite values.
Results may differ from a plain program's by a relative error of at most 0.013.
Values may be sent and summed in bfloat16 or wider, within the bound.
No kernel may reach another device: no remote copies, remote signals or barrier semaphores. Data moves between devices by JAX's collectives and lax.ppermute only.
A program may use at most 128 MiB of HBM per device.

v0:
```python
import math

import jax
import jax.numpy as jnp
from jax import lax
from jax.sharding import PartitionSpec as P

HQ = 64
KVH = 8
HD = 128
STEPS = 4


def merged_2(value, axis, join):
    pieces = jax.tree.map(lambda part: lax.all_gather(part, axis), value)
    head = jax.tree.map(lambda part: part[0], pieces)
    tail = jax.tree.map(lambda part: part[1:], pieces)
    so_far, _ = lax.scan(lambda so_far, slab: (join(so_far, slab), None), head, tail)
    return so_far


def rope_freqs():
    indices = jnp.arange(HD // 2, dtype=jnp.float32)
    base_freq = jnp.exp(-2.0 * indices / HD * math.log(500000.0))
    wavelength = 2.0 * math.pi / base_freq
    blend_weight = (8192.0 / wavelength - 1.0) / 3.0
    middle = (1.0 - blend_weight) * base_freq / 8.0 + blend_weight * base_freq
    return jnp.where(
        wavelength > 8192.0, base_freq / 8.0, jnp.where(wavelength < 2048.0, base_freq, middle)
    )


def rotate(vectors, position, freqs):
    angles = position.astype(jnp.float32)[..., None, None] * freqs
    half_width = vectors.shape[-1] // 2
    first_half = vectors[..., :half_width]
    second = vectors[..., half_width:]
    cosine = jnp.cos(angles)
    sine_part = jnp.sin(angles)
    return jnp.concatenate(
        [first_half * cosine - second * sine_part, second * cosine + first_half * sine_part],
        axis=-1,
    )


def normalize(hidden, norm_gain):
    widened = hidden.astype(jnp.float32)
    rescale = lax.rsqrt(jnp.mean(widened * widened, axis=-1, keepdims=True) + 1e-05)
    return (widened * rescale * norm_gain).astype(jnp.bfloat16)


def combine_parts(earlier, later):
    peak_first, sum_first, mix_first = earlier
    peak_second, sum_second, mix_second = later
    peak_score = jnp.maximum(peak_first, peak_second)
    weight_first = jnp.exp(peak_first - peak_score)
    weight_second = jnp.exp(peak_second - peak_score)
    weight_sum = sum_first * weight_first + sum_second * weight_second
    mixture = mix_first * weight_first[..., None] + mix_second * weight_second[..., None]
    return (peak_score, weight_sum, mixture)


def shards(context_hidden, norm_gain, kv_weight, queries, new_kv, lengths, slab_start):
    freqs = rope_freqs()
    seq_count = lax.axis_size("seq")
    head_count = lax.axis_size("head")
    seq_index = lax.axis_index("seq")
    head_index = lax.axis_index("head")
    row_count, pos_dev, model_width = context_hidden.shape
    local_width = kv_weight.shape[2]
    context = pos_dev * head_count
    all_columns = lax.all_gather(kv_weight, "head", axis=2, tiled=True)
    normed = normalize(context_hidden, norm_gain).reshape(row_count * pos_dev, model_width)
    projected = jnp.einsum(
        "td,kdc->ktc",
        normed,
        lax.all_gather(all_columns, "seq", axis=1, tiled=True),
        preferred_element_type=jnp.float32,
    )
    block_index = seq_index * head_count + head_index
    position = (
        slab_start[:, None] + block_index * pos_dev + jnp.arange(pos_dev, dtype=jnp.int32)[None, :]
    )
    rotated = rotate(projected[0].reshape(row_count, pos_dev, -1, HD), position, freqs).reshape(
        row_count, pos_dev, -1
    )
    value_rows = projected[1].reshape(row_count, pos_dev, -1)
    stacked = jnp.stack([rotated, value_rows]).astype(jnp.bfloat16)
    restored = lax.all_to_all(stacked, "head", split_axis=3, concat_axis=2, tiled=True)
    k_cache = restored[0]
    v_cache = restored[1]
    k_cache, v_cache = lax.optimization_barrier((k_cache, v_cache))
    group_size = HQ // KVH
    local_heads = local_width // HD
    step_pos = (slab_start + lengths)[None, :] + jnp.arange(STEPS, dtype=jnp.int32)[:, None]
    rotated_query = rotate(
        queries.astype(jnp.float32).reshape(STEPS, row_count, -1, HD), step_pos, freqs
    )
    rotated_query = rotated_query.reshape(STEPS, row_count, local_heads, group_size, HD)
    factor = 1.0 / math.sqrt(HD)
    cache_keys = k_cache.astype(jnp.float32).reshape(row_count, context, local_heads, HD)
    cache_values = v_cache.astype(jnp.float32).reshape(row_count, context, local_heads, HD)
    scores = jnp.einsum("ibgrd,bpgd->ibgrp", rotated_query, cache_keys) * factor
    cache_pos = seq_index * context + jnp.arange(context, dtype=jnp.int32)
    live_mask = (cache_pos[None, :] < lengths[:, None])[None, :, None, None, :]
    scores = jnp.where(live_mask, scores, -1e30)
    peak_score = scores.max(-1)
    weights = jnp.where(live_mask, jnp.exp(scores - peak_score[..., None]), 0.0)
    weight_sum = weights.sum(-1)
    mixture = jnp.einsum("ibgrp,bpgd->ibgrd", weights, cache_values)
    row_share = row_count // seq_count
    first_row = seq_index * row_share
    merged = merged_2((peak_score, weight_sum, mixture), "seq", combine_parts)
    part_peak = lax.dynamic_slice_in_dim(merged[0], first_row, row_share, 1)
    part_sum = lax.dynamic_slice_in_dim(merged[1], first_row, row_share, 1)
    part_mix = lax.dynamic_slice_in_dim(merged[2], first_row, row_share, 1)
    own_query = lax.dynamic_slice_in_dim(rotated_query, first_row, row_share, 1)
    own_pos = lax.dynamic_slice_in_dim(step_pos, first_row, row_share, 1)
    own_fresh = lax.dynamic_slice_in_dim(new_kv, first_row, row_share, 2).astype(jnp.float32)
    fresh_keys = rotate(own_fresh[0].reshape(STEPS, row_share, local_heads, HD), own_pos, freqs)
    fresh_values = own_fresh[1].reshape(STEPS, row_share, local_heads, HD)
    fresh_scores = jnp.einsum("ibgrd,jbgd->ibgrj", own_query, fresh_keys) * factor
    steps_index = jnp.arange(STEPS, dtype=jnp.int32)
    causal = (steps_index[None, :] <= steps_index[:, None])[:, None, None, None, :]
    fresh_scores = jnp.where(causal, fresh_scores, -1e30)
    fresh_peak = fresh_scores.max(-1)
    fresh_weights = jnp.where(causal, jnp.exp(fresh_scores - fresh_peak[..., None]), 0.0)
    fresh_mix = jnp.einsum("ibgrj,jbgd->ibgrd", fresh_weights, fresh_values)
    final_parts = combine_parts(
        (part_peak, part_sum, part_mix), (fresh_peak, fresh_weights.sum(-1), fresh_mix)
    )
    attention = (
        (final_parts[2] / final_parts[1][..., None])
        .reshape(STEPS, row_share, -1)
        .astype(jnp.bfloat16)
    )
    return (k_cache, v_cache, attention)


def solution(mesh):
    return jax.shard_map(
        shards,
        mesh=mesh,
        in_specs=(
            P(None, ("seq", "head"), None),
            P(),
            P(None, "seq", "head"),
            P(None, None, "head"),
            P(None, None, None, "head"),
            P(),
            P(),
        ),
        out_specs=(P(None, "seq", "head"), P(None, "seq", "head"), P(None, "seq", "head")),
        check_vma=False,
    )
```

profile of v0, /device:TPU:1, one launch (start us, length us, event | category | flops | bytes accessed | tf_op | source)
XLA Modules:
  0.0 407.6 jit_solution(2840506179734593406)
XLA Ops:
  8.0 62.1 %all-gather.7.cloned.1.call-done = bf16[2,512,1024]{2,1,0:T(8,128)(2,1)} async-done(((bf16[2,512,128]{2,1,0:T(8,128)(2,1)}), bf16[2,512,1024]{2,1,0:T(8,128)(2,1)}) %all-gather.7.cloned.1.call-update) | async-done | bytes 2097168 | tf_op jit(solution)/shard_map/all_gather | solution.py:72
  71.8 3.1 fusion.6
  75.6 166.9 %all-gather.9.cloned.1.call-done = bf16[2,8192,1024]{2,1,0:T(8,128)(2,1)} async-done(((bf16[2,512,1024]{2,1,0:T(8,128)(2,1)}), bf16[2,8192,1024]{2,1,0:T(8,128)(2,1)}) %all-gather.9.cloned.1.call-update) | async-done | bytes 33554448 | tf_op jit(solution)/shard_map/all_gather | solution.py:77
  242.5 16.3 %fusion.14 = f32[2,256,1024]{2,1,0:T(8,128)S(1)} fusion(bf16[2,8192,1024]{2,1,0:T(8,128)(2,1)} %all-gather.9.cloned.1.call-done, bf16[32,8,8192]{2,1,0:T(8,128)(2,1)} %param.9, f32[8192]{0:T(1024)S(1)} %copy-done.2, f32[32,8]{1,0:T(8,128)S(1)} %add_rsqrt_fusion), kind=kOutput, calls=%fused_computation.21 | convolution fusion | flops 8598323200 | bytes 39879680 | tf_op jit(solution)/shard_map/td,kdc->ktc/dot_general | solution.py:74
  259.9 5.1 %copy.52 = bf16[2,32,8,1024]{1,2,0,3:T(8,128)(2,1)} copy(bf16[2,32,8,1024]{3,2,1,0:T(8,128)(2,1)S(1)} %pad_maximum_fusion) | data formatting | bytes 2097152 | tf_op jit(solution)/shard_map/stack | solution.py:88
  265.0 7.8 %reshape.276 = bf16[8,2,32768]{2,1,0:T(2,128)(2,1)} reshape(bf16[1024,2,8,32]{3,2,1,0:T(8,128)(2,1)} %bitcast.169) | data formatting | bytes 2097152
  272.8 6.4 %all-to-all-start = ((bf16[8,2,32768]{2,1,0:T(2,128)(2,1)}), bf16[8,2,32768]{2,1,0:T(2,128)(2,1)S(1)}, u32[]{:S(2)}, u32[]{:S(2)}) async-start(bf16[8,2,32768]{2,1,0:T(2,128)(2,1)} %reshape.276), calls=%async_computation | async-start | bytes 2097152 | tf_op jit(solution)/shard_map/all_to_all | solution.py:89
  280.5 14.7 %all-to-all-done = bf16[8,2,32768]{2,1,0:T(2,128)(2,1)S(1)} async-done(((bf16[8,2,32768]{2,1,0:T(2,128)(2,1)}), bf16[8,2,32768]{2,1,0:T(2,128)(2,1)S(1)}, u32[]{:S(2)}, u32[]{:S(2)}) %all-to-all-start) | async-done | bytes 1048608 | tf_op jit(solution)/shard_map/all_to_all | solution.py:89
  295.2 4.5 %reshape.277 = bf16[1024,2,8,32]{3,2,1,0:T(8,128)(2,1)} reshape(bf16[8,2,32768]{2,1,0:T(2,128)(2,1)S(1)} %all-to-all-done) | data formatting | bytes 2097152
  299.7 3.9 fusion.66
  303.6 2.9 copy.53
  306.5 2.3 copy.54
  309.3 2.2 convolution_bitcast_fusion
  313.5 21.5 %all-gather = f32[64,32,8]{1,2,0:T(8,128)S(1)} all-gather(f32[4,32,8]{1,2,0:T(8,128)S(1)} %copy.56), channel_id=2, replica_groups=mesh['seq'=16,'head'=8] {'seq'}, dimensions={0}, use_global_device_ids=true | all-gather | bytes 69632 | tf_op jit(solution)/shard_map/all_gather | solution.py:15
  335.0 19.8 %all-gather.1 = f32[64,32,8]{1,2,0:T(8,128)S(1)} all-gather(f32[4,32,8]{1,2,0:T(8,128)S(1)} %copy.57), channel_id=3, replica_groups=mesh['seq'=16,'head'=8] {'seq'}, dimensions={0}, use_global_device_ids=true | all-gather | bytes 69632 | tf_op jit(solution)/shard_map/all_gather | solution.py:15
  354.8 11.8 %all-gather.11.cloned.1.call-done = f32[64,32,1,8,128]{4,3,0,1,2:T(8,128)} async-done(((f32[4,32,1,8,128]{4,3,0,1,2:T(8,128)}), f32[64,32,1,8,128]{4,3,0,1,2:T(8,128)}) %all-gather.11.cloned.1.call-update) | async-done | bytes 8388624 | tf_op jit(solution)/shard_map/all_gather | solution.py:15
  367.8 6.8 %slice.95 = f32[60,32,1,8,128]{4,3,0,1,2:T(8,128)} slice(f32[64,32,1,8,128]{4,3,0,1,2:T(8,128)} %all-gather.11.cloned.1.call-done), slice={[4:64], [0:32], [0:1], [0:8], [0:128]} | slice | bytes 15728640 | tf_op jit(solution)/shard_map/slice | solution.py:17
  374.6 25.3 %while.14 = (s32[]{:T(128)}, f32[4,32,1,8]{1,3,2,0:T(8,128)S(1)}, f32[4,32,1,8]{1,3,2,0:T(8,128)S(1)}, f32[4,32,1,8,128]{4,3,2,1,0:T(8,128)S(1)}, f32[15,4,32,1,...) while((s32[]{:T(128)}, f32[4,32,1,8]{1,3,2,0:T(8,128)S(1)}, ...), condition=%wide.region_4.5_spmd, body=%wide.region_3.4_spmd.sunk | while | flops 400386 | bytes 1650793 | solution.py:18
  374.8 1.5 fusion.78
  376.5 1.5 fusion.78
  378.2 1.5 fusion.78
  386.6 1.5 fusion.78
  391.7 1.5 fusion.78
  396.8 1.5 fusion.78
  (139 shorter events, 26.1 us)
Async XLA Ops:
  7.2 235.3 %copy-start.2 = (f32[8192]{0:T(1024)S(1)}, f32[8192]{0:T(1024)}, u32[]{:S(2)}) copy-start(f32[8192]{0:T(1024)} %param.10) | copy-start | bytes 98308
  7.2 62.8 %all-gather.7.cloned.1.call-start = ((), (), s32[]{:S(2)}) async-start(), calls=%async_computation.1 | async-start | bytes 2359296 | tf_op jit(solution)/shard_map/all_gather | solution.py:72
  7.9 234.6 %all-gather.9.cloned.1.call-start = ((), (), s32[]{:S(2)}) async-start(), calls=%async_computation.2 | async-start | bytes 35651584 | tf_op jit(solution)/shard_map/all_gather | solution.py:77
  265.0 14.5 %copy-start.1 = (s32[32]{0:T(128)S(1)}, s32[32]{0:T(128)}, u32[]{:S(2)}) copy-start(s32[32]{0:T(128)} %param.14) | copy-start | bytes 388
  272.8 22.3 %all-to-all-start = ((bf16[8,2,32768]{2,1,0:T(2,128)(2,1)}), bf16[8,2,32768]{2,1,0:T(2,128)(2,1)S(1)}, u32[]{:S(2)}, u32[]{:S(2)}) async-start(bf16[8,2,32768]{2,1,0:T(2,128)(2,1)} %reshape.276), calls=%async_computation | async-start | bytes 2097152 | tf_op jit(solution)/shard_map/all_to_all | solution.py:89
  279.3 87.4 %all-gather.11.cloned.1.call-start = ((), (), s32[]{:S(2)}) async-start(), calls=%async_computation.3 | async-start | bytes 8912896 | tf_op jit(solution)/shard_map/all_gather | solution.py:15
  306.5 28.5 %copy-start = (bf16[1,32,8,8,128]{4,3,2,1,0:T(8,128)(2,1)}, bf16[1,32,8,8,128]{4,3,2,1,0:T(8,128)(2,1)S(1)}, u32[]{:S(2)}) copy-start(bf16[1,32,8,8,128]{4,3,2,1,0:T(8,128)(2,1)S(1)} %copy.53) | copy-start | bytes 1572868
Sparse Core Ops, SparseCore 0:
  10.2 59.7 all-gather.6
  71.7 170.7 all-gather.8
  311.7 54.8 all-gather.10
where the time goes:
time: 409 us; the launch traced here: 408 us
  waiting for transfers between devices  256 us (63%)
  blocking collectives  41.3 us (10%)
  local copies, waits for them, and re-layouts  39.9 us (10%)
  other arithmetic  29.3 us (7%)
  matrix products  19.6 us (5%)
  between operations  14 us (3%)
  starting transfers between devices  6.72 us (2%)
    all_gather x1, waiting for transfers between devices, shards(): lax.all_gather(all_columns, 'seq', axis=1, tiled=True)  167 us
    all_gather x1, waiting for transfers between devices, shards(): all_columns = lax.all_gather(kv_weight, 'head', axis=2, tiled=True)  62.1 us
    all_gather x2, blocking collectives, merged_2(): pieces = jax.tree.map(lambda part: lax.all_gather(part, axis), value)  41.3 us
    add x15, other arithmetic, combine_parts(): mix_first * weight_first[..., None] + mix_second * weight_second[..., None]  21.8 us
    dot_general x1, matrix products, shards(): jnp.einsum('td,kdc->ktc', normed, lax.all_gather(all_columns, 'seq', axis...  16.3 us
    all_to_all x1, waiting for transfers between devices, shards(): lax.all_to_all(stacked, 'head', split_axis=3, concat_axis=2, tiled=True)  14.7 us
    unnamed x10, local copies, waits for them, and re-layouts  14 us
    all_gather x1, waiting for transfers between devices, merged_2(): pieces = jax.tree.map(lambda part: lax.all_gather(part, axis), value)  11.8 us
  transfers between devices with their start and end apart: 4, of which 4 were waited for; matrix products, arithmetic and copies ran while one was open for 2% of the time, Pallas kernels for 0%

commit v1 on v0

v1 whole, which is shorter than its diff:
```python
import functools
import math

import jax
import jax.numpy as jnp
from jax import lax
from jax.experimental import pallas as pl
from jax.experimental.pallas import tpu as pltpu
from jax.sharding import PartitionSpec as P

HQ = 64
KVH = 8
HD = 128
STEPS = 4
B = 32
GROUP = HQ // KVH
ROWS = STEPS * GROUP
AXES = ("seq", "head")
X, Y, Z = 0, 1, 2
MIB = 1024 * 1024
VMEM = pl.BlockSpec(memory_space=pltpu.VMEM)
SMEM = pl.BlockSpec(memory_space=pltpu.SMEM)

PARTS = {"a": (192, (Y, Z, X)), "b": (192, (Z, X, Y)), "c": (128, (X, Y, Z))}


def place(n):
    s, h = n >> 3, n & 7
    return [h >> 1, (h & 1) * 2 + ((s >> 1) & 1), s >> 2, s & 1]


def flat(x, y, z, core):
    return (((z * 2 + (y & 1)) * 2 + core) * 4 + x) * 2 + (y >> 1)


def exchange(dim, step):
    pairs = []
    for n in range(128):
        spot = place(n)
        spot[dim] ^= (1, 3)[spot[3] ^ step]
        pairs.append((flat(*spot), n))
    return pairs


def siblings():
    return [(n, flat(*place(n)[:3], 1 - place(n)[3])) for n in range(128)]


def swap(value, dim, step):
    return lax.ppermute(value, AXES, exchange(dim, step))


def doubled(block, dim):
    pair = jnp.stack([block, swap(block, dim, 0)])
    return jnp.concatenate([pair, swap(pair, dim, 1)])


def rope_freqs():
    indices = jnp.arange(HD // 2, dtype=jnp.float32)
    base_freq = jnp.exp(-2.0 * indices / HD * math.log(500000.0))
    wavelength = 2.0 * math.pi / base_freq
    blend_weight = (8192.0 / wavelength - 1.0) / 3.0
    middle = (1.0 - blend_weight) * base_freq / 8.0 + blend_weight * base_freq
    return jnp.where(
        wavelength > 8192.0, base_freq / 8.0, jnp.where(wavelength < 2048.0, base_freq, middle)
    )


def tables(position, freqs):
    angles = position.astype(jnp.float32)[..., None] * freqs
    cosine, sine = jnp.cos(angles), jnp.sin(angles)
    return jnp.concatenate([cosine, cosine], -1), jnp.concatenate([-sine, sine], -1)


def rotated(vectors, cosine, sine):
    half = HD // 2
    swapped = jnp.concatenate([vectors[..., half:], vectors[..., :half]], -1)
    return vectors * cosine + swapped * sine


def prep_kernel(spot, even, odd, gain_even, gain_odd, own, send, scale, total):
    step = pl.program_id(0)
    core = spot[3]

    @pl.when(step == 0)
    def _():
        total[...] = jnp.zeros_like(total)

    x_even = even[...].astype(jnp.float32)
    x_odd = odd[...].astype(jnp.float32)
    squares = x_even * x_even + x_odd * x_odd
    total[...] += sum(squares[:, 128 * i : 128 * i + 128] for i in range(8))
    g_even = (x_even * gain_even[...]).astype(jnp.bfloat16)
    g_odd = (x_odd * gain_odd[...]).astype(jnp.bfloat16)
    lower = lax.broadcasted_iota(jnp.int32, (256, 128), 1) < 64
    ylo, zh = step // 2, step % 2
    tiles = []
    for parity in range(2):
        e = [g_even[:, 512 * parity + 128 * i : 512 * parity + 128 * i + 128] for i in range(4)]
        o = [g_odd[:, 512 * parity + 128 * i : 512 * parity + 128 * i + 128] for i in range(4)]
        tiles.append(
            (
                jnp.concatenate([e[0], jnp.where(lower, e[1], o[2]), o[3]], 1),
                jnp.concatenate([o[1], jnp.where(lower, o[2], e[1]), e[2]], 1),
                e[3],
                o[0],
            )
        )
    spots = (step * 384, 1536 + step * 384, 3072 + (4 * zh + ylo) * 128, 3072 + (4 * zh + 2 + ylo) * 128)
    for at, zero, one in zip(spots, *tiles):
        lanes = pl.ds(pl.multiple_of(at, 128), zero.shape[1])

        @pl.when(core == 0)
        def _():
            own[:, lanes] = zero
            send[:, lanes] = one

        @pl.when(core == 1)
        def _():
            own[:, lanes] = one
            send[:, lanes] = zero

    @pl.when(step == 3)
    def _():
        mean = jnp.sum(total[...], axis=1, keepdims=True) / 8192.0
        scale[...] = jnp.broadcast_to(lax.rsqrt(mean + 1e-05), (256, 128))


def prep(spot, hidden, gain):
    even = lambda step, spot: (0, 4 * (step % 2) + step // 2)
    odd = lambda step, spot: (0, 4 * (step % 2) + 2 + step // 2)
    whole = lambda step, spot: (0, 0)
    return pl.pallas_call(
        prep_kernel,
        out_shape=(
            jax.ShapeDtypeStruct((256, 4096), jnp.bfloat16),
            jax.ShapeDtypeStruct((256, 4096), jnp.bfloat16),
            jax.ShapeDtypeStruct((256, 128), jnp.float32),
        ),
        grid_spec=pltpu.PrefetchScalarGridSpec(
            num_scalar_prefetch=1,
            grid=(4,),
            in_specs=[
                pl.BlockSpec((256, 1024), even),
                pl.BlockSpec((256, 1024), odd),
                pl.BlockSpec((1, 1024), even),
                pl.BlockSpec((1, 1024), odd),
            ],
            out_specs=[
                pl.BlockSpec((256, 4096), whole),
                pl.BlockSpec((256, 4096), whole),
                pl.BlockSpec((256, 128), whole),
            ],
            scratch_shapes=[pltpu.VMEM((256, 128), jnp.float32)],
        ),
        compiler_params=pltpu.CompilerParams(vmem_limit_bytes=20 * MIB),
        cost_estimate=pl.CostEstimate(flops=8_000_000, bytes_accessed=8 * MIB, transcendentals=0),
    )(spot, hidden, hidden, gain, gain)


def product_kernel(slots, inputs, carried, narrow, spot, *refs):
    x_refs = refs[:inputs]
    piece_refs = refs[inputs : inputs + 3]
    if not carried:
        groups = list(zip("abc", piece_refs))
        rest = refs[inputs + 3 :]
    else:
        groups = list(zip("abc", piece_refs))
        rest = refs[inputs + 3 + inputs :]
        before = refs[inputs + 3 : inputs + 3 + inputs]
    outs, sums = rest[:inputs], rest[inputs:]
    mine = [spot[0], spot[1], spot[2]]
    core = spot[3]
    flips = [0, 1 + 2 * core, 3 - 2 * core, 2]

    def slot_of(flip):
        return jnp.where(flip == 0, 0, jnp.where(flip == flips[1], 1, jnp.where(flip == flips[2], 2, 3)))

    def at(dim, slot):
        return mine[dim] ^ flips[slot]

    for i in range(inputs):
        sums[i][...] = before[i][...] if carried else jnp.zeros_like(sums[i])

    def add(x_at, depth, weight, heads):
        for x_ref, total in zip(x_refs, sums):
            left = x_ref[:, pl.ds(pl.multiple_of(x_at, 128), depth)]
            result = jnp.dot(left, weight, preferred_element_type=jnp.float32)
            for i, head in enumerate(heads):
                total[head] += result[:, 128 * i : 128 * i + 128]

    z_slots = [slot_of(z ^ mine[Z]) for z in range(4)]
    y_slots = [slot_of(y ^ mine[Y]) for y in range(4)]
    for part, ref in groups:
        for index, slot in enumerate(slots):
            if part == "a":
                x = at(X, slot)
                for first, second in ((0, 3), (1, 2)):
                    y0, y1 = at(Y, first), at(Y, second)
                    weight = jnp.concatenate(
                        [
                            jnp.concatenate([ref[index, s, first], ref[index, s, second]], 1)
                            for s in z_slots
                        ],
                        0,
                    )
                    add(768 * (y0 & 1), 768, weight, [2 * x + (y0 >> 1), 2 * x + (y1 >> 1)])
            elif part == "b":
                y = at(Y, slot)
                weight = jnp.concatenate(
                    [
                        jnp.concatenate([ref[index, xs, z_slots[z]] for xs in range(4)], 1)
                        for z in (1, 0, 3, 2)
                    ],
                    0,
                )
                add(1536 + 768 * (y & 1), 768, weight, [2 * at(X, xs) + (y >> 1) for xs in range(4)])
            else:
                z = at(Z, slot)
                for yhi in range(2):
                    weight = jnp.concatenate(
                        [
                            jnp.concatenate([ref[index, y_slots[2 * yhi + ylo], xs] for xs in range(4)], 1)
                            for ylo in range(2)
                        ],
                        0,
                    )
                    add(3072 + 256 * z, 256, weight, [2 * at(X, xs) + yhi for xs in range(4)])
    if narrow:
        for i in range(inputs):
            outs[i][...] = sums[i][...].astype(outs[i].dtype)


def product(spot, rows, pieces, slots, before=None, narrow=False):
    carried = before is not None
    kind = jnp.bfloat16 if narrow else jnp.float32
    shape = (KVH, 256, HD)
    count = len(rows)

    def body(*refs):
        if narrow:
            product_kernel(slots, count, carried, True, *refs)
        else:
            product_kernel(slots, count, carried, False, *refs, *refs[-count:])

    return pl.pallas_call(
        body,
        out_shape=[jax.ShapeDtypeStruct(shape, kind)] * count,
        in_specs=[SMEM] + [VMEM] * (count + 3 + (count if carried else 0)),
        out_specs=[VMEM] * count,
        scratch_shapes=[pltpu.VMEM(shape, jnp.float32)] * (count if narrow else 0),
        compiler_params=pltpu.CompilerParams(vmem_limit_bytes=40 * MIB),
        cost_estimate=pl.CostEstimate(
            flops=count * len(slots) * 2 * 256 * 4096 * 256, bytes_accessed=4 * MIB, transcendentals=0
        ),
    )(spot, *rows, *pieces, *(before or ()))


def finish_kernel(keys, own, other, scale, *refs):
    out = refs[-1]
    for head in range(KVH):
        value = (own[head] + other[head].astype(jnp.float32)) * scale[...]
        if keys:
            value = value * refs[0][...] + pltpu.roll(value, HD // 2, 1) * refs[1][...]
        out[head] = value.astype(jnp.bfloat16)


def finish(own, other, scale, angles=()):
    return pl.pallas_call(
        functools.partial(finish_kernel, bool(angles)),
        out_shape=jax.ShapeDtypeStruct((KVH, 256, HD), jnp.bfloat16),
        in_specs=[VMEM] * (3 + len(angles)),
        out_specs=VMEM,
        compiler_params=pltpu.CompilerParams(vmem_limit_bytes=16 * MIB),
        cost_estimate=pl.CostEstimate(flops=2_000_000, bytes_accessed=3 * MIB, transcendentals=0),
    )(own, other, scale, *angles)


def cache_of(received):
    blocks = [received[i].astype(jnp.float32).reshape(B, 8, HD) for i in range(8)]
    return jnp.stack(blocks, axis=1).reshape(B, 64, HD)


def split(value):
    high = value.astype(jnp.bfloat16)
    return high, (value - high.astype(jnp.float32)).astype(jnp.bfloat16)


NT = (((1,), (1,)), ((), ()))


def score_kernel(spot, lengths, received, query, fresh, cache, weights, fresh_weights, marks):
    seq = spot[4]
    cache[...] = cache_of(received).astype(jnp.bfloat16)
    column = lax.broadcasted_iota(jnp.int32, (ROWS, 64), 1) + seq * 64
    late = lax.broadcasted_iota(jnp.int32, (ROWS, 8), 1)
    token = lax.broadcasted_iota(jnp.int32, (ROWS, 8), 0) // GROUP
    causal = late <= token
    diagonal = lax.broadcasted_iota(jnp.int32, (2 * ROWS, 128), 0)
    lane = lax.broadcasted_iota(jnp.int32, (2 * ROWS, 128), 1)
    factor = 1.0 / math.sqrt(HD)
    for pair in range(B // 2):
        peaks, sums = [], []
        for b in (2 * pair, 2 * pair + 1):
            high, low = split(query[b])
            both = lax.dot_general(
                jnp.concatenate([high, low], 0), cache[b], NT, preferred_element_type=jnp.float32
            )
            score = (both[:ROWS] + both[ROWS:]) * factor
            late_score = (
                lax.dot_general(
                    query[b], fresh[b], NT, preferred_element_type=jnp.float32, precision=lax.Precision.HIGHEST
                )
                * factor
            )
            live = column < lengths[b]
            new = causal & (seq == pair)
            score = jnp.where(live, score, -1e30)
            late_score = jnp.where(new, late_score, -1e30)
            peak = jnp.maximum(
                jnp.max(score, axis=1, keepdims=True), jnp.max(late_score, axis=1, keepdims=True)
            )
            weight = jnp.where(live, jnp.exp(score - peak), 0.0)
            late_weight = jnp.where(new, jnp.exp(late_score - peak), 0.0)
            weights[b] = weight
            fresh_weights[b] = late_weight
            peaks.append(peak)
            sums.append(jnp.sum(weight, axis=1, keepdims=True) + jnp.sum(late_weight, axis=1, keepdims=True))
        peak, total = jnp.concatenate(peaks, 0), jnp.concatenate(sums, 0)
        line = jnp.where(diagonal == lane, peak, 0.0) + jnp.where(diagonal + 64 == lane, total, 0.0)
        marks[pair] = jnp.broadcast_to(jnp.sum(line, axis=0, keepdims=True), (8, 128))


def score(spot, lengths, received, query, fresh):
    return pl.pallas_call(
        score_kernel,
        out_shape=(
            jax.ShapeDtypeStruct((B, 64, HD), jnp.bfloat16),
            jax.ShapeDtypeStruct((B, ROWS, 64), jnp.float32),
            jax.ShapeDtypeStruct((B, ROWS, 8), jnp.float32),
            jax.ShapeDtypeStruct((B // 2, 8, 128), jnp.float32),
        ),
        in_specs=[SMEM, SMEM, VMEM, VMEM, VMEM],
        out_specs=[VMEM] * 4,
        compiler_params=pltpu.CompilerParams(vmem_limit_bytes=16 * MIB),
        cost_estimate=pl.CostEstimate(flops=60_000_000, bytes_accessed=4 * MIB, transcendentals=70_000),
    )(spot, lengths, received, query, fresh)


def mix_kernel(received, weights, fresh_weights, fresh, marks, cache, packed):
    cache[...] = cache_of(received).astype(jnp.bfloat16)
    for b in range(B):
        high, low = split(weights[b])
        both = jnp.dot(jnp.concatenate([high, low], 0), cache[b], preferred_element_type=jnp.float32)
        high, low = split(fresh_weights[b])
        late = jnp.dot(jnp.concatenate([high, low], 0), fresh[b], preferred_element_type=jnp.float32)
        packed[b // 2, pl.ds(ROWS * (b % 2), ROWS)] = both[:ROWS] + both[ROWS:] + late[:ROWS] + late[ROWS:]
    packed[:, pl.ds(64, 8)] = marks[...]


def mix(received, weights, fresh_weights, fresh, marks):
    return pl.pallas_call(
        mix_kernel,
        out_shape=(
            jax.ShapeDtypeStruct((B, 64, HD), jnp.bfloat16),
            jax.ShapeDtypeStruct((B // 2, 72, HD), jnp.float32),
        ),
        in_specs=[VMEM] * 5,
        out_specs=[VMEM] * 2,
        compiler_params=pltpu.CompilerParams(vmem_limit_bytes=16 * MIB),
        cost_estimate=pl.CostEstimate(flops=60_000_000, bytes_accessed=4 * MIB, transcendentals=0),
    )(received, weights, fresh_weights, fresh, marks)


def merge_kernel(parts, out):
    marks = parts[:, 64]
    lane = lax.broadcasted_iota(jnp.int32, (16, 128), 1)
    peak = jnp.max(marks, axis=0, keepdims=True)
    grow = jnp.where(lane < 64, jnp.exp(marks - peak), 0.0)
    total = jnp.sum(grow * pltpu.roll(marks, 64, 1), axis=0, keepdims=True)
    share = grow / jnp.where(lane[:1] < 64, total, 1.0)
    columns = jnp.concatenate([share, jnp.zeros((112, 128), jnp.float32)], 0).T
    result = sum(parts[i, :64] * columns[:64, i : i + 1] for i in range(16))
    for b in range(2):
        for i in range(STEPS):
            out[i, b] = result[ROWS * b + GROUP * i : ROWS * b + GROUP * i + GROUP]


def merge(parts):
    return pl.pallas_call(
        merge_kernel,
        out_shape=jax.ShapeDtypeStruct((STEPS, 2, GROUP, HD), jnp.float32),
        in_specs=[VMEM],
        out_specs=VMEM,
        cost_estimate=pl.CostEstimate(flops=300_000, bytes_accessed=MIB, transcendentals=2048),
    )(parts)


def shards(context_hidden, norm_gain, kv_weight, queries, new_kv, lengths, slab_start):
    seq, head = lax.axis_index("seq"), lax.axis_index("head")
    z, ylo, core = seq >> 2, (seq >> 1) & 1, seq & 1
    x, yhi = head >> 1, head & 1
    spot = jnp.stack([x, yhi * 2 + ylo, z, core, seq]).astype(jnp.int32)
    odd = z & 1
    starts = {
        "a": jnp.where(odd, 320, 0),
        "b": jnp.where(odd, 128, 192),
        "c": jnp.where(odd, 0, 384),
    }

    first = {
        part: doubled(lax.dynamic_slice_in_dim(kv_weight, starts[part], depth, 1), dims[0])
        for part, (depth, dims) in PARTS.items()
    }

    own_rows, sent_rows, scale = prep(spot, context_hidden.reshape(256, 8192), norm_gain.reshape(1, 8192))
    other_rows = lax.ppermute(sent_rows, AXES, siblings())

    freqs = rope_freqs()
    position = (
        slab_start[:, None] + (seq * 8 + head) * 8 + jnp.arange(8, dtype=jnp.int32)[None, :]
    ).reshape(256)
    angles = tables(position, freqs)
    step_pos = (slab_start + lengths)[:, None] + jnp.arange(STEPS, dtype=jnp.int32)[None, :]
    step_cos, step_sin = tables(step_pos, freqs)
    query = queries.astype(jnp.float32).reshape(STEPS, B, GROUP, HD).transpose(1, 0, 2, 3)
    query = rotated(query, step_cos[:, :, None], step_sin[:, :, None]).reshape(B, ROWS, HD)
    fresh = new_kv.astype(jnp.float32).transpose(0, 2, 1, 3)
    padding = ((0, 0), (0, 8 - STEPS), (0, 0))
    fresh_keys = jnp.pad(rotated(fresh[0], step_cos, step_sin), padding)
    fresh_values = jnp.pad(new_kv[1].transpose(1, 0, 2), padding)

    finished = []
    for kind in range(2):
        near, far = [], []
        for part, (depth, dims) in PARTS.items():
            block = doubled(first[part][:, kind], dims[1])
            pair = jnp.stack([block, swap(block, dims[2], 0)])
            near.append(pair)
            far.append(swap(pair, dims[2], 1))
        own, other = product(spot, [own_rows, other_rows], near, (0, 1))
        (other,) = product(spot, [other_rows], far, (2, 3), [other], narrow=True)
        (own,) = product(spot, [own_rows], far, (2, 3), [own])
        arrived = lax.ppermute(other, AXES, siblings())
        rows = finish(own, arrived, scale, angles if kind == 0 else ())
        received = lax.all_to_all(rows, "head", 0, 0)
        if kind == 0:
            k_cache, weights, late, marks = score(spot, lengths, received, query, fresh_keys)
        else:
            v_cache, packed = mix(received, weights, late, fresh_values, marks)
    parts = lax.all_to_all(packed, "seq", 0, 0)
    attention = merge(parts).astype(jnp.bfloat16).reshape(STEPS, 2, GROUP * HD)
    return k_cache, v_cache, attention


def solution(mesh):
    return jax.shard_map(
        shards,
        mesh=mesh,
        in_specs=(
            P(None, ("seq", "head"), None),
            P(),
            P(None, "seq", "head"),
            P(None, None, "head"),
            P(None, None, None, "head"),
            P(),
            P(),
        ),
        out_specs=(P(None, "seq", "head"), P(None, "seq", "head"), P(None, "seq", "head")),
        check_vma=False,
    )
```

time: 409 us -> 195 us (0.48)
  waiting for transfers between devices: 256 us -> 56.3 us
  starting transfers between devices: 6.72 us -> 55.7 us
  Pallas kernels: 0 us -> 40.8 us
  local copies, waits for them, and re-layouts: 39.9 us -> 12.5 us
  blocking collectives: 41.3 us -> 15.5 us
  matrix products: 19.6 us -> 0 us
  other arithmetic: 29.3 us -> 12.5 us
  between operations: 14 us -> 1.15 us
    all_gather x3 -> x0, waiting for transfers between devices: 241 us -> none  [the longest x1 167 us: shards(): lax.all_gather(all_columns, 'seq', axis=1, tiled=True)]
    ppermute x0 -> x33, waiting for transfers between devices: none -> 48.1 us  [the longest x30 48.1 us: swap(): return lax.ppermute(value, AXES, exchange(dim, step))]
    ppermute x0 -> x33, starting transfers between devices: none -> 46.7 us  [the longest x30 26.9 us: swap(): return lax.ppermute(value, AXES, exchange(dim, step))]
    all_gather x2 -> x0, blocking collectives: 41.3 us -> none  [merged_2(): pieces = jax.tree.map(lambda part: lax.all_gather(part, axis), value)]
    pallas_call x0 -> x12, Pallas kernels: none -> 40.8 us  [the longest x6 26.8 us: product(): pl.pallas_call(body, out_shape=[jax.ShapeDtypeStruct(shape, kind)] * coun...]
    add x17 -> x1, other arithmetic: 21.9 us -> 0.82 us  [rotated(): return vectors * cosine + swapped * sine]
    dot_general x5 -> x0, matrix products: 19.6 us -> none  [the longest x1 16.3 us: shards(): jnp.einsum('td,kdc->ktc', normed, lax.all_gather(all_columns, 'seq', axis...]
    slice x9 -> x1, local copies, waits for them, and re-layouts: 18 us -> 0.21 us  [rotated(): swapped = jnp.concatenate([vectors[..., half:], vectors[..., :half]], -1)]
  transfers between devices with their start and end apart: 4 -> 35, of which waited for: 4 -> 18; matrix products, arithmetic and copies ran while one was open for 2% -> 9% of each run, Pallas kernels for 0% -> 19%
where the time goes in v1:
time: 195 us; the launch traced here: 194 us
  waiting for transfers between devices  56.3 us (29%)
  starting transfers between devices  55.7 us (29%)
  Pallas kernels  40.8 us (21%)
  blocking collectives  15.5 us (8%)
  local copies, waits for them, and re-layouts  12.5 us (6%)
  other arithmetic  12.5 us (6%)
    ppermute x30, waiting for transfers between devices, swap(): return lax.ppermute(value, AXES, exchange(dim, step))  48.1 us
    ppermute x30, starting transfers between devices, swap(): return lax.ppermute(value, AXES, exchange(dim, step))  26.9 us
    pallas_call x6, Pallas kernels, product(): pl.pallas_call(body, out_shape=[jax.ShapeDtypeStruct(shape, kind)] * coun...  26.8 us
    ppermute x2, starting transfers between devices, shards(): arrived = lax.ppermute(other, AXES, siblings())  19.7 us
    all_to_all x1, blocking collectives, shards(): parts = lax.all_to_all(packed, 'seq', 0, 0)  15.5 us
    all_to_all x2, starting transfers between devices, shards(): received = lax.all_to_all(rows, 'head', 0, 0)  9.02 us
    another operation x12, other arithmetic, shards(): pair = jnp.stack([block, swap(block, dims[2], 0)])  8.99 us
    all_to_all x2, waiting for transfers between devices, shards(): received = lax.all_to_all(rows, 'head', 0, 0)  8.23 us
  transfers between devices with their start and end apart: 35, of which 18 were waited for; matrix products, arithmetic and copies ran while one was open for 9% of the time, Pallas kernels for 19%

profile of v1, /device:TPU:1, one launch (start us, length us, event | category | flops | bytes accessed | tf_op | source)
XLA Modules:
  0.0 194.4 jit_solution(10032713134657909039)
XLA Ops:
  1.6 3.6 %collective-permute-start = (bf16[2,192,128]{2,1,0:T(8,128)(2,1)S(1)}, bf16[2,192,128]{2,1,0:T(8,128)(2,1)S(1)}, u32[]{:S(2)}, u32[]{:S(2)}) collective-permute-start(bf16[2,192,128]{2,1,0:T(8,128)(2,1)S(1)} %get-tuple-element.58), channel_id=1, source_target_pairs={{16,0},{17,1},{18,2},{19,3},{20,4},{21,5},{22,6},{23,7},{25,8},{24... | collective-permute-start | bytes 294920 | tf_op jit(solution)/shard_map/ppermute | solution.py:50
  5.3 3.8 %collective-permute-start.6 = (bf16[2,192,128]{2,1,0:T(8,128)(2,1)S(1)}, bf16[2,192,128]{2,1,0:T(8,128)(2,1)S(1)}, u32[]{:S(2)}, u32[]{:S(2)}) collective-permute-start(bf16[2,192,128]{2,1,0:T(8,128)(2,1)S(1)} %get-tuple-element.57), channel_id=1, source_target_pairs={{32,0},{33,1},{34,2},{35,3},{36,4},{37,5},{38,6},{39,7},{104,8},{1... | collective-permute-start | bytes 294920 | tf_op jit(solution)/shard_map/ppermute | solution.py:50
  15.4 4.4 %shard_map.94 = (bf16[256,4096]{1,0:T(8,128)(2,1)S(1)}, bf16[256,4096]{1,0:T(8,128)(2,1)}, f32[256,128]{1,0:T(8,128)S(1)}) custom-call(s32[5]{0:T(128)S(1)} %stack.140.spot.refs_0_, bf16[256,8192]{1,0:T(8,128)(2,1)S(1)} %bitcast.96, bf16[256,8192]{1,0:T(8,128)(2,1)S(1)} %bitcast.97, f32[1,8192]{1,0:T(1,128)S(1)} %bitcast.98, f32[1,8192]{1,0:T(1,128)S(1)} %bitcast.99), custom_call_target="tpu_custom_call" | custom-call | flops 8000000 | bytes 8388608 | tf_op jit(solution)/shard_map/pallas_call | solution.py:133
  21.0 3.5 %collective-permute-done.13 = bf16[2,2,128,128]{3,2,0,1:T(8,128)(2,1)S(1)} collective-permute-done((bf16[2,2,128,128]{3,2,0,1:T(8,128)(2,1)S(1)}, bf16[2,2,128,128]{3,2,0,1:T(8,128)(2,1)S(1)}, u32[]{:S(2)}, u32[]{:S(2)}) %collective-permute-start.13) | collective-permute-done | bytes 131104 | tf_op jit(solution)/shard_map/ppermute | solution.py:50
  24.9 2.6 %collective-permute-start.14 = (bf16[4,128,128]{2,1,0:T(8,128)(2,1)S(1)}, bf16[4,128,128]{2,1,0:T(8,128)(2,1)S(1)}, u32[]{:S(2)}, u32[]{:S(2)}) collective-permute-start(bf16[4,128,128]{2,1,0:T(8,128)(2,1)S(1)} %get-tuple-element.54), channel_id=1, source_target_pairs={{16,0},{17,1},{18,2},{19,3},{20,4},{21,5},{22,6},{23,7},{25,8},{24... | collective-permute-start | bytes 393224 | tf_op jit(solution)/shard_map/ppermute | solution.py:50
  33.5 3.4 %collective-permute-done.8 = bf16[4,192,128]{2,1,0:T(8,128)(2,1)S(1)} collective-permute-done((bf16[4,192,128]{2,1,0:T(8,128)(2,1)S(1)}, bf16[4,192,128]{2,1,0:T(8,128)(2,1)S(1)}, u32[]{:S(2)}, u32[]{:S(2)}) %collective-permute-start.8) | collective-permute-done | bytes 196640 | tf_op jit(solution)/shard_map/ppermute | solution.py:50
  42.5 3.6 %collective-permute-done.9 = bf16[2,4,192,128]{3,2,1,0:T(8,128)(2,1)S(1)} collective-permute-done((bf16[2,4,192,128]{3,2,1,0:T(8,128)(2,1)S(1)}, bf16[2,4,192,128]{3,2,1,0:T(8,128)(2,1)S(1)}, u32[]{:S(2)}, u32[]{:S(2)}) %collective-permute-start.9) | collective-permute-done | bytes 393248 | tf_op jit(solution)/shard_map/ppermute | solution.py:50
  47.3 3.5 %collective-permute-done.21 = bf16[2,4,192,128]{3,2,1,0:T(8,128)(2,1)S(1)} collective-permute-done((bf16[2,4,192,128]{3,2,1,0:T(8,128)(2,1)S(1)}, bf16[2,4,192,128]{3,2,1,0:T(8,128)(2,1)S(1)}, u32[]{:S(2)}, u32[]{:S(2)}) %collective-permute-start.21) | collective-permute-done | bytes 393248 | tf_op jit(solution)/shard_map/ppermute | solution.py:50
  53.0 3.2 %collective-permute-done.29 = bf16[2,4,128,128]{3,2,1,0:T(8,128)(2,1)S(1)} collective-permute-done((bf16[2,4,128,128]{3,2,1,0:T(8,128)(2,1)S(1)}, bf16[2,4,128,128]{3,2,1,0:T(8,128)(2,1)S(1)}, u32[]{:S(2)}, u32[]{:S(2)}) %collective-permute-start.29) | collective-permute-done | bytes 262176 | tf_op jit(solution)/shard_map/ppermute | solution.py:50
  67.8 7.1 %collective-permute-done.22 = bf16[4,4,192,128]{3,2,1,0:T(8,128)(2,1)S(1)} collective-permute-done((bf16[4,4,192,128]{3,2,1,0:T(8,128)(2,1)S(1)}, bf16[4,4,192,128]{3,2,1,0:T(8,128)(2,1)S(1)}, u32[]{:S(2)}, u32[]{:S(2)}) %collective-permute-start.22) | collective-permute-done | bytes 786464 | tf_op jit(solution)/shard_map/ppermute | solution.py:50
  84.0 5.6 %shard_map.95 = (f32[8,256,128]{2,1,0:T(8,128)S(1)}, f32[8,256,128]{2,1,0:T(8,128)S(1)}) custom-call(s32[5]{0:T(128)S(1)} %stack.140.spot.refs_0_, bf16[256,4096]{1,0:T(8,128)(2,1)S(1)} %get-tuple-element.16.refs_1_, bf16[256,4096]{1,0:T(8,128)(2,1)} %collective-permute-done.18.refs_2_.refs_1_, bf16[2,4,4,192,128]{4,3,2,1,0:T(8,128)(2,1)} %pad_maximum_fusion.refs_3_, ...), custom_call_target="tpu_custom_call" | custom-call | flops 2147483648 | bytes 4194304 | tf_op jit(solution)/shard_map/pallas_call | solution.py:246
  89.7 13.6 %collective-permute-done.11.refs_3_ = bf16[2,4,4,192,128]{4,3,2,1,0:T(8,128)(2,1)} collective-permute-done((bf16[2,4,4,192,128]{4,3,2,1,0:T(8,128)(2,1)}, bf16[2,4,4,192,128]{4,3,2,1,0:T(8,128)(2,1)}, u32[]{:S(2)}, u32[]{:S(2)}) %collective-permute-start.11) | collective-permute-done | bytes 1572896 | tf_op jit(solution)/shard_map/ppermute | solution.py:50
  103.5 4.0 %shard_map.97 = bf16[8,256,128]{2,1,0:T(8,128)(2,1)S(1)} custom-call(s32[5]{0:T(128)S(1)} %stack.140.spot.refs_0_, bf16[256,4096]{1,0:T(8,128)(2,1)} %collective-permute-done.18.refs_2_.refs_1_, bf16[2,4,4,192,128]{4,3,2,1,0:T(8,128)(2,1)} %collective-permute-done.5.refs_2_, bf16[2,4,4,192,128]{4,3,2,1,0:T(8,128)(2,1)} %collective-permute-done.11.refs_3_, ...), custom_call_target="tpu_custom_call" | custom-call | flops 1073741824 | bytes 4194304 | tf_op jit(solution)/shard_map/pallas_call | solution.py:246
  107.5 14.7 %collective-permute-start.19 = (bf16[8,256,128]{2,1,0:T(8,128)(2,1)S(1)}, bf16[8,256,128]{2,1,0:T(8,128)(2,1)S(1)}, u32[]{:S(2)}, u32[]{:S(2)}) collective-permute-start(bf16[8,256,128]{2,1,0:T(8,128)(2,1)S(1)} %shard_map.97), channel_id=1, source_target_pairs={{0,8},{1,9},{2,10},{3,11},{4,12},{5,13},{6,14},{7,15},{8,0},{9,1},... | collective-permute-start | bytes 1572872 | tf_op jit(solution)/shard_map/ppermute | solution.py:444
  123.1 5.3 %shard_map.100 = (f32[8,256,128]{2,1,0:T(8,128)S(1)}, f32[8,256,128]{2,1,0:T(8,128)S(1)}) custom-call(s32[5]{0:T(128)S(1)} %stack.140.spot.refs_0_, bf16[256,4096]{1,0:T(8,128)(2,1)S(1)} %get-tuple-element.16.refs_1_, bf16[256,4096]{1,0:T(8,128)(2,1)} %collective-permute-done.18.refs_2_.refs_1_, bf16[2,4,4,192,128]{4,3,2,1,0:T(8,128)(2,1)} %pad_maximum_fusion.2.refs_3_, ...), custom_call_target="tpu_custom_call" | custom-call | flops 2147483648 | bytes 4194304 | tf_op jit(solution)/shard_map/pallas_call | solution.py:246
  129.4 5.2 %shard_map.102 = bf16[8,256,128]{2,1,0:T(8,128)(2,1)} custom-call(s32[5]{0:T(128)S(1)} %stack.140.spot.refs_0_, bf16[256,4096]{1,0:T(8,128)(2,1)} %collective-permute-done.18.refs_2_.refs_1_, bf16[2,4,4,192,128]{4,3,2,1,0:T(8,128)(2,1)} %collective-permute-done.23.refs_2_, bf16[2,4,4,192,128]{4,3,2,1,0:T(8,128)(2,1)} %collective-permute-done.27.refs_3_, ...), custom_call_target="tpu_custom_call" | custom-call | flops 1073741824 | bytes 4194304 | tf_op jit(solution)/shard_map/pallas_call | solution.py:246
  134.6 5.1 %collective-permute-start.32 = (bf16[8,256,128]{2,1,0:T(8,128)(2,1)}, bf16[8,256,128]{2,1,0:T(8,128)(2,1)}, u32[]{:S(2)}, u32[]{:S(2)}) collective-permute-start(bf16[8,256,128]{2,1,0:T(8,128)(2,1)} %shard_map.102), channel_id=1, source_target_pairs={{0,8},{1,9},{2,10},{3,11},{4,12},{5,13},{6,14},{7,15},{8,0},{9,1},... | collective-permute-start | bytes 1572872 | tf_op jit(solution)/shard_map/ppermute | solution.py:444
  139.7 3.3 %shard_map.96.own = f32[8,256,128]{2,1,0:T(8,128)S(1)} custom-call(s32[5]{0:T(128)S(1)} %stack.140.spot.refs_0_, bf16[256,4096]{1,0:T(8,128)(2,1)S(1)} %get-tuple-element.16.refs_1_, bf16[2,4,4,192,128]{4,3,2,1,0:T(8,128)(2,1)} %collective-permute-done.5.refs_2_, bf16[2,4,4,192,128]{4,3,2,1,0:T(8,128)(2,1)} %collective-permute-done.11.refs_3_, ...), custom_call_target="tpu_custom_call" | custom-call | flops 1073741824 | bytes 4194304 | tf_op jit(solution)/shard_map/pallas_call | solution.py:246
  144.3 4.5 %all-to-all-start = ((bf16[8,256,128]{2,1,0:T(8,128)(2,1)}), bf16[8,256,128]{2,1,0:T(8,128)(2,1)}, u32[]{:S(2)}, u32[]{:S(2)}) async-start(bf16[8,256,128]{2,1,0:T(8,128)(2,1)} %copy-done.3), calls=%async_computation | async-start | bytes 1048576 | tf_op jit(solution)/shard_map/all_to_all | solution.py:446
  151.7 3.3 %shard_map.101.own = f32[8,256,128]{2,1,0:T(8,128)S(1)} custom-call(s32[5]{0:T(128)S(1)} %stack.140.spot.refs_0_, bf16[256,4096]{1,0:T(8,128)(2,1)S(1)} %get-tuple-element.16.refs_1_, bf16[2,4,4,192,128]{4,3,2,1,0:T(8,128)(2,1)} %collective-permute-done.23.refs_2_, bf16[2,4,4,192,128]{4,3,2,1,0:T(8,128)(2,1)} %collective-permute-done.27.refs_3_, ...), custom_call_target="tpu_custom_call" | custom-call | flops 1073741824 | bytes 4194304 | tf_op jit(solution)/shard_map/pallas_call | solution.py:246
  159.1 4.5 %all-to-all-start.1 = ((bf16[8,256,128]{2,1,0:T(8,128)(2,1)}), bf16[8,256,128]{2,1,0:T(8,128)(2,1)S(1)}, u32[]{:S(2)}, u32[]{:S(2)}) async-start(bf16[8,256,128]{2,1,0:T(8,128)(2,1)} %shard_map.103), calls=%async_computation.1 | async-start | bytes 1048576 | tf_op jit(solution)/shard_map/all_to_all | solution.py:446
  164.1 3.9 %shard_map.99 = (bf16[32,64,128]{2,1,0:T(8,128)(2,1)}, f32[32,32,64]{2,1,0:T(8,128)S(1)}, f32[32,32,8]{2,1,0:T(8,128)S(1)}, f32[16,8,128]{2,1,0:T(8,128)S(1)}) custom-call(s32[5]{0:T(128)S(1)} %stack.140.spot.refs_0_, s32[32]{0:T(128)S(1)} %copy-done.7, bf16[8,256,128]{2,1,0:T(8,128)(2,1)} %all-to-all-done.received, f32[32,32,128]{2,1,0:T(8,128)S(1)} %fusion.1.query, ...), custom_call_target="tpu_custom_call" | custom-call | flops 60000000 | bytes 4194304 | tf_op jit(solution)/shard_map/pallas_call | solution.py:335
  168.0 6.3 %all-to-all-done.1.received = bf16[8,256,128]{2,1,0:T(8,128)(2,1)S(1)} async-done(((bf16[8,256,128]{2,1,0:T(8,128)(2,1)}), bf16[8,256,128]{2,1,0:T(8,128)(2,1)S(1)}, u32[]{:S(2)}, u32[]{:S(2)}) %all-to-all-start.1) | async-done | bytes 524320 | tf_op jit(solution)/shard_map/all_to_all | solution.py:446
  175.4 15.5 %all_to_all.15.parts = f32[16,72,128]{2,1,0:T(8,128)} all-to-all(f32[16,72,128]{2,1,0:T(8,128)S(1)} %get-tuple-element.28), channel_id=1, replica_groups=mesh['seq'=16,'head'=8] {'seq'}, dimensions={0} | all-to-all | bytes 1179648 | tf_op jit(solution)/shard_map/all_to_all | solution.py:451
  (140 shorter events, 59.6 us)
Async XLA Ops:
  1.6 19.2 %collective-permute-start = (bf16[2,192,128]{2,1,0:T(8,128)(2,1)S(1)}, bf16[2,192,128]{2,1,0:T(8,128)(2,1)S(1)}, u32[]{:S(2)}, u32[]{:S(2)}) collective-permute-start(bf16[2,192,128]{2,1,0:T(8,128)(2,1)S(1)} %get-tuple-element.58), channel_id=1, source_target_pairs={{16,0},{17,1},{18,2},{19,3},{20,4},{21,5},{22,6},{23,7},{25,8},{24... | collective-permute-start | bytes 294920 | tf_op jit(solution)/shard_map/ppermute | solution.py:50
  5.3 15.6 %collective-permute-start.6 = (bf16[2,192,128]{2,1,0:T(8,128)(2,1)S(1)}, bf16[2,192,128]{2,1,0:T(8,128)(2,1)S(1)}, u32[]{:S(2)}, u32[]{:S(2)}) collective-permute-start(bf16[2,192,128]{2,1,0:T(8,128)(2,1)S(1)} %get-tuple-element.57), channel_id=1, source_target_pairs={{32,0},{33,1},{34,2},{35,3},{36,4},{37,5},{38,6},{39,7},{104,8},{1... | collective-permute-start | bytes 294920 | tf_op jit(solution)/shard_map/ppermute | solution.py:50
  9.9 10.8 %collective-permute-start.12 = (bf16[2,128,128]{2,1,0:T(8,128)(2,1)S(1)}, bf16[2,128,128]{2,1,0:T(8,128)(2,1)S(1)}, u32[]{:S(2)}, u32[]{:S(2)}) collective-permute-start(bf16[2,128,128]{2,1,0:T(8,128)(2,1)S(1)} %constant_dynamic-slice_fusion), channel_id=1, source_target_pairs={{2,0},{3,1},{0,2},{1,3},{6,4},{7,5},{4,6},{5,7},{14,8},{15,9},{12,... | collective-permute-start | bytes 196616 | tf_op jit(solution)/shard_map/ppermute | solution.py:50
  19.7 60.6 %collective-permute-start.18 = (bf16[256,4096]{1,0:T(8,128)(2,1)}, bf16[256,4096]{1,0:T(8,128)(2,1)}, u32[]{:S(2)}, u32[]{:S(2)}) collective-permute-start(bf16[256,4096]{1,0:T(8,128)(2,1)} %get-tuple-element.17), channel_id=1, source_target_pairs={{0,8},{1,9},{2,10},{3,11},{4,12},{5,13},{6,14},{7,15},{8,0},{9,1},... | collective-permute-start | bytes 6291464 | tf_op jit(solution)/shard_map/ppermute | solution.py:417
  24.7 15.0 %collective-permute-start.28 = (bf16[4,128,128]{2,1,0:T(8,128)(2,1)S(1)}, bf16[4,128,128]{2,1,0:T(8,128)(2,1)S(1)}, u32[]{:S(2)}, u32[]{:S(2)}) collective-permute-start(bf16[4,128,128]{2,1,0:T(8,128)(2,1)S(1)} %get-tuple-element.55), channel_id=1, source_target_pairs={{16,0},{17,1},{18,2},{19,3},{20,4},{21,5},{22,6},{23,7},{25,8},{24... | collective-permute-start | bytes 393224 | tf_op jit(solution)/shard_map/ppermute | solution.py:50
  27.9 11.6 %collective-permute-start.24 = (bf16[4,192,128]{2,1,0:T(8,128)(2,1)S(1)}, bf16[4,192,128]{2,1,0:T(8,128)(2,1)S(1)}, u32[]{:S(2)}, u32[]{:S(2)}) collective-permute-start(bf16[4,192,128]{2,1,0:T(8,128)(2,1)S(1)} %get-tuple-element.47), channel_id=1, source_target_pairs={{2,0},{3,1},{0,2},{1,3},{6,4},{7,5},{4,6},{5,7},{14,8},{15,9},{12,... | collective-permute-start | bytes 589832 | tf_op jit(solution)/shard_map/ppermute | solution.py:50
  39.7 11.1 %collective-permute-start.21 = (bf16[2,4,192,128]{3,2,1,0:T(8,128)(2,1)S(1)}, bf16[2,4,192,128]{3,2,1,0:T(8,128)(2,1)S(1)}, u32[]{:S(2)}, u32[]{:S(2)}) collective-permute-start(bf16[2,4,192,128]{3,2,1,0:T(8,128)(2,1)S(1)} %pad_maximum_fusion.16), channel_id=1, source_target_pairs={{96,0},{97,1},{98,2},{99,3},{100,4},{101,5},{102,6},{103,7},{40,8}... | collective-permute-start | bytes 1179656 | tf_op jit(solution)/shard_map/ppermute | solution.py:50
  42.1 8.6 %collective-permute-start.25 = (bf16[2,4,192,128]{3,2,1,0:T(8,128)(2,1)S(1)}, bf16[2,4,192,128]{3,2,1,0:T(8,128)(2,1)S(1)}, u32[]{:S(2)}, u32[]{:S(2)}) collective-permute-start(bf16[2,4,192,128]{3,2,1,0:T(8,128)(2,1)S(1)} %pad_maximum_fusion.17), channel_id=1, source_target_pairs={{6,0},{7,1},{4,2},{5,3},{2,4},{3,5},{0,6},{1,7},{10,8},{11,9},{8,1... | collective-permute-start | bytes 1179656 | tf_op jit(solution)/shard_map/ppermute | solution.py:50
  46.1 14.4 %collective-permute-start.16 = (bf16[4,4,128,128]{3,2,1,0:T(8,128)(2,1)S(1)}, bf16[4,4,128,128]{3,2,1,0:T(8,128)(2,1)S(1)}, u32[]{:S(2)}, u32[]{:S(2)}) collective-permute-start(bf16[4,4,128,128]{3,2,1,0:T(8,128)(2,1)S(1)} %get-tuple-element.44), channel_id=1, source_target_pairs={{32,0},{33,1},{34,2},{35,3},{36,4},{37,5},{38,6},{39,7},{104,8},{1... | collective-permute-start | bytes 1572872 | tf_op jit(solution)/shard_map/ppermute | solution.py:50
  46.5 17.1 %collective-permute-start.10 = (bf16[4,4,192,128]{3,2,1,0:T(8,128)(2,1)S(1)}, bf16[4,4,192,128]{3,2,1,0:T(8,128)(2,1)S(1)}, u32[]{:S(2)}, u32[]{:S(2)}) collective-permute-start(bf16[4,4,192,128]{3,2,1,0:T(8,128)(2,1)S(1)} %get-tuple-element.36), channel_id=1, source_target_pairs={{16,0},{17,1},{18,2},{19,3},{20,4},{21,5},{22,6},{23,7},{25,8},{24... | collective-permute-start | bytes 2359304 | tf_op jit(solution)/shard_map/ppermute | solution.py:50
  50.7 15.8 %collective-permute-start.4 = (bf16[4,4,192,128]{3,2,1,0:T(8,128)(2,1)S(1)}, bf16[4,4,192,128]{3,2,1,0:T(8,128)(2,1)S(1)}, u32[]{:S(2)}, u32[]{:S(2)}) collective-permute-start(bf16[4,4,192,128]{3,2,1,0:T(8,128)(2,1)S(1)} %get-tuple-element.38), channel_id=1, source_target_pairs={{2,0},{3,1},{0,2},{1,3},{6,4},{7,5},{4,6},{5,7},{14,8},{15,9},{12,... | collective-permute-start | bytes 2359304 | tf_op jit(solution)/shard_map/ppermute | solution.py:50
  56.3 18.7 %collective-permute-start.22 = (bf16[4,4,192,128]{3,2,1,0:T(8,128)(2,1)S(1)}, bf16[4,4,192,128]{3,2,1,0:T(8,128)(2,1)S(1)}, u32[]{:S(2)}, u32[]{:S(2)}) collective-permute-start(bf16[4,4,192,128]{3,2,1,0:T(8,128)(2,1)S(1)} %get-tuple-element.34), channel_id=1, source_target_pairs={{2,0},{3,1},{0,2},{1,3},{6,4},{7,5},{4,6},{5,7},{14,8},{15,9},{12,... | collective-permute-start | bytes 2359304 | tf_op jit(solution)/shard_map/ppermute | solution.py:50
  60.5 14.9 %collective-permute-start.26 = (bf16[4,4,192,128]{3,2,1,0:T(8,128)(2,1)S(1)}, bf16[4,4,192,128]{3,2,1,0:T(8,128)(2,1)S(1)}, u32[]{:S(2)}, u32[]{:S(2)}) collective-permute-start(bf16[4,4,192,128]{3,2,1,0:T(8,128)(2,1)S(1)} %get-tuple-element.32), channel_id=1, source_target_pairs={{16,0},{17,1},{18,2},{19,3},{20,4},{21,5},{22,6},{23,7},{25,8},{24... | collective-permute-start | bytes 2359304 | tf_op jit(solution)/shard_map/ppermute | solution.py:50
  63.6 15.6 %collective-permute-start.30 = (bf16[4,4,128,128]{3,2,1,0:T(8,128)(2,1)S(1)}, bf16[4,4,128,128]{3,2,1,0:T(8,128)(2,1)S(1)}, u32[]{:S(2)}, u32[]{:S(2)}) collective-permute-start(bf16[4,4,128,128]{3,2,1,0:T(8,128)(2,1)S(1)} %get-tuple-element.40), channel_id=1, source_target_pairs={{32,0},{33,1},{34,2},{35,3},{36,4},{37,5},{38,6},{39,7},{104,8},{1... | collective-permute-start | bytes 1572872 | tf_op jit(solution)/shard_map/ppermute | solution.py:50
  66.5 16.9 %collective-permute-start.17 = (bf16[2,4,4,128,128]{4,3,2,1,0:T(8,128)(2,1)}, bf16[2,4,4,128,128]{4,3,2,1,0:T(8,128)(2,1)S(1)}, u32[]{:S(2)}, u32[]{:S(2)}) collective-permute-start(bf16[2,4,4,128,128]{4,3,2,1,0:T(8,128)(2,1)} %pad_maximum_fusion.4.refs_5_), channel_id=1, source_target_pairs={{96,0},{97,1},{98,2},{99,3},{100,4},{101,5},{102,6},{103,7},{40,8}... | collective-permute-start | bytes 3145736 | tf_op jit(solution)/shard_map/ppermute | solution.py:50
  74.9 28.3 %collective-permute-start.11 = (bf16[2,4,4,192,128]{4,3,2,1,0:T(8,128)(2,1)}, bf16[2,4,4,192,128]{4,3,2,1,0:T(8,128)(2,1)}, u32[]{:S(2)}, u32[]{:S(2)}) collective-permute-start(bf16[2,4,4,192,128]{4,3,2,1,0:T(8,128)(2,1)} %pad_maximum_fusion.1.refs_4_), channel_id=1, source_target_pairs={{17,0},{16,1},{19,2},{18,3},{21,4},{20,5},{23,6},{22,7},{24,8},{25... | collective-permute-start | bytes 4718600 | tf_op jit(solution)/shard_map/ppermute | solution.py:50
  75.4 28.1 %collective-permute-start.5 = (bf16[2,4,4,192,128]{4,3,2,1,0:T(8,128)(2,1)}, bf16[2,4,4,192,128]{4,3,2,1,0:T(8,128)(2,1)}, u32[]{:S(2)}, u32[]{:S(2)}) collective-permute-start(bf16[2,4,4,192,128]{4,3,2,1,0:T(8,128)(2,1)} %pad_maximum_fusion.refs_3_), channel_id=1, source_target_pairs={{6,0},{7,1},{4,2},{5,3},{2,4},{3,5},{0,6},{1,7},{10,8},{11,9},{8,1... | collective-permute-start | bytes 4718600 | tf_op jit(solution)/shard_map/ppermute | solution.py:50
  80.0 49.4 %collective-permute-start.23 = (bf16[2,4,4,192,128]{4,3,2,1,0:T(8,128)(2,1)}, bf16[2,4,4,192,128]{4,3,2,1,0:T(8,128)(2,1)}, u32[]{:S(2)}, u32[]{:S(2)}) collective-permute-start(bf16[2,4,4,192,128]{4,3,2,1,0:T(8,128)(2,1)} %pad_maximum_fusion.2.refs_3_), channel_id=1, source_target_pairs={{6,0},{7,1},{4,2},{5,3},{2,4},{3,5},{0,6},{1,7},{10,8},{11,9},{8,1... | collective-permute-start | bytes 4718600 | tf_op jit(solution)/shard_map/ppermute | solution.py:50
  80.4 49.1 %collective-permute-start.27 = (bf16[2,4,4,192,128]{4,3,2,1,0:T(8,128)(2,1)}, bf16[2,4,4,192,128]{4,3,2,1,0:T(8,128)(2,1)}, u32[]{:S(2)}, u32[]{:S(2)}) collective-permute-start(bf16[2,4,4,192,128]{4,3,2,1,0:T(8,128)(2,1)} %pad_maximum_fusion.3.refs_4_), channel_id=1, source_target_pairs={{17,0},{16,1},{19,2},{18,3},{21,4},{20,5},{23,6},{22,7},{24,8},{25... | collective-permute-start | bytes 4718600 | tf_op jit(solution)/shard_map/ppermute | solution.py:50
  83.4 46.0 %collective-permute-start.31 = (bf16[2,4,4,128,128]{4,3,2,1,0:T(8,128)(2,1)S(1)}, bf16[2,4,4,128,128]{4,3,2,1,0:T(8,128)(2,1)S(1)}, u32[]{:S(2)}, u32[]{:S(2)}) collective-permute-start(bf16[2,4,4,128,128]{4,3,2,1,0:T(8,128)(2,1)S(1)} %pad_maximum_fusion.5.refs_5_), channel_id=1, source_target_pairs={{96,0},{97,1},{98,2},{99,3},{100,4},{101,5},{102,6},{103,7},{40,8}... | collective-permute-start | bytes 3145736 | tf_op jit(solution)/shard_map/ppermute | solution.py:50
  107.5 35.6 %collective-permute-start.19 = (bf16[8,256,128]{2,1,0:T(8,128)(2,1)S(1)}, bf16[8,256,128]{2,1,0:T(8,128)(2,1)S(1)}, u32[]{:S(2)}, u32[]{:S(2)}) collective-permute-start(bf16[8,256,128]{2,1,0:T(8,128)(2,1)S(1)} %shard_map.97), channel_id=1, source_target_pairs={{0,8},{1,9},{2,10},{3,11},{4,12},{5,13},{6,14},{7,15},{8,0},{9,1},... | collective-permute-start | bytes 1572872 | tf_op jit(solution)/shard_map/ppermute | solution.py:444
  134.6 20.4 %collective-permute-start.32 = (bf16[8,256,128]{2,1,0:T(8,128)(2,1)}, bf16[8,256,128]{2,1,0:T(8,128)(2,1)}, u32[]{:S(2)}, u32[]{:S(2)}) collective-permute-start(bf16[8,256,128]{2,1,0:T(8,128)(2,1)} %shard_map.102), channel_id=1, source_target_pairs={{0,8},{1,9},{2,10},{3,11},{4,12},{5,13},{6,14},{7,15},{8,0},{9,1},... | collective-permute-start | bytes 1572872 | tf_op jit(solution)/shard_map/ppermute | solution.py:444
  144.3 14.8 %all-to-all-start = ((bf16[8,256,128]{2,1,0:T(8,128)(2,1)}), bf16[8,256,128]{2,1,0:T(8,128)(2,1)}, u32[]{:S(2)}, u32[]{:S(2)}) async-start(bf16[8,256,128]{2,1,0:T(8,128)(2,1)} %copy-done.3), calls=%async_computation | async-start | bytes 1048576 | tf_op jit(solution)/shard_map/all_to_all | solution.py:446
  159.1 15.2 %all-to-all-start.1 = ((bf16[8,256,128]{2,1,0:T(8,128)(2,1)}), bf16[8,256,128]{2,1,0:T(8,128)(2,1)S(1)}, u32[]{:S(2)}, u32[]{:S(2)}) async-start(bf16[8,256,128]{2,1,0:T(8,128)(2,1)} %shard_map.103), calls=%async_computation.1 | async-start | bytes 1048576 | tf_op jit(solution)/shard_map/all_to_all | solution.py:446
  (26 other events, 135.6 us)

commit v2 on v0

v2 whole, which is shorter than its diff:
```python
import functools
import math

import jax
import jax.numpy as jnp
from jax import lax
from jax.experimental import pallas as pl
from jax.experimental.pallas import tpu as pltpu
from jax.sharding import Mesh
from jax.sharding import PartitionSpec as P

HQ = 64
KVH = 8
HD = 128
STEPS = 4
B = 32
GROUP = HQ // KVH
ROWS = STEPS * GROUP
AXES = ("z", "ylo", "core", "x", "yhi")
SEQ, HEAD = AXES[:3], AXES[3:]
X, Y, Z = 0, 1, 2
MIB = 1024 * 1024
LIMIT = 8
VMEM = pl.BlockSpec(memory_space=pltpu.VMEM)
SMEM = pl.BlockSpec(memory_space=pltpu.SMEM)

HALF = 256


def place(n):
    s, h = n >> 3, n & 7
    return [h >> 1, (h & 1) * 2 + ((s >> 1) & 1), s >> 2, s & 1]


def flat(x, y, z, core):
    return (((z * 2 + (y & 1)) * 2 + core) * 4 + x) * 2 + (y >> 1)


def exchange(dim, step):
    pairs = []
    for n in range(128):
        spot = place(n)
        spot[dim] ^= (1, 3)[spot[3] ^ step]
        pairs.append((flat(*spot), n))
    return pairs


def flipped(x=0, y=0, core=0):
    pairs = []
    for n in range(128):
        spot = place(n)
        pairs.append((flat(spot[0] ^ x, spot[1] ^ y, spot[2], spot[3] ^ core), n))
    return pairs


def swap(value, dim, step):
    return lax.ppermute(value, AXES, exchange(dim, step))


def together(*values):
    return lax.optimization_barrier(values)


def doubled(block, dim):
    pair = jnp.stack([block, swap(block, dim, 0)])
    return jnp.concatenate([pair, swap(pair, dim, 1)])


def rope_freqs():
    indices = jnp.arange(HD // 2, dtype=jnp.float32)
    base_freq = jnp.exp(-2.0 * indices / HD * math.log(500000.0))
    wavelength = 2.0 * math.pi / base_freq
    blend_weight = (8192.0 / wavelength - 1.0) / 3.0
    middle = (1.0 - blend_weight) * base_freq / 8.0 + blend_weight * base_freq
    return jnp.where(
        wavelength > 8192.0, base_freq / 8.0, jnp.where(wavelength < 2048.0, base_freq, middle)
    )


def tables(position, freqs):
    angles = position.astype(jnp.float32)[..., None] * freqs
    cosine, sine = jnp.cos(angles), jnp.sin(angles)
    return jnp.concatenate([cosine, cosine], -1), jnp.concatenate([-sine, sine], -1)


def rotated(vectors, cosine, sine):
    half = HD // 2
    swapped = jnp.concatenate([vectors[..., half:], vectors[..., :half]], -1)
    return vectors * cosine + swapped * sine


def prep_kernel(spot, hidden, gain, own, side, across, corner, total):
    step = pl.program_id(1)
    mine = 2 * (spot[1] & 1) + spot[3]
    x = hidden[...].astype(jnp.float32)

    @pl.when(pl.program_id(0) == 0)
    def _():
        squares = x * x
        part = sum(squares[:, 128 * i : 128 * i + 128] for i in range(16))

        @pl.when(step == 0)
        def _():
            total[...] = part

        @pl.when(step > 0)
        def _():
            total[...] += part

        @pl.when(step == 3)
        def _():
            mean = jnp.sum(total[...], axis=1, keepdims=True) / 8192.0
            total[...] = jnp.broadcast_to(lax.rsqrt(mean + 1e-05), (256, 128))

    @pl.when(pl.program_id(0) == 1)
    def _():
        normed = (x * total[:, :1] * gain[...]).astype(jnp.bfloat16)
        quarters = [normed[:, 512 * i : 512 * i + 512] for i in range(4)]
        for at in range(2):
            lanes = pl.ds(pl.multiple_of(1024 * at + HALF * step, HALF), HALF)
            blocks = [quarter[:, HALF * at : HALF * at + HALF] for quarter in quarters]
            for owner in range(4):

                @pl.when(mine == owner)
                def _():
                    own[:, lanes] = blocks[owner]
                    side[:, lanes] = blocks[owner ^ 1]
                    across[:, lanes] = blocks[owner ^ 2]
                    corner[:, lanes] = blocks[owner ^ 3]


def prep(spot, hidden, gain):
    block = lambda turn, step, spot: (0, step)
    whole = lambda turn, step, spot: (0, 0)
    return pl.pallas_call(
        prep_kernel,
        out_shape=(
            *[jax.ShapeDtypeStruct((256, 2048), jnp.bfloat16)] * 4,
        ),
        grid_spec=pltpu.PrefetchScalarGridSpec(
            num_scalar_prefetch=1,
            grid=(2, 4),
            in_specs=[pl.BlockSpec((256, 2048), block), pl.BlockSpec((1, 2048), block)],
            out_specs=[pl.BlockSpec((256, 2048), whole)] * 4,
            scratch_shapes=[pltpu.VMEM((256, 128), jnp.float32)],
        ),
        compiler_params=pltpu.CompilerParams(vmem_limit_bytes=20 * MIB),
        cost_estimate=pl.CostEstimate(flops=1_000_000, bytes_accessed=MIB // 4, transcendentals=0),
    )(spot, hidden, gain)


def product_kernel(slots, inputs, carried, narrow, spot, *refs):
    x_refs, refs = refs[:inputs], refs[inputs:]
    piece_refs, refs = refs[: 2 * len(slots)], refs[2 * len(slots) :]
    if carried:
        before, refs = refs[:inputs], refs[inputs:]
    if narrow:
        out, sums = refs[0], refs[1:]
    else:
        sums = refs
    mine = [spot[0], spot[1], spot[2]]
    core = spot[3]
    flips = [0, 1 + 2 * core, 3 - 2 * core, 2]

    def slot_of(flip):
        return jnp.where(flip == 0, 0, jnp.where(flip == flips[1], 1, jnp.where(flip == flips[2], 2, 3)))

    for i in range(inputs):
        sums[i][...] = before[i][...] if carried else jnp.zeros_like(sums[i])

    def add(x_at, depth, weight, heads):
        for x_ref, total in zip(x_refs, sums):
            left = x_ref[:, pl.ds(pl.multiple_of(x_at, HALF), depth)]
            result = jnp.dot(left, weight, preferred_element_type=jnp.float32)
            for i, (head, kind) in enumerate(heads):
                total[kind, head] += result[:, 128 * i : 128 * i + 128]

    z_slots = [slot_of(z ^ mine[Z]) for z in range(4)]
    yhi = [mine[Y] >> 1, 1 - (mine[Y] >> 1)]
    places = [(ys, kind) for ys in range(2) for kind in range(2)]
    for i, slot in enumerate(slots):
        ref = piece_refs[2 * i]
        x = mine[X] ^ flips[slot]
        weight = jnp.concatenate(
            [jnp.concatenate([ref[s, ys, kind] for ys, kind in places], 1) for s in z_slots], 0
        )
        add(0, 1024, weight, [(2 * x + yhi[ys], kind) for ys, kind in places])
        ref = piece_refs[2 * i + 1]
        z = mine[Z] ^ flips[slot]
        for xs in range(4):
            weight = jnp.concatenate([ref[xs, ys, kind] for ys, kind in places], 1)
            x = mine[X] ^ flips[xs]
            add(1024 + HALF * z, HALF, weight, [(2 * x + yhi[ys], kind) for ys, kind in places])
    if narrow:
        for i in range(inputs):
            out[i] = sums[i][...].astype(out.dtype)


def product(spot, rows, pieces, slots, before=None, narrow=False):
    carried = before is not None
    shape = (2, KVH, 256, HD)
    count = len(rows)
    if narrow:
        out_shape = [jax.ShapeDtypeStruct((count, *shape), jnp.bfloat16)]
    else:
        out_shape = [jax.ShapeDtypeStruct(shape, jnp.float32)] * count
    return pl.pallas_call(
        functools.partial(product_kernel, slots, count, carried, narrow),
        out_shape=out_shape,
        in_specs=[SMEM] + [VMEM] * (count + len(pieces) + (count if carried else 0)),
        out_specs=[VMEM] * len(out_shape),
        scratch_shapes=[pltpu.VMEM(shape, jnp.float32)] * (count if narrow else 0),
        compiler_params=pltpu.CompilerParams(vmem_limit_bytes=LIMIT * MIB),
        cost_estimate=pl.CostEstimate(flops=1_000_000, bytes_accessed=MIB // 4, transcendentals=0),
    )(spot, *rows, *pieces, *(before or ()))


def finish_kernel(spot, own, across, side, *refs):
    out = refs[-1]
    mine = spot[1] & 1
    for i, part in enumerate((own, across)):
        for kind in range(2):
            for head in range(KVH):
                value = part[kind, head] + side[i, kind, head].astype(jnp.float32)
                if kind == 0:
                    value = value * refs[2 * i][...] + pltpu.roll(value, HD // 2, 1) * refs[2 * i + 1][...]
                out[mine ^ i, head, kind] = value.astype(jnp.bfloat16)


def finish(spot, own, across, side, angles):
    out = pl.pallas_call(
        finish_kernel,
        out_shape=jax.ShapeDtypeStruct((2, KVH, 2, 256, HD), jnp.bfloat16),
        in_specs=[SMEM] + [VMEM] * (3 + len(angles)),
        out_specs=VMEM,
        compiler_params=pltpu.CompilerParams(vmem_limit_bytes=8 * MIB),
        cost_estimate=pl.CostEstimate(flops=4_000_000, bytes_accessed=MIB, transcendentals=0),
    )(spot, own, across, side, *angles)
    return out.reshape(16, 2, 256, HD)


def cache_of(received, kind):
    blocks = [
        (received[i, kind].astype(jnp.float32) + received[8 + i, kind].astype(jnp.float32)).reshape(B, 8, HD)
        for i in range(8)
    ]
    return jnp.stack(blocks, axis=1).reshape(B, 64, HD)


def split(value):
    high = value.astype(jnp.bfloat16)
    return high, (value - high.astype(jnp.float32)).astype(jnp.bfloat16)


NT = (((1,), (1,)), ((), ()))


def line_of(peak, total):
    row = lax.broadcasted_iota(jnp.int32, (2 * ROWS, 128), 0)
    lane = lax.broadcasted_iota(jnp.int32, (2 * ROWS, 128), 1)
    line = jnp.where(row == lane, peak, 0.0) + jnp.where(row + 64 == lane, total, 0.0)
    line = jnp.sum(line, axis=0, keepdims=True)
    high = line.astype(jnp.bfloat16).astype(jnp.float32)
    middle = (line - high).astype(jnp.bfloat16).astype(jnp.float32)
    at = lax.broadcasted_iota(jnp.int32, (16, 128), 0)
    terms = jnp.where(at == 0, high, jnp.where(at == 1, middle, line - high - middle))
    return jnp.where(at < 3, terms, 0.0).astype(jnp.bfloat16)


def scored(query, keys, length, column):
    both = lax.dot_general(jnp.concatenate(split(query), 0), keys, NT, preferred_element_type=jnp.float32)
    return jnp.where(column < length, (both[:ROWS] + both[ROWS:]) * (1.0 / math.sqrt(HD)), -1e30)


def weighted(weight, values):
    both = jnp.dot(jnp.concatenate(split(weight), 0), values, preferred_element_type=jnp.float32)
    return both[:ROWS] + both[ROWS:]


def attend_kernel(spot, lengths, received, query, fresh_keys, fresh_values, keys, values, packed, scores):
    seq = spot[4]
    keys[...] = cache_of(received, 0).astype(jnp.bfloat16)
    values[...] = cache_of(received, 1).astype(jnp.bfloat16)
    column = lax.broadcasted_iota(jnp.int32, (ROWS, 64), 1) + seq * 64
    for b in range(B):
        scores[pl.ds(ROWS * b, ROWS)] = scored(query[b], keys[b], lengths[b], column)
    score = scores[...]
    peak = jnp.max(score, axis=1, keepdims=True)
    weight = jnp.where(score > -1e29, jnp.exp(score - peak), 0.0)
    total = jnp.sum(weight, axis=1, keepdims=True)
    for b in range(B):
        mixed = weighted(weight[ROWS * b : ROWS * b + ROWS], values[b])
        packed[b // 2, pl.ds(ROWS * (b % 2), ROWS)] = mixed.astype(jnp.bfloat16)
    for pair in range(B // 2):
        rows = slice(2 * ROWS * pair, 2 * ROWS * pair + 2 * ROWS)
        packed[pair, pl.ds(64, 16)] = line_of(peak[rows], total[rows])

    late = lax.broadcasted_iota(jnp.int32, (ROWS, 8), 1)
    token = lax.broadcasted_iota(jnp.int32, (ROWS, 8), 0) // GROUP
    peaks, totals = [], []
    for i in range(2):
        b = 2 * seq + i
        score = scored(query[b], keys[b], lengths[b], column)
        late_score = (1.0 / math.sqrt(HD)) * lax.dot_general(
            query[b], fresh_keys[b], NT, preferred_element_type=jnp.float32, precision=lax.Precision.HIGHEST
        )
        late_score = jnp.where(late <= token, late_score, -1e30)
        peak = jnp.maximum(jnp.max(score, axis=1, keepdims=True), jnp.max(late_score, axis=1, keepdims=True))
        weight = jnp.where(score > -1e29, jnp.exp(score - peak), 0.0)
        late_weight = jnp.where(late <= token, jnp.exp(late_score - peak), 0.0)
        mixed = weighted(weight, values[b]) + weighted(late_weight, fresh_values[b])
        packed[seq, pl.ds(ROWS * i, ROWS)] = mixed.astype(jnp.bfloat16)
        peaks.append(peak)
        totals.append(jnp.sum(weight, axis=1, keepdims=True) + jnp.sum(late_weight, axis=1, keepdims=True))
    packed[seq, pl.ds(64, 16)] = line_of(jnp.concatenate(peaks, 0), jnp.concatenate(totals, 0))


def attend(spot, lengths, received, query, fresh_keys, fresh_values):
    return pl.pallas_call(
        attend_kernel,
        out_shape=(
            jax.ShapeDtypeStruct((B, 64, HD), jnp.bfloat16),
            jax.ShapeDtypeStruct((B, 64, HD), jnp.bfloat16),
            jax.ShapeDtypeStruct((B // 2, 80, HD), jnp.bfloat16),
        ),
        in_specs=[SMEM, SMEM] + [VMEM] * 4,
        out_specs=[VMEM] * 3,
        scratch_shapes=[pltpu.VMEM((B * ROWS, 64), jnp.float32)],
        compiler_params=pltpu.CompilerParams(vmem_limit_bytes=16 * MIB),
        cost_estimate=pl.CostEstimate(flops=60_000_000, bytes_accessed=4 * MIB, transcendentals=70_000),
    )(spot, lengths, received, query, fresh_keys, fresh_values)


def merge_kernel(parts, out):
    lines = [jnp.sum(parts[i, 64:80].astype(jnp.float32), axis=0, keepdims=True) for i in range(16)]
    marks = jnp.concatenate(lines, 0)
    lane = lax.broadcasted_iota(jnp.int32, (16, 128), 1)
    peak = jnp.max(marks, axis=0, keepdims=True)
    grow = jnp.where(lane < 64, jnp.exp(marks - peak), 0.0)
    total = jnp.sum(grow * pltpu.roll(marks, 64, 1), axis=0, keepdims=True)
    share = grow / jnp.where(lane[:1] < 64, total, 1.0)
    columns = jnp.concatenate([share, jnp.zeros((112, 128), jnp.float32)], 0).T
    result = sum(parts[i, :64].astype(jnp.float32) * columns[:64, i : i + 1] for i in range(16))
    for i in range(STEPS):
        rows = [
            jnp.concatenate(
                [result[at + r : at + r + 1] for r in range(GROUP)], 1
            )
            for at in (GROUP * i, ROWS + GROUP * i)
        ]
        out[i] = jnp.concatenate(rows, 0).astype(jnp.bfloat16)


def merge(parts):
    return pl.pallas_call(
        merge_kernel,
        out_shape=jax.ShapeDtypeStruct((STEPS, 2, GROUP * HD), jnp.bfloat16),
        in_specs=[VMEM],
        out_specs=VMEM,
        cost_estimate=pl.CostEstimate(flops=300_000, bytes_accessed=MIB, transcendentals=2048),
    )(parts)


def shards(context_hidden, norm_gain, kv_weight, queries, new_kv, lengths, slab_start):
    seq, head = lax.axis_index(SEQ), lax.axis_index(HEAD)
    z, ylo, core = seq >> 2, (seq >> 1) & 1, seq & 1
    x, yhi = head >> 1, head & 1
    spot = jnp.stack([x, yhi * 2 + ylo, z, core, seq]).astype(jnp.int32)

    weight = jnp.stack([kv_weight, lax.ppermute(kv_weight, AXES, flipped(y=2))])
    own_rows, to_side, to_across, to_corner = prep(
        spot, context_hidden.reshape(256, 8192), norm_gain.reshape(1, 8192)
    )
    weight, own_rows = together(weight, own_rows)
    corner_rows = lax.ppermute(to_corner, AXES, flipped(y=1))
    across_rows = lax.ppermute(to_across, AXES, flipped(y=1))
    side_rows = lax.ppermute(to_side, AXES, flipped(core=1))
    middle, last = (Z, X), (X, Z)
    halves = [weight[:, :, :HALF], weight[:, :, HALF:]]
    firsts = [swap(half, dim, 0) for half, dim in zip(halves, middle)]
    firsts = together(*firsts)
    pairs = [jnp.stack(pair) for pair in zip(halves, firsts)]
    seconds = [swap(pair, dim, 1) for pair, dim in zip(pairs, middle)]
    blocks = [jnp.concatenate(both) for both in zip(pairs, seconds)]
    blocks, side_rows, queries, new_kv, slab_start = together(blocks, side_rows, queries, new_kv, slab_start)

    one = [swap(block, dim, 0) for block, dim in zip(blocks, last)]
    two = [swap(block, dim, 1) for block, dim in zip(blocks, last)]
    one, two, corner_rows = together(one, two, corner_rows)
    far = [swap(block, dim, 1) for block, dim in zip(one, last)]
    corner_rows = lax.ppermute(corner_rows, AXES, flipped(core=1))

    freqs = rope_freqs()
    angles = ()
    for near in (seq, seq ^ 2):
        position = slab_start[:, None] + (near * 8 + head) * 8 + jnp.arange(8, dtype=jnp.int32)[None, :]
        angles += tables(position.reshape(256), freqs)
    step_pos = (slab_start + lengths)[:, None] + jnp.arange(STEPS, dtype=jnp.int32)[None, :]
    step_cos, step_sin = tables(step_pos, freqs)
    query = queries.astype(jnp.float32).reshape(STEPS, B, GROUP, HD).transpose(1, 0, 2, 3)
    query = rotated(query, step_cos[:, :, None], step_sin[:, :, None]).reshape(B, ROWS, HD)
    fresh = new_kv.astype(jnp.float32).transpose(0, 2, 1, 3)
    padding = ((0, 0), (0, 8 - STEPS), (0, 0))
    fresh_keys = jnp.pad(rotated(fresh[0], step_cos, step_sin), padding)
    fresh_values = jnp.pad(new_kv[1].transpose(1, 0, 2), padding)
    spot_ready, *_ = together(spot, query, fresh_keys, fresh_values, angles)

    near = [*blocks, *one, *two]
    own, side = product(spot_ready, [own_rows, side_rows], near, (0, 1, 2))
    spot_later, own, side = together(spot_ready, own, side)
    corner, across = product(spot_later, [corner_rows, across_rows], near, (0, 1, 2))
    (sent,) = product(spot, [side_rows, corner_rows], far, (3,), [side, corner], narrow=True)
    side = lax.ppermute(sent, AXES, flipped(core=1))
    own, across = product(spot, [own_rows, across_rows], far, (3,), [own, across])
    rows = finish(spot, own, across, side, angles)
    received = lax.all_to_all(rows, ("ylo", "x", "yhi"), 0, 0)
    k_cache, v_cache, packed = attend(spot, lengths, received, query, fresh_keys, fresh_values)
    parts = lax.all_to_all(packed, SEQ, 0, 0)
    attention = merge(parts)
    return k_cache, v_cache, attention


def solution(mesh):
    fine = Mesh(mesh.devices.reshape(4, 2, 2, 4, 2), AXES)
    return jax.shard_map(
        shards,
        mesh=fine,
        in_specs=(
            P(None, AXES, None),
            P(),
            P(None, SEQ, HEAD),
            P(None, None, HEAD),
            P(None, None, None, HEAD),
            P(),
            P(),
        ),
        out_specs=(P(None, SEQ, HEAD), P(None, SEQ, HEAD), P(None, SEQ, HEAD)),
        check_vma=False,
    )
```

time: 409 us -> 140 us (0.34)
  waiting for transfers between devices: 256 us -> 31.1 us
  local copies, waits for them, and re-layouts: 39.9 us -> 4.76 us
  Pallas kernels: 0 us -> 29.9 us
  other arithmetic: 29.3 us -> 5.8 us
  matrix products: 19.6 us -> 0 us
  starting transfers between devices: 6.72 us -> 22.9 us
  between operations: 14 us -> 0.94 us
    all_gather x3 -> x0, waiting for transfers between devices: 241 us -> none  [the longest x1 167 us: shards(): lax.all_gather(all_columns, 'seq', axis=1, tiled=True)]
    all_to_all x0 -> x2, blocking collectives: none -> 44.2 us  [the longest x1 30.7 us: shards(): received = lax.all_to_all(rows, ('ylo', 'x', 'yhi'), 0, 0)]
    all_gather x2 -> x0, blocking collectives: 41.3 us -> none  [merged_2(): pieces = jax.tree.map(lambda part: lax.all_gather(part, axis), value)]
    ppermute x0 -> x16, waiting for transfers between devices: none -> 31.1 us  [the longest x10 24.5 us: swap(): return lax.ppermute(value, AXES, exchange(dim, step))]
    pallas_call x0 -> x8, Pallas kernels: none -> 29.9 us  [the longest x4 17.6 us: product(): pl.pallas_call(functools.partial(product_kernel, slots, count, carried, n...]
    ppermute x0 -> x16, starting transfers between devices: none -> 22.9 us  [the longest x10 11.6 us: swap(): return lax.ppermute(value, AXES, exchange(dim, step))]
    add x18 -> x2, other arithmetic: 22.6 us -> 0.18 us  [the longest x1 0.17 us: rotated(): return vectors * cosine + swapped * sine]
    dot_general x5 -> x0, matrix products: 19.6 us -> none  [the longest x1 16.3 us: shards(): jnp.einsum('td,kdc->ktc', normed, lax.all_gather(all_columns, 'seq', axis...]
  transfers between devices with their start and end apart: 4 -> 16, of which waited for: 4 -> 9; matrix products, arithmetic and copies ran while one was open for 2% -> 5% of each run, Pallas kernels for 0% -> 15%
where the time goes in v2:
time: 140 us
  blocking collectives  44.2 us (32%)
  waiting for transfers between devices  31.1 us (22%)
  Pallas kernels  29.9 us (21%)
  starting transfers between devices  22.9 us (16%)
  other arithmetic  5.8 us (4%)
  local copies, waits for them, and re-layouts  4.76 us (3%)
    all_to_all x1, blocking collectives, shards(): received = lax.all_to_all(rows, ('ylo', 'x', 'yhi'), 0, 0)  30.7 us
    ppermute x10, waiting for transfers between devices, swap(): return lax.ppermute(value, AXES, exchange(dim, step))  24.5 us
    pallas_call x4, Pallas kernels, product(): pl.pallas_call(functools.partial(product_kernel, slots, count, carried, n...  17.6 us
    all_to_all x1, blocking collectives, shards(): parts = lax.all_to_all(packed, SEQ, 0, 0)  13.5 us
    ppermute x10, starting transfers between devices, swap(): return lax.ppermute(value, AXES, exchange(dim, step))  11.6 us
    pallas_call x1, Pallas kernels, prep(): pl.pallas_call(prep_kernel, out_shape=(*[jax.ShapeDtypeStruct((256, 2048)...  6.42 us
    ppermute x1, waiting for transfers between devices, shards(): corner_rows = lax.ppermute(to_corner, AXES, flipped(y=1))  4.87 us
    ppermute x1, starting transfers between devices, shards(): corner_rows = lax.ppermute(corner_rows, AXES, flipped(core=1))  4.24 us
  transfers between devices with their start and end apart: 16, of which 9 were waited for; matrix products, arithmetic and copies ran while one was open for 5% of the time, Pallas kernels for 15%

profile of v2, /device:TPU:1, one launch (start us, length us, event | category | flops | bytes accessed | tf_op | source)
XLA Modules:
  0.0 139.6 jit_solution(14038166379663493681)
XLA Ops:
  0.6 3.8 %collective-permute-start = (bf16[2,512,128]{2,1,0:T(8,128)(2,1)}, bf16[2,512,128]{2,1,0:T(8,128)(2,1)S(1)}, u32[]{:S(2)}, u32[]{:S(2)}) collective-permute-start(bf16[2,512,128]{2,1,0:T(8,128)(2,1)} %param.9), channel_id=1, source_target_pairs={{1,0},{0,1},{3,2},{2,3},{5,4},{4,5},{7,6},{6,7},{9,8},{8,9},{11,10... | collective-permute-start | bytes 786440 | tf_op jit(solution)/shard_map/ppermute | solution.py:370
  4.5 2.2 %copy-done = bf16[32,8,8192]{2,1,0:T(8,128)(2,1)S(1)} copy-done((bf16[32,8,8192]{2,1,0:T(8,128)(2,1)S(1)}, bf16[32,8,8192]{2,1,0:T(8,128)(2,1)}, u32[]{:S(2)}) %copy-start) | copy-done | bytes 4194328
  7.5 6.4 %shard_map.94 = (bf16[256,2048]{1,0:T(8,128)(2,1)S(1)}, bf16[256,2048]{1,0:T(8,128)(2,1)}, bf16[256,2048]{1,0:T(8,128)(2,1)S(1)}, bf16[256,2048]{1,0:T(8,128)(2,1)}) custom-call(s32[5]{0:T(128)S(1)} %stack.50.spot, bf16[256,8192]{1,0:T(8,128)(2,1)S(1)} %bitcast.49, f32[1,8192]{1,0:T(1,128)S(1)} %bitcast.50), custom_call_target="tpu_custom_call" | custom-call | flops 1000000 | bytes 262144 | tf_op jit(solution)/shard_map/pallas_call | solution.py:135
  14.2 3.8 %collective-permute-start.2 = (bf16[2,2,256,128]{3,2,1,0:T(8,128)(2,1)S(1)}, bf16[2,2,256,128]{3,2,1,0:T(8,128)(2,1)S(1)}, u32[]{:S(2)}, u32[]{:S(2)}) collective-permute-start(bf16[2,2,256,128]{3,2,1,0:T(8,128)(2,1)S(1)} %get-tuple-element.74), channel_id=1, source_target_pairs={{32,0},{33,1},{34,2},{35,3},{36,4},{37,5},{38,6},{39,7},{104,8},{1... | collective-permute-start | bytes 786440 | tf_op jit(solution)/shard_map/ppermute | solution.py:57
  18.0 2.5 %collective-permute-start.3 = (bf16[2,2,256,128]{3,2,1,0:T(8,128)(2,1)S(1)}, bf16[2,2,256,128]{3,2,1,0:T(8,128)(2,1)S(1)}, u32[]{:S(2)}, u32[]{:S(2)}) collective-permute-start(bf16[2,2,256,128]{3,2,1,0:T(8,128)(2,1)S(1)} %get-tuple-element.73), channel_id=1, source_target_pairs={{2,0},{3,1},{0,2},{1,3},{6,4},{7,5},{4,6},{5,7},{14,8},{15,9},{12,... | collective-permute-start | bytes 786440 | tf_op jit(solution)/shard_map/ppermute | solution.py:57
  21.8 2.7 %collective-permute-done.3 = bf16[2,2,256,128]{3,2,1,0:T(8,128)(2,1)S(1)} collective-permute-done((bf16[2,2,256,128]{3,2,1,0:T(8,128)(2,1)S(1)}, bf16[2,2,256,128]{3,2,1,0:T(8,128)(2,1)S(1)}, u32[]{:S(2)}, u32[]{:S(2)}) %collective-permute-start.3) | collective-permute-done | bytes 262176 | tf_op jit(solution)/shard_map/ppermute | solution.py:57
  25.9 7.1 %collective-permute-done.5 = bf16[2,2,2,256,128]{4,3,2,1,0:T(8,128)(2,1)} collective-permute-done((bf16[2,2,2,256,128]{4,3,2,1,0:T(8,128)(2,1)S(1)}, bf16[2,2,2,256,128]{4,3,2,1,0:T(8,128)(2,1)}, u32[]{:S(2)}, u32[]{:S(2)}) %collective-permute-start.5) | collective-permute-done | bytes 524320 | tf_op jit(solution)/shard_map/ppermute | solution.py:57
  36.7 1.8 %collective-permute-start.7 = (bf16[4,2,2,256,128]{4,3,2,1,0:T(8,128)(2,1)S(1)}, bf16[4,2,2,256,128]{4,3,2,1,0:T(8,128)(2,1)}, u32[]{:S(2)}, u32[]{:S(2)}) collective-permute-start(bf16[4,2,2,256,128]{4,3,2,1,0:T(8,128)(2,1)S(1)} %pad_maximum_fusion.refs_2_), channel_id=1, source_target_pairs={{2,0},{3,1},{0,2},{1,3},{6,4},{7,5},{4,6},{5,7},{14,8},{15,9},{12,... | collective-permute-start | bytes 3145736 | tf_op jit(solution)/shard_map/ppermute | solution.py:57
  41.2 4.9 %collective-permute-done.11 = bf16[256,2048]{1,0:T(8,128)(2,1)} collective-permute-done((bf16[256,2048]{1,0:T(8,128)(2,1)}, bf16[256,2048]{1,0:T(8,128)(2,1)}, u32[]{:S(2)}, u32[]{:S(2)}) %collective-permute-start.11) | collective-permute-done | bytes 1048608 | tf_op jit(solution)/shard_map/ppermute | solution.py:375
  46.5 7.4 %collective-permute-done.10.refs_7_ = bf16[4,2,2,256,128]{4,3,2,1,0:T(8,128)(2,1)} collective-permute-done((bf16[4,2,2,256,128]{4,3,2,1,0:T(8,128)(2,1)S(1)}, bf16[4,2,2,256,128]{4,3,2,1,0:T(8,128)(2,1)}, u32[]{:S(2)}, u32[]{:S(2)}) %collective-permute-start.10) | collective-permute-done | bytes 1048608 | tf_op jit(solution)/shard_map/ppermute | solution.py:57
  53.9 3.4 %collective-permute-done.7.refs_4_ = bf16[4,2,2,256,128]{4,3,2,1,0:T(8,128)(2,1)} collective-permute-done((bf16[4,2,2,256,128]{4,3,2,1,0:T(8,128)(2,1)S(1)}, bf16[4,2,2,256,128]{4,3,2,1,0:T(8,128)(2,1)}, u32[]{:S(2)}, u32[]{:S(2)}) %collective-permute-start.7) | collective-permute-done | bytes 1048608 | tf_op jit(solution)/shard_map/ppermute | solution.py:57
  57.8 2.1 %collective-permute-done.9.refs_6_ = bf16[4,2,2,256,128]{4,3,2,1,0:T(8,128)(2,1)} collective-permute-done((bf16[4,2,2,256,128]{4,3,2,1,0:T(8,128)(2,1)S(1)}, bf16[4,2,2,256,128]{4,3,2,1,0:T(8,128)(2,1)}, u32[]{:S(2)}, u32[]{:S(2)}) %collective-permute-start.9) | collective-permute-done | bytes 1048608 | tf_op jit(solution)/shard_map/ppermute | solution.py:57
  59.9 4.2 %collective-permute-start.14 = (bf16[256,2048]{1,0:T(8,128)(2,1)}, bf16[256,2048]{1,0:T(8,128)(2,1)S(1)}, u32[]{:S(2)}, u32[]{:S(2)}) collective-permute-start(bf16[256,2048]{1,0:T(8,128)(2,1)} %collective-permute-done.11), channel_id=1, source_target_pairs={{8,0},{9,1},{10,2},{11,3},{12,4},{13,5},{14,6},{15,7},{0,8},{1,9},... | collective-permute-start | bytes 3145736 | tf_op jit(solution)/shard_map/ppermute | solution.py:391
  67.7 6.5 %shard_map.95 = (f32[2,8,256,128]{3,2,1,0:T(8,128)S(1)}, f32[2,8,256,128]{3,2,1,0:T(8,128)S(1)}) custom-call(s32[5]{0:T(128)S(1)} %stack.50.spot, bf16[256,2048]{1,0:T(8,128)(2,1)S(1)} %get-tuple-element.36.refs_0_, bf16[256,2048]{1,0:T(8,128)(2,1)} %collective-permute-done.6.refs_1_.refs_0_, bf16[4,2,2,256,128]{4,3,2,1,0:T(8,128)(2,1)S(1)} %pad_maximum_fusion.refs_2_, ...), custom_call_target="tpu_custom_call" | custom-call | flops 1000000 | bytes 262144 | tf_op jit(solution)/shard_map/pallas_call | solution.py:207
  74.2 6.2 %shard_map.96 = (f32[2,8,256,128]{3,2,1,0:T(8,128)S(1)}, f32[2,8,256,128]{3,2,1,0:T(8,128)S(1)}) custom-call(s32[5]{0:T(128)S(1)} %stack.50.spot, bf16[256,2048]{1,0:T(8,128)(2,1)S(1)} %collective-permute-done.14.refs_0_.refs_1_, bf16[256,2048]{1,0:T(8,128)(2,1)S(1)} %collective-permute-done.1.refs_1_, ...), custom_call_target="tpu_custom_call" | custom-call | flops 1000000 | bytes 262144 | tf_op jit(solution)/shard_map/pallas_call | solution.py:207
  80.4 2.9 %shard_map.98 = bf16[2,2,8,256,128]{4,3,2,1,0:T(8,128)(2,1)S(1)} custom-call(s32[5]{0:T(128)S(1)} %stack.50.spot, bf16[256,2048]{1,0:T(8,128)(2,1)} %collective-permute-done.6.refs_1_.refs_0_, bf16[256,2048]{1,0:T(8,128)(2,1)S(1)} %collective-permute-done.14.refs_0_.refs_1_, bf16[4,2,2,256,128]{4,3,2,1,0:T(8,128)(2,1)S(1)} %collective-permute-done.12.refs_2_, ...), custom_call_target="tpu_custom_call" | custom-call | flops 1000000 | bytes 262144 | tf_op jit(solution)/shard_map/pallas_call | solution.py:207
  83.4 2.4 %collective-permute-start.15 = (bf16[2,2,8,256,128]{4,3,2,1,0:T(8,128)(2,1)S(1)}, bf16[2,2,8,256,128]{4,3,2,1,0:T(8,128)(2,1)S(1)}, u32[]{:S(2)}, u32[]{:S(2)}) collective-permute-start(bf16[2,2,8,256,128]{4,3,2,1,0:T(8,128)(2,1)S(1)} %shard_map.98), channel_id=1, source_target_pairs={{8,0},{9,1},{10,2},{11,3},{12,4},{13,5},{14,6},{15,7},{0,8},{1,9},... | collective-permute-start | bytes 6291464 | tf_op jit(solution)/shard_map/ppermute | solution.py:413
  85.8 2.0 %shard_map.97 = (f32[2,8,256,128]{3,2,1,0:T(8,128)S(1)}, f32[2,8,256,128]{3,2,1,0:T(8,128)S(1)}) custom-call(s32[5]{0:T(128)S(1)} %stack.50.spot, bf16[256,2048]{1,0:T(8,128)(2,1)S(1)} %get-tuple-element.36.refs_0_, bf16[256,2048]{1,0:T(8,128)(2,1)S(1)} %collective-permute-done.1.refs_1_, bf16[4,2,2,256,128]{4,3,2,1,0:T(8,128)(2,1)S(1)} %collective-permute-done.12.refs_2_, ...), custom_call_target="tpu_custom_call" | custom-call | flops 1000000 | bytes 262144 | tf_op jit(solution)/shard_map/pallas_call | solution.py:207
  87.8 1.7 %collective-permute-done.15.side = bf16[2,2,8,256,128]{4,3,2,1,0:T(8,128)(2,1)S(1)} collective-permute-done((bf16[2,2,8,256,128]{4,3,2,1,0:T(8,128)(2,1)S(1)}, bf16[2,2,8,256,128]{4,3,2,1,0:T(8,128)(2,1)S(1)}, u32[]{:S(2)}, u32[]{:S(2)}) %collective-permute-start.15) | collective-permute-done | bytes 2097184 | tf_op jit(solution)/shard_map/ppermute | solution.py:413
  89.6 1.5 %shard_map.99 = bf16[2,8,2,256,128]{4,3,2,1,0:T(8,128)(2,1)S(1)} custom-call(s32[5]{0:T(128)S(1)} %stack.50.spot, f32[2,8,256,128]{3,2,1,0:T(8,128)S(1)} %get-tuple-element.60.own, f32[2,8,256,128]{3,2,1,0:T(8,128)S(1)} %get-tuple-element.61.across, bf16[2,2,8,256,128]{4,3,2,1,0:T(8,128)(2,1)S(1)} %collective-permute-done.15.side, ...), custom_call_target="tpu_custom_call" | custom-call | flops 4000000 | bytes 1048576 | tf_op jit(solution)/shard_map/pallas_call | solution.py:231
  91.0 30.7 %all_to_all.10.received = bf16[16,2,256,128]{3,2,1,0:T(8,128)(2,1)S(1)} all-to-all(bf16[16,2,256,128]{3,2,1,0:T(8,128)(2,1)S(1)} %bitcast.48), channel_id=1, replica_groups=mesh['z'=4,'ylo'=2,'core'=2,'x'=4,'yhi'=2] {'ylo','x','yhi'}, dimensions={0} | all-to-all | bytes 4194304 | tf_op jit(solution)/shard_map/all_to_all | solution.py:416
  121.8 2.4 %shard_map.100 = (bf16[32,64,128]{2,1,0:T(8,128)(2,1)}, bf16[32,64,128]{2,1,0:T(8,128)(2,1)}, bf16[16,80,128]{2,1,0:T(8,128)(2,1)S(1)}) custom-call(s32[5]{0:T(128)S(1)} %stack.50.spot, s32[32]{0:T(128)S(1)} %copy-done.2, bf16[16,2,256,128]{3,2,1,0:T(8,128)(2,1)S(1)} %all_to_all.10.received, f32[32,32,128]{2,1,0:T(8,128)S(1)} %fusion.1.query, ...), custom_call_target="tpu_custom_call" | custom-call | flops 60000000 | bytes 4194304 | tf_op jit(solution)/shard_map/pallas_call | solution.py:319
  124.1 13.5 %all_to_all.11.parts = bf16[16,80,128]{2,1,0:T(8,128)(2,1)} all-to-all(bf16[16,80,128]{2,1,0:T(8,128)(2,1)S(1)} %get-tuple-element.66), channel_id=1, replica_groups=mesh['z'=4,'ylo'=2,'core'=2,'x'=4,'yhi'=2] {'z','ylo','core'}, dimensions={0} | all-to-all | bytes 655360 | tf_op jit(solution)/shard_map/all_to_all | solution.py:418
  137.6 2.0 %shard_map.101 = bf16[4,2,1024]{2,1,0:T(2,128)(2,1)} custom-call(bf16[16,80,128]{2,1,0:T(8,128)(2,1)} %all_to_all.11.parts), custom_call_target="tpu_custom_call" | custom-call | flops 300000 | bytes 1048576 | tf_op jit(solution)/shard_map/pallas_call | solution.py:355
  (65 shorter events, 14.5 us)
Async XLA Ops:
  0.6 13.3 %collective-permute-start = (bf16[2,512,128]{2,1,0:T(8,128)(2,1)}, bf16[2,512,128]{2,1,0:T(8,128)(2,1)S(1)}, u32[]{:S(2)}, u32[]{:S(2)}) collective-permute-start(bf16[2,512,128]{2,1,0:T(8,128)(2,1)} %param.9), channel_id=1, source_target_pairs={{1,0},{0,1},{3,2},{2,3},{5,4},{4,5},{7,6},{6,7},{9,8},{8,9},{11,10... | collective-permute-start | bytes 786440 | tf_op jit(solution)/shard_map/ppermute | solution.py:370
  4.5 2.2 %copy-start = (bf16[32,8,8192]{2,1,0:T(8,128)(2,1)S(1)}, bf16[32,8,8192]{2,1,0:T(8,128)(2,1)}, u32[]{:S(2)}) copy-start(bf16[32,8,8192]{2,1,0:T(8,128)(2,1)} %param.7) | copy-start | bytes 12582916
  7.5 6.4 %copy-start.6 = (bf16[2,512,128]{2,1,0:T(8,128)(2,1)S(1)}, bf16[2,512,128]{2,1,0:T(8,128)(2,1)}, u32[]{:S(2)}) copy-start(bf16[2,512,128]{2,1,0:T(8,128)(2,1)} %param.9) | copy-start | bytes 786436
  13.9 11.5 %copy-start.3 = (bf16[256,2048]{1,0:T(8,128)(2,1)}, bf16[256,2048]{1,0:T(8,128)(2,1)S(1)}, u32[]{:S(2)}) copy-start(bf16[256,2048]{1,0:T(8,128)(2,1)S(1)} %get-tuple-element.37) | copy-start | bytes 3145732
  14.2 7.6 %collective-permute-start.2 = (bf16[2,2,256,128]{3,2,1,0:T(8,128)(2,1)S(1)}, bf16[2,2,256,128]{3,2,1,0:T(8,128)(2,1)S(1)}, u32[]{:S(2)}, u32[]{:S(2)}) collective-permute-start(bf16[2,2,256,128]{3,2,1,0:T(8,128)(2,1)S(1)} %get-tuple-element.74), channel_id=1, source_target_pairs={{32,0},{33,1},{34,2},{35,3},{36,4},{37,5},{38,6},{39,7},{104,8},{1... | collective-permute-start | bytes 786440 | tf_op jit(solution)/shard_map/ppermute | solution.py:57
  18.0 6.4 %collective-permute-start.3 = (bf16[2,2,256,128]{3,2,1,0:T(8,128)(2,1)S(1)}, bf16[2,2,256,128]{3,2,1,0:T(8,128)(2,1)S(1)}, u32[]{:S(2)}, u32[]{:S(2)}) collective-permute-start(bf16[2,2,256,128]{3,2,1,0:T(8,128)(2,1)S(1)} %get-tuple-element.73), channel_id=1, source_target_pairs={{2,0},{3,1},{0,2},{1,3},{6,4},{7,5},{4,6},{5,7},{14,8},{15,9},{12,... | collective-permute-start | bytes 786440 | tf_op jit(solution)/shard_map/ppermute | solution.py:57
  20.5 14.9 %collective-permute-start.6 = (bf16[256,2048]{1,0:T(8,128)(2,1)}, bf16[256,2048]{1,0:T(8,128)(2,1)}, u32[]{:S(2)}, u32[]{:S(2)}) collective-permute-start(bf16[256,2048]{1,0:T(8,128)(2,1)} %get-tuple-element.41), channel_id=1, source_target_pairs={{8,0},{9,1},{10,2},{11,3},{12,4},{13,5},{14,6},{15,7},{0,8},{1,9},... | collective-permute-start | bytes 3145736 | tf_op jit(solution)/shard_map/ppermute | solution.py:377
  21.8 12.4 %copy-start.5 = (bf16[2,2,256,128]{3,2,1,0:T(8,128)(2,1)}, bf16[2,2,256,128]{3,2,1,0:T(8,128)(2,1)S(1)}, u32[]{:S(2)}) copy-start(bf16[2,2,256,128]{3,2,1,0:T(8,128)(2,1)S(1)} %collective-permute-done.2) | copy-start | bytes 786436
  24.5 8.5 %collective-permute-start.5 = (bf16[2,2,2,256,128]{4,3,2,1,0:T(8,128)(2,1)S(1)}, bf16[2,2,2,256,128]{4,3,2,1,0:T(8,128)(2,1)}, u32[]{:S(2)}, u32[]{:S(2)}) collective-permute-start(bf16[2,2,2,256,128]{4,3,2,1,0:T(8,128)(2,1)S(1)} %pad_maximum_fusion.4), channel_id=1, source_target_pairs={{6,0},{7,1},{4,2},{5,3},{2,4},{3,5},{0,6},{1,7},{10,8},{11,9},{8,1... | collective-permute-start | bytes 1572872 | tf_op jit(solution)/shard_map/ppermute | solution.py:57
  25.4 8.7 %collective-permute-start.4 = (bf16[2,2,2,256,128]{4,3,2,1,0:T(8,128)(2,1)}, bf16[2,2,2,256,128]{4,3,2,1,0:T(8,128)(2,1)}, u32[]{:S(2)}, u32[]{:S(2)}) collective-permute-start(bf16[2,2,2,256,128]{4,3,2,1,0:T(8,128)(2,1)} %pad_maximum_fusion.3), channel_id=1, source_target_pairs={{96,0},{97,1},{98,2},{99,3},{100,4},{101,5},{102,6},{103,7},{40,8}... | collective-permute-start | bytes 1572872 | tf_op jit(solution)/shard_map/ppermute | solution.py:57
  25.4 20.6 %collective-permute-start.11 = (bf16[256,2048]{1,0:T(8,128)(2,1)}, bf16[256,2048]{1,0:T(8,128)(2,1)}, u32[]{:S(2)}, u32[]{:S(2)}) collective-permute-start(bf16[256,2048]{1,0:T(8,128)(2,1)} %get-tuple-element.44), channel_id=1, source_target_pairs={{16,0},{17,1},{18,2},{19,3},{20,4},{21,5},{22,6},{23,7},{24,8},{25... | collective-permute-start | bytes 3145736 | tf_op jit(solution)/shard_map/ppermute | solution.py:375
  25.9 13.1 %copy-start.2 = (s32[32]{0:T(128)S(1)}, s32[32]{0:T(128)}, u32[]{:S(2)}) copy-start(s32[32]{0:T(128)} %lengths.1) | copy-start | bytes 388
  25.9 13.1 %copy-start.8 = (s32[32]{0:T(128)S(1)}, s32[32]{0:T(128)}, u32[]{:S(2)}) copy-start(s32[32]{0:T(128)} %param.13) | copy-start | bytes 388
  25.9 14.4 %copy-start.7 = (bf16[2,4,32,128]{3,2,1,0:T(8,128)(2,1)S(1)}, bf16[2,4,32,128]{3,2,1,0:T(8,128)(2,1)}, u32[]{:S(2)}) copy-start(bf16[2,4,32,128]{3,2,1,0:T(8,128)(2,1)} %param.11) | copy-start | bytes 196612
  35.4 18.5 %collective-permute-start.10 = (bf16[4,2,2,256,128]{4,3,2,1,0:T(8,128)(2,1)S(1)}, bf16[4,2,2,256,128]{4,3,2,1,0:T(8,128)(2,1)}, u32[]{:S(2)}, u32[]{:S(2)}) collective-permute-start(bf16[4,2,2,256,128]{4,3,2,1,0:T(8,128)(2,1)S(1)} %pad_maximum_fusion.1.refs_3_), channel_id=1, source_target_pairs={{96,0},{97,1},{98,2},{99,3},{100,4},{101,5},{102,6},{103,7},{40,8}... | collective-permute-start | bytes 3145736 | tf_op jit(solution)/shard_map/ppermute | solution.py:57
  35.5 22.4 %collective-permute-start.8 = (bf16[4,2,2,256,128]{4,3,2,1,0:T(8,128)(2,1)S(1)}, bf16[4,2,2,256,128]{4,3,2,1,0:T(8,128)(2,1)}, u32[]{:S(2)}, u32[]{:S(2)}) collective-permute-start(bf16[4,2,2,256,128]{4,3,2,1,0:T(8,128)(2,1)S(1)} %pad_maximum_fusion.1.refs_3_), channel_id=1, source_target_pairs={{32,0},{33,1},{34,2},{35,3},{36,4},{37,5},{38,6},{39,7},{104,8},{1... | collective-permute-start | bytes 3145736 | tf_op jit(solution)/shard_map/ppermute | solution.py:57
  36.7 20.6 %collective-permute-start.7 = (bf16[4,2,2,256,128]{4,3,2,1,0:T(8,128)(2,1)S(1)}, bf16[4,2,2,256,128]{4,3,2,1,0:T(8,128)(2,1)}, u32[]{:S(2)}, u32[]{:S(2)}) collective-permute-start(bf16[4,2,2,256,128]{4,3,2,1,0:T(8,128)(2,1)S(1)} %pad_maximum_fusion.refs_2_), channel_id=1, source_target_pairs={{2,0},{3,1},{0,2},{1,3},{6,4},{7,5},{4,6},{5,7},{14,8},{15,9},{12,... | collective-permute-start | bytes 3145736 | tf_op jit(solution)/shard_map/ppermute | solution.py:57
  38.5 21.4 %collective-permute-start.9 = (bf16[4,2,2,256,128]{4,3,2,1,0:T(8,128)(2,1)S(1)}, bf16[4,2,2,256,128]{4,3,2,1,0:T(8,128)(2,1)}, u32[]{:S(2)}, u32[]{:S(2)}) collective-permute-start(bf16[4,2,2,256,128]{4,3,2,1,0:T(8,128)(2,1)S(1)} %pad_maximum_fusion.refs_2_), channel_id=1, source_target_pairs={{6,0},{7,1},{4,2},{5,3},{2,4},{3,5},{0,6},{1,7},{10,8},{11,9},{8,1... | collective-permute-start | bytes 3145736 | tf_op jit(solution)/shard_map/ppermute | solution.py:57
  39.2 6.9 %copy-start.4 = (bf16[256,2048]{1,0:T(8,128)(2,1)S(1)}, bf16[256,2048]{1,0:T(8,128)(2,1)}, u32[]{:S(2)}) copy-start(bf16[256,2048]{1,0:T(8,128)(2,1)} %copy-done.3) | copy-start | bytes 3145732
  46.1 28.2 %collective-permute-start.1 = (bf16[256,2048]{1,0:T(8,128)(2,1)S(1)}, bf16[256,2048]{1,0:T(8,128)(2,1)S(1)}, u32[]{:S(2)}, u32[]{:S(2)}) collective-permute-start(bf16[256,2048]{1,0:T(8,128)(2,1)S(1)} %copy-done.4), channel_id=1, source_target_pairs={{16,0},{17,1},{18,2},{19,3},{20,4},{21,5},{22,6},{23,7},{24,8},{25... | collective-permute-start | bytes 3145736 | tf_op jit(solution)/shard_map/ppermute | solution.py:376
  59.9 14.3 %collective-permute-start.14 = (bf16[256,2048]{1,0:T(8,128)(2,1)}, bf16[256,2048]{1,0:T(8,128)(2,1)S(1)}, u32[]{:S(2)}, u32[]{:S(2)}) collective-permute-start(bf16[256,2048]{1,0:T(8,128)(2,1)} %collective-permute-done.11), channel_id=1, source_target_pairs={{8,0},{9,1},{10,2},{11,3},{12,4},{13,5},{14,6},{15,7},{0,8},{1,9},... | collective-permute-start | bytes 3145736 | tf_op jit(solution)/shard_map/ppermute | solution.py:391
  64.2 16.2 %collective-permute-start.12 = (bf16[4,2,2,256,128]{4,3,2,1,0:T(8,128)(2,1)}, bf16[4,2,2,256,128]{4,3,2,1,0:T(8,128)(2,1)S(1)}, u32[]{:S(2)}, u32[]{:S(2)}) collective-permute-start(bf16[4,2,2,256,128]{4,3,2,1,0:T(8,128)(2,1)} %collective-permute-done.7.refs_4_), channel_id=1, source_target_pairs={{6,0},{7,1},{4,2},{5,3},{2,4},{3,5},{0,6},{1,7},{10,8},{11,9},{8,1... | collective-permute-start | bytes 3145736 | tf_op jit(solution)/shard_map/ppermute | solution.py:57
  64.6 15.8 %collective-permute-start.13 = (bf16[4,2,2,256,128]{4,3,2,1,0:T(8,128)(2,1)}, bf16[4,2,2,256,128]{4,3,2,1,0:T(8,128)(2,1)S(1)}, u32[]{:S(2)}, u32[]{:S(2)}) collective-permute-start(bf16[4,2,2,256,128]{4,3,2,1,0:T(8,128)(2,1)} %collective-permute-done.8.refs_5_), channel_id=1, source_target_pairs={{96,0},{97,1},{98,2},{99,3},{100,4},{101,5},{102,6},{103,7},{40,8}... | collective-permute-start | bytes 3145736 | tf_op jit(solution)/shard_map/ppermute | solution.py:57
  83.4 6.2 %collective-permute-start.15 = (bf16[2,2,8,256,128]{4,3,2,1,0:T(8,128)(2,1)S(1)}, bf16[2,2,8,256,128]{4,3,2,1,0:T(8,128)(2,1)S(1)}, u32[]{:S(2)}, u32[]{:S(2)}) collective-permute-start(bf16[2,2,8,256,128]{4,3,2,1,0:T(8,128)(2,1)S(1)} %shard_map.98), channel_id=1, source_target_pairs={{8,0},{9,1},{10,2},{11,3},{12,4},{13,5},{14,6},{15,7},{0,8},{1,9},... | collective-permute-start | bytes 6291464 | tf_op jit(solution)/shard_map/ppermute | solution.py:413
  (1 other events, 0.8 us)

commit v3 on v2

--- a/solution.py
+++ b/solution.py
@@ -89,62 +89,60 @@
     return vectors * cosine + swapped * sine
 
 
-def prep_kernel(spot, hidden, gain, own, side, across, corner, total):
-    step = pl.program_id(1)
+def prep_kernel(spot, hidden, gain, own, side, across, corner, rows, total, sems):
     mine = 2 * (spot[1] & 1) + spot[3]
-    x = hidden[...].astype(jnp.float32)
-
-    @pl.when(pl.program_id(0) == 0)
-    def _():
-        squares = x * x
-        part = sum(squares[:, 128 * i : 128 * i + 128] for i in range(16))
-
-        @pl.when(step == 0)
+    copies = []
+    for i in range(4):
+        lanes = pl.ds(2048 * i, 2048)
+        copies.append(pltpu.make_async_copy(hidden.at[:, lanes], rows.at[:, lanes], sems.at[i]))
+        copies[i].start()
+    for i in range(4):
+        copies[i].wait()
+
+        def add(tile, _, i=i):
+            at = pl.ds(pl.multiple_of(16 * tile, 16), 16)
+            part = 0.0 if i == 0 else total[at, :]
+            for lane in range(2048 * i, 2048 * i + 2048, 128):
+                x = rows[at, lane : lane + 128].astype(jnp.float32)
+                part = part + x * x
+            total[at, :] = part
+            return 0
+
+        lax.fori_loop(0, 16, add, 0)
+    mean = jnp.sum(total[...], axis=1, keepdims=True) / 8192.0
+    total[...] = jnp.broadcast_to(lax.rsqrt(mean + 1e-05), (256, 128))
+    for owner in range(4):
+
+        @pl.when(mine == owner)
         def _():
-            total[...] = part
-
-        @pl.when(step > 0)
-        def _():
-            total[...] += part
-
-        @pl.when(step == 3)
-        def _():
-            mean = jnp.sum(total[...], axis=1, keepdims=True) / 8192.0
-            total[...] = jnp.broadcast_to(lax.rsqrt(mean + 1e-05), (256, 128))
-
-    @pl.when(pl.program_id(0) == 1)
-    def _():
-        normed = (x * total[:, :1] * gain[...]).astype(jnp.bfloat16)
-        quarters = [normed[:, 512 * i : 512 * i + 512] for i in range(4)]
-        for at in range(2):
-            lanes = pl.ds(pl.multiple_of(1024 * at + HALF * step, HALF), HALF)
-            blocks = [quarter[:, HALF * at : HALF * at + HALF] for quarter in quarters]
-            for owner in range(4):
-
-                @pl.when(mine == owner)
-                def _():
-                    own[:, lanes] = blocks[owner]
-                    side[:, lanes] = blocks[owner ^ 1]
-                    across[:, lanes] = blocks[owner ^ 2]
-                    corner[:, lanes] = blocks[owner ^ 3]
+            outs = (own, side, across, corner)
+
+            def write(tile, _):
+                at = pl.ds(pl.multiple_of(16 * tile, 16), 16)
+                scale = total[at, :]
+                for lane in range(0, 8192, 128):
+                    z, quarter, half, rest = lane // 2048, lane // 512 % 4, lane // HALF % 2, lane % HALF
+                    x = rows[at, lane : lane + 128].astype(jnp.float32)
+                    x = x * scale * gain[:, lane : lane + 128]
+                    to = 1024 * half + HALF * z + rest
+                    outs[quarter ^ owner][at, to : to + 128] = x.astype(jnp.bfloat16)
+                return 0
+
+            lax.fori_loop(0, 16, write, 0)
 
 
 def prep(spot, hidden, gain):
-    block = lambda turn, step, spot: (0, step)
-    whole = lambda turn, step, spot: (0, 0)
     return pl.pallas_call(
         prep_kernel,
-        out_shape=(
-            *[jax.ShapeDtypeStruct((256, 2048), jnp.bfloat16)] * 4,
-        ),
-        grid_spec=pltpu.PrefetchScalarGridSpec(
-            num_scalar_prefetch=1,
-            grid=(2, 4),
-            in_specs=[pl.BlockSpec((256, 2048), block), pl.BlockSpec((1, 2048), block)],
-            out_specs=[pl.BlockSpec((256, 2048), whole)] * 4,
-            scratch_shapes=[pltpu.VMEM((256, 128), jnp.float32)],
-        ),
-        compiler_params=pltpu.CompilerParams(vmem_limit_bytes=20 * MIB),
+        out_shape=[jax.ShapeDtypeStruct((256, 2048), jnp.bfloat16)] * 4,
+        in_specs=[SMEM, pl.BlockSpec(memory_space=pl.ANY), VMEM],
+        out_specs=[VMEM] * 4,
+        scratch_shapes=[
+            pltpu.VMEM((256, 8192), jnp.bfloat16),
+            pltpu.VMEM((256, 128), jnp.float32),
+            pltpu.SemaphoreType.DMA((4,)),
+        ],
+        compiler_params=pltpu.CompilerParams(vmem_limit_bytes=48 * MIB),
         cost_estimate=pl.CostEstimate(flops=1_000_000, bytes_accessed=MIB // 4, transcendentals=0),
     )(spot, hidden, gain)
 
@@ -155,7 +153,7 @@
     if carried:
         before, refs = refs[:inputs], refs[inputs:]
     if narrow:
-        out, sums = refs[0], refs[1:]
+        out = refs[0]
     else:
         sums = refs
     mine = [spot[0], spot[1], spot[2]]
@@ -165,35 +163,33 @@
     def slot_of(flip):
         return jnp.where(flip == 0, 0, jnp.where(flip == flips[1], 1, jnp.where(flip == flips[2], 2, 3)))
 
-    for i in range(inputs):
-        sums[i][...] = before[i][...] if carried else jnp.zeros_like(sums[i])
-
-    def add(x_at, depth, weight, heads):
-        for x_ref, total in zip(x_refs, sums):
-            left = x_ref[:, pl.ds(pl.multiple_of(x_at, HALF), depth)]
-            result = jnp.dot(left, weight, preferred_element_type=jnp.float32)
-            for i, (head, kind) in enumerate(heads):
-                total[kind, head] += result[:, 128 * i : 128 * i + 128]
-
     z_slots = [slot_of(z ^ mine[Z]) for z in range(4)]
     yhi = [mine[Y] >> 1, 1 - (mine[Y] >> 1)]
     places = [(ys, kind) for ys in range(2) for kind in range(2)]
-    for i, slot in enumerate(slots):
-        ref = piece_refs[2 * i]
-        x = mine[X] ^ flips[slot]
-        weight = jnp.concatenate(
-            [jnp.concatenate([ref[s, ys, kind] for ys, kind in places], 1) for s in z_slots], 0
-        )
-        add(0, 1024, weight, [(2 * x + yhi[ys], kind) for ys, kind in places])
-        ref = piece_refs[2 * i + 1]
-        z = mine[Z] ^ flips[slot]
-        for xs in range(4):
-            weight = jnp.concatenate([ref[xs, ys, kind] for ys, kind in places], 1)
-            x = mine[X] ^ flips[xs]
-            add(1024 + HALF * z, HALF, weight, [(2 * x + yhi[ys], kind) for ys, kind in places])
-    if narrow:
-        for i in range(inputs):
-            out[i] = sums[i][...].astype(out.dtype)
+    for xs in range(4):
+        lanes, weight = [], []
+        for i, slot in enumerate(slots):
+            ref = piece_refs[2 * i + 1]
+            z = mine[Z] ^ flips[slot]
+            lanes.append(pl.ds(pl.multiple_of(1024 + HALF * z, HALF), HALF))
+            weight.append(jnp.concatenate([ref[xs, ys, kind] for ys, kind in places], 1))
+            if slot == xs:
+                ref = piece_refs[2 * i]
+                lanes.append(pl.ds(0, 1024))
+                weight += [jnp.concatenate([ref[s, ys, kind] for ys, kind in places], 1) for s in z_slots]
+        weight = jnp.concatenate(weight, 0)
+        x = mine[X] ^ flips[xs]
+        left = jnp.concatenate([jnp.concatenate([rows[:, at] for rows in x_refs], 0) for at in lanes], 1)
+        result = jnp.dot(left, weight, preferred_element_type=jnp.float32)
+        for n in range(inputs):
+            for i, (ys, kind) in enumerate(places):
+                value = result[256 * n : 256 * n + 256, 128 * i : 128 * i + 128]
+                if carried:
+                    value = value + before[n][kind, 2 * x + yhi[ys]]
+                if narrow:
+                    out[n, kind, 2 * x + yhi[ys]] = value.astype(out.dtype)
+                else:
+                    sums[n][kind, 2 * x + yhi[ys]] = value
 
 
 def product(spot, rows, pieces, slots, before=None, narrow=False):
@@ -209,7 +205,6 @@
         out_shape=out_shape,
         in_specs=[SMEM] + [VMEM] * (count + len(pieces) + (count if carried else 0)),
         out_specs=[VMEM] * len(out_shape),
-        scratch_shapes=[pltpu.VMEM(shape, jnp.float32)] * (count if narrow else 0),
         compiler_params=pltpu.CompilerParams(vmem_limit_bytes=LIMIT * MIB),
         cost_estimate=pl.CostEstimate(flops=1_000_000, bytes_accessed=MIB // 4, transcendentals=0),
     )(spot, *rows, *pieces, *(before or ()))
@@ -382,14 +377,10 @@
     pairs = [jnp.stack(pair) for pair in zip(halves, firsts)]
     seconds = [swap(pair, dim, 1) for pair, dim in zip(pairs, middle)]
     blocks = [jnp.concatenate(both) for both in zip(pairs, seconds)]
-    blocks, side_rows, queries, new_kv, slab_start = together(blocks, side_rows, queries, new_kv, slab_start)
+    _, side_rows, queries, new_kv, slab_start = together(blocks[0], side_rows, queries, new_kv, slab_start)
 
     one = [swap(block, dim, 0) for block, dim in zip(blocks, last)]
     two = [swap(block, dim, 1) for block, dim in zip(blocks, last)]
-    one, two, corner_rows = together(one, two, corner_rows)
-    far = [swap(block, dim, 1) for block, dim in zip(one, last)]
-    corner_rows = lax.ppermute(corner_rows, AXES, flipped(core=1))
-
     freqs = rope_freqs()
     angles = ()
     for near in (seq, seq ^ 2):
@@ -403,12 +394,16 @@
     padding = ((0, 0), (0, 8 - STEPS), (0, 0))
     fresh_keys = jnp.pad(rotated(fresh[0], step_cos, step_sin), padding)
     fresh_values = jnp.pad(new_kv[1].transpose(1, 0, 2), padding)
-    spot_ready, *_ = together(spot, query, fresh_keys, fresh_values, angles)
-
-    near = [*blocks, *one, *two]
-    own, side = product(spot_ready, [own_rows, side_rows], near, (0, 1, 2))
-    spot_later, own, side = together(spot_ready, own, side)
-    corner, across = product(spot_later, [corner_rows, across_rows], near, (0, 1, 2))
+    own, side = product(spot, [own_rows, side_rows], blocks, (0,))
+    far = [swap(block, dim, 1) for block, dim in zip(one, last)]
+    one, two, corner_rows, own, side, query, fresh_keys, fresh_values, angles = together(
+        one, two, corner_rows, own, side, query, fresh_keys, fresh_values, angles
+    )
+    corner_rows = lax.ppermute(corner_rows, AXES, flipped(core=1))
+
+    own, side = product(spot, [own_rows, side_rows], [*one, *two], (1, 2), [own, side])
+    spot_later, own, side = together(spot, own, side)
+    corner, across = product(spot_later, [corner_rows, across_rows], [*blocks, *one, *two], (0, 1, 2))
     (sent,) = product(spot, [side_rows, corner_rows], far, (3,), [side, corner], narrow=True)
     side = lax.ppermute(sent, AXES, flipped(core=1))
     own, across = product(spot, [own_rows, across_rows], far, (3,), [own, across])

time: 140 us -> 137 us (0.979)
  waiting for transfers between devices: 31.1 us -> 28.2 us
  local copies, waits for them, and re-layouts: 4.76 us -> 3.3 us
    ppermute x1, waiting for transfers between devices: 4.87 us -> 0.05 us  [shards(): corner_rows = lax.ppermute(to_corner, AXES, flipped(y=1))]
    all_to_all x1, blocking collectives: 30.7 us -> 32.6 us  [shards(): received = lax.all_to_all(rows, ('ylo', 'x', 'yhi'), 0, 0)]
    ppermute x10, waiting for transfers between devices: 24.5 us -> 26.4 us  [swap(): return lax.ppermute(value, AXES, exchange(dim, step))]
    unnamed x19 -> x17, local copies, waits for them, and re-layouts: 3.97 us -> 2.52 us
    pallas_call x4 -> x5, Pallas kernels: 17.6 us -> 17.8 us  [product(): pl.pallas_call(functools.partial(product_kernel, slots, count, carried, n...]
where the time goes in v3:
time: 137 us
  blocking collectives  45.5 us (33%)
  Pallas kernels  29.6 us (22%)
  waiting for transfers between devices  28.2 us (21%)
  starting transfers between devices  23.6 us (17%)
  other arithmetic  5.82 us (4%)
  local copies, waits for them, and re-layouts  3.3 us (2%)
    all_to_all x1, blocking collectives, shards(): received = lax.all_to_all(rows, ('ylo', 'x', 'yhi'), 0, 0)  32.6 us
    ppermute x10, waiting for transfers between devices, swap(): return lax.ppermute(value, AXES, exchange(dim, step))  26.4 us
    pallas_call x5, Pallas kernels, product(): pl.pallas_call(functools.partial(product_kernel, slots, count, carried, n...  17.8 us
    all_to_all x1, blocking collectives, shards(): parts = lax.all_to_all(packed, SEQ, 0, 0)  12.9 us
    ppermute x10, starting transfers between devices, swap(): return lax.ppermute(value, AXES, exchange(dim, step))  11.1 us
    pallas_call x1, Pallas kernels, prep(): pl.pallas_call(prep_kernel, out_shape=[jax.ShapeDtypeStruct((256, 2048),...  5.94 us
    ppermute x1, starting transfers between devices, shards(): corner_rows = lax.ppermute(corner_rows, AXES, flipped(core=1))  4.28 us
    ppermute x1, starting transfers between devices, shards(): weight = jnp.stack([kv_weight, lax.ppermute(kv_weight, AXES, flipped(y=2))])  3.82 us
  transfers between devices with their start and end apart: 16, of which 9 were waited for; matrix products, arithmetic and copies ran while one was open for 5% of the time, Pallas kernels for 15%

profile of v3, /device:TPU:1, one launch (start us, length us, event | category | flops | bytes accessed | tf_op | source)
XLA Modules:
  0.0 137.0 jit_solution(1691844129371737362)
XLA Ops:
  0.6 3.8 %collective-permute-start = (bf16[2,512,128]{2,1,0:T(8,128)(2,1)}, bf16[2,512,128]{2,1,0:T(8,128)(2,1)S(1)}, u32[]{:S(2)}, u32[]{:S(2)}) collective-permute-start(bf16[2,512,128]{2,1,0:T(8,128)(2,1)} %param.9), channel_id=1, source_target_pairs={{1,0},{0,1},{3,2},{2,3},{5,4},{4,5},{7,6},{6,7},{9,8},{8,9},{11,10... | collective-permute-start | bytes 786440 | tf_op jit(solution)/shard_map/ppermute | solution.py:365
  5.3 5.9 %shard_map.94 = (bf16[256,2048]{1,0:T(8,128)(2,1)S(1)}, bf16[256,2048]{1,0:T(8,128)(2,1)}, bf16[256,2048]{1,0:T(8,128)(2,1)S(1)}, bf16[256,2048]{1,0:T(8,128)(2,1)}) custom-call(s32[5]{0:T(128)S(1)} %stack.50.spot, bf16[256,8192]{1,0:T(8,128)(2,1)} %bitcast.52, f32[1,8192]{1,0:T(1,128)S(1)} %bitcast.49), custom_call_target="tpu_custom_call" | custom-call | flops 1000000 | bytes 262144 | tf_op jit(solution)/shard_map/pallas_call | solution.py:135
  11.5 3.8 %collective-permute-start.2 = (bf16[2,2,256,128]{3,2,1,0:T(8,128)(2,1)S(1)}, bf16[2,2,256,128]{3,2,1,0:T(8,128)(2,1)S(1)}, u32[]{:S(2)}, u32[]{:S(2)}) collective-permute-start(bf16[2,2,256,128]{3,2,1,0:T(8,128)(2,1)S(1)} %get-tuple-element.90), channel_id=1, source_target_pairs={{32,0},{33,1},{34,2},{35,3},{36,4},{37,5},{38,6},{39,7},{104,8},{1... | collective-permute-start | bytes 786440 | tf_op jit(solution)/shard_map/ppermute | solution.py:57
  15.4 2.5 %collective-permute-start.3 = (bf16[2,2,256,128]{3,2,1,0:T(8,128)(2,1)S(1)}, bf16[2,2,256,128]{3,2,1,0:T(8,128)(2,1)S(1)}, u32[]{:S(2)}, u32[]{:S(2)}) collective-permute-start(bf16[2,2,256,128]{3,2,1,0:T(8,128)(2,1)S(1)} %get-tuple-element.89), channel_id=1, source_target_pairs={{2,0},{3,1},{0,2},{1,3},{6,4},{7,5},{4,6},{5,7},{14,8},{15,9},{12,... | collective-permute-start | bytes 786440 | tf_op jit(solution)/shard_map/ppermute | solution.py:57
  17.8 1.3 collective-permute-done.2
  19.1 2.7 %collective-permute-done.3 = bf16[2,2,256,128]{3,2,1,0:T(8,128)(2,1)S(1)} collective-permute-done((bf16[2,2,256,128]{3,2,1,0:T(8,128)(2,1)S(1)}, bf16[2,2,256,128]{3,2,1,0:T(8,128)(2,1)S(1)}, u32[]{:S(2)}, u32[]{:S(2)}) %collective-permute-start.3) | collective-permute-done | bytes 262176 | tf_op jit(solution)/shard_map/ppermute | solution.py:57
  23.6 6.8 %collective-permute-done.7 = bf16[2,2,2,256,128]{4,3,2,1,0:T(8,128)(2,1)} collective-permute-done((bf16[2,2,2,256,128]{4,3,2,1,0:T(8,128)(2,1)S(1)}, bf16[2,2,2,256,128]{4,3,2,1,0:T(8,128)(2,1)}, u32[]{:S(2)}, u32[]{:S(2)}) %collective-permute-start.7) | collective-permute-done | bytes 524320 | tf_op jit(solution)/shard_map/ppermute | solution.py:57
  34.2 2.4 %collective-permute-start.5 = (bf16[4,2,2,256,128]{4,3,2,1,0:T(8,128)(2,1)S(1)}, bf16[4,2,2,256,128]{4,3,2,1,0:T(8,128)(2,1)}, u32[]{:S(2)}, u32[]{:S(2)}) collective-permute-start(bf16[4,2,2,256,128]{4,3,2,1,0:T(8,128)(2,1)S(1)} %pad_maximum_fusion.refs_2_), channel_id=1, source_target_pairs={{2,0},{3,1},{0,2},{1,3},{6,4},{7,5},{4,6},{5,7},{14,8},{15,9},{12,... | collective-permute-start | bytes 3145736 | tf_op jit(solution)/shard_map/ppermute | solution.py:57
  40.1 2.6 %shard_map.95 = (f32[2,8,256,128]{3,2,1,0:T(8,128)S(1)}, f32[2,8,256,128]{3,2,1,0:T(8,128)S(1)}) custom-call(s32[5]{0:T(128)S(1)} %stack.50.spot, bf16[256,2048]{1,0:T(8,128)(2,1)S(1)} %get-tuple-element.44.refs_0_, bf16[256,2048]{1,0:T(8,128)(2,1)} %collective-permute-done.10.refs_1_.refs_0_, bf16[4,2,2,256,128]{4,3,2,1,0:T(8,128)(2,1)S(1)} %pad_maximum_fusion.refs_2_, ...), custom_call_target="tpu_custom_call" | custom-call | flops 1000000 | bytes 262144 | tf_op jit(solution)/shard_map/pallas_call | solution.py:203
  44.6 8.1 %collective-permute-done.12.refs_5_.refs_7_ = bf16[4,2,2,256,128]{4,3,2,1,0:T(8,128)(2,1)} collective-permute-done((bf16[4,2,2,256,128]{4,3,2,1,0:T(8,128)(2,1)S(1)}, bf16[4,2,2,256,128]{4,3,2,1,0:T(8,128)(2,1)}, u32[]{:S(2)}, u32[]{:S(2)}) %collective-permute-start.12) | collective-permute-done | bytes 1048608 | tf_op jit(solution)/shard_map/ppermute | solution.py:57
  52.7 3.9 %collective-permute-done.8.refs_3_.refs_5_ = bf16[4,2,2,256,128]{4,3,2,1,0:T(8,128)(2,1)} collective-permute-done((bf16[4,2,2,256,128]{4,3,2,1,0:T(8,128)(2,1)S(1)}, bf16[4,2,2,256,128]{4,3,2,1,0:T(8,128)(2,1)}, u32[]{:S(2)}, u32[]{:S(2)}) %collective-permute-start.8) | collective-permute-done | bytes 1048608 | tf_op jit(solution)/shard_map/ppermute | solution.py:57
  56.8 4.3 %collective-permute-start.14 = (bf16[256,2048]{1,0:T(8,128)(2,1)}, bf16[256,2048]{1,0:T(8,128)(2,1)S(1)}, u32[]{:S(2)}, u32[]{:S(2)}) collective-permute-start(bf16[256,2048]{1,0:T(8,128)(2,1)} %collective-permute-done.13), channel_id=1, source_target_pairs={{8,0},{9,1},{10,2},{11,3},{12,4},{13,5},{14,6},{15,7},{0,8},{1,9},... | collective-permute-start | bytes 3145736 | tf_op jit(solution)/shard_map/ppermute | solution.py:402
  62.0 5.0 %shard_map.96 = (f32[2,8,256,128]{3,2,1,0:T(8,128)S(1)}, f32[2,8,256,128]{3,2,1,0:T(8,128)S(1)}) custom-call(s32[5]{0:T(128)S(1)} %stack.50.spot, bf16[256,2048]{1,0:T(8,128)(2,1)S(1)} %get-tuple-element.44.refs_0_, bf16[256,2048]{1,0:T(8,128)(2,1)} %collective-permute-done.10.refs_1_.refs_0_, ...), custom_call_target="tpu_custom_call" | custom-call | flops 1000000 | bytes 262144 | tf_op jit(solution)/shard_map/pallas_call | solution.py:203
  67.0 5.7 %shard_map.97 = (f32[2,8,256,128]{3,2,1,0:T(8,128)S(1)}, f32[2,8,256,128]{3,2,1,0:T(8,128)S(1)}) custom-call(s32[5]{0:T(128)S(1)} %stack.50.spot, bf16[256,2048]{1,0:T(8,128)(2,1)S(1)} %collective-permute-done.14.refs_0_.refs_1_, bf16[256,2048]{1,0:T(8,128)(2,1)S(1)} %collective-permute-done.1.refs_1_, ...), custom_call_target="tpu_custom_call" | custom-call | flops 1000000 | bytes 262144 | tf_op jit(solution)/shard_map/pallas_call | solution.py:203
  72.7 2.6 %collective-permute-done.9.refs_3_ = bf16[4,2,2,256,128]{4,3,2,1,0:T(8,128)(2,1)S(1)} collective-permute-done((bf16[4,2,2,256,128]{4,3,2,1,0:T(8,128)(2,1)}, bf16[4,2,2,256,128]{4,3,2,1,0:T(8,128)(2,1)S(1)}, u32[]{:S(2)}, u32[]{:S(2)}) %collective-permute-start.9) | collective-permute-done | bytes 1048608 | tf_op jit(solution)/shard_map/ppermute | solution.py:57
  76.0 2.6 %shard_map.99 = bf16[2,2,8,256,128]{4,3,2,1,0:T(8,128)(2,1)S(1)} custom-call(s32[5]{0:T(128)S(1)} %stack.50.spot, bf16[256,2048]{1,0:T(8,128)(2,1)} %collective-permute-done.10.refs_1_.refs_0_, bf16[256,2048]{1,0:T(8,128)(2,1)S(1)} %collective-permute-done.14.refs_0_.refs_1_, bf16[4,2,2,256,128]{4,3,2,1,0:T(8,128)(2,1)S(1)} %collective-permute-done.6.refs_2_, ...), custom_call_target="tpu_custom_call" | custom-call | flops 1000000 | bytes 262144 | tf_op jit(solution)/shard_map/pallas_call | solution.py:203
  78.6 3.2 %collective-permute-start.15 = (bf16[2,2,8,256,128]{4,3,2,1,0:T(8,128)(2,1)S(1)}, bf16[2,2,8,256,128]{4,3,2,1,0:T(8,128)(2,1)S(1)}, u32[]{:S(2)}, u32[]{:S(2)}) collective-permute-start(bf16[2,2,8,256,128]{4,3,2,1,0:T(8,128)(2,1)S(1)} %shard_map.99), channel_id=1, source_target_pairs={{8,0},{9,1},{10,2},{11,3},{12,4},{13,5},{14,6},{15,7},{0,8},{1,9},... | collective-permute-start | bytes 6291464 | tf_op jit(solution)/shard_map/ppermute | solution.py:408
  81.8 2.0 %shard_map.98 = (f32[2,8,256,128]{3,2,1,0:T(8,128)S(1)}, f32[2,8,256,128]{3,2,1,0:T(8,128)S(1)}) custom-call(s32[5]{0:T(128)S(1)} %stack.50.spot, bf16[256,2048]{1,0:T(8,128)(2,1)S(1)} %get-tuple-element.44.refs_0_, bf16[256,2048]{1,0:T(8,128)(2,1)S(1)} %collective-permute-done.1.refs_1_, bf16[4,2,2,256,128]{4,3,2,1,0:T(8,128)(2,1)S(1)} %collective-permute-done.6.refs_2_, ...), custom_call_target="tpu_custom_call" | custom-call | flops 1000000 | bytes 262144 | tf_op jit(solution)/shard_map/pallas_call | solution.py:203
  83.9 1.8 %collective-permute-done.15.side = bf16[2,2,8,256,128]{4,3,2,1,0:T(8,128)(2,1)S(1)} collective-permute-done((bf16[2,2,8,256,128]{4,3,2,1,0:T(8,128)(2,1)S(1)}, bf16[2,2,8,256,128]{4,3,2,1,0:T(8,128)(2,1)S(1)}, u32[]{:S(2)}, u32[]{:S(2)}) %collective-permute-start.15) | collective-permute-done | bytes 2097184 | tf_op jit(solution)/shard_map/ppermute | solution.py:408
  85.6 1.5 %shard_map.100 = bf16[2,8,2,256,128]{4,3,2,1,0:T(8,128)(2,1)S(1)} custom-call(s32[5]{0:T(128)S(1)} %stack.50.spot, f32[2,8,256,128]{3,2,1,0:T(8,128)S(1)} %get-tuple-element.69.own, f32[2,8,256,128]{3,2,1,0:T(8,128)S(1)} %get-tuple-element.70.across, bf16[2,2,8,256,128]{4,3,2,1,0:T(8,128)(2,1)S(1)} %collective-permute-done.15.side, ...), custom_call_target="tpu_custom_call" | custom-call | flops 4000000 | bytes 1048576 | tf_op jit(solution)/shard_map/pallas_call | solution.py:226
  87.1 32.6 %all_to_all.10.received = bf16[16,2,256,128]{3,2,1,0:T(8,128)(2,1)S(1)} all-to-all(bf16[16,2,256,128]{3,2,1,0:T(8,128)(2,1)S(1)} %bitcast.48), channel_id=1, replica_groups=mesh['z'=4,'ylo'=2,'core'=2,'x'=4,'yhi'=2] {'ylo','x','yhi'}, dimensions={0} | all-to-all | bytes 4194304 | tf_op jit(solution)/shard_map/all_to_all | solution.py:411
  119.7 2.4 %shard_map.101 = (bf16[32,64,128]{2,1,0:T(8,128)(2,1)}, bf16[32,64,128]{2,1,0:T(8,128)(2,1)}, bf16[16,80,128]{2,1,0:T(8,128)(2,1)S(1)}) custom-call(s32[5]{0:T(128)S(1)} %stack.50.spot, s32[32]{0:T(128)S(1)} %copy-done.1, bf16[16,2,256,128]{3,2,1,0:T(8,128)(2,1)S(1)} %all_to_all.10.received, f32[32,32,128]{2,1,0:T(8,128)S(1)} %fusion.1.query, ...), custom_call_target="tpu_custom_call" | custom-call | flops 60000000 | bytes 4194304 | tf_op jit(solution)/shard_map/pallas_call | solution.py:314
  122.1 12.9 %all_to_all.11.parts = bf16[16,80,128]{2,1,0:T(8,128)(2,1)} all-to-all(bf16[16,80,128]{2,1,0:T(8,128)(2,1)S(1)} %get-tuple-element.82), channel_id=1, replica_groups=mesh['z'=4,'ylo'=2,'core'=2,'x'=4,'yhi'=2] {'z','ylo','core'}, dimensions={0} | all-to-all | bytes 655360 | tf_op jit(solution)/shard_map/all_to_all | solution.py:413
  135.0 2.0 %shard_map.102 = bf16[4,2,1024]{2,1,0:T(2,128)(2,1)} custom-call(bf16[16,80,128]{2,1,0:T(8,128)(2,1)} %all_to_all.11.parts), custom_call_target="tpu_custom_call" | custom-call | flops 300000 | bytes 1048576 | tf_op jit(solution)/shard_map/pallas_call | solution.py:350
  (64 shorter events, 13.7 us)
Async XLA Ops:
  0.6 10.6 %collective-permute-start = (bf16[2,512,128]{2,1,0:T(8,128)(2,1)}, bf16[2,512,128]{2,1,0:T(8,128)(2,1)S(1)}, u32[]{:S(2)}, u32[]{:S(2)}) collective-permute-start(bf16[2,512,128]{2,1,0:T(8,128)(2,1)} %param.9), channel_id=1, source_target_pairs={{1,0},{0,1},{3,2},{2,3},{5,4},{4,5},{7,6},{6,7},{9,8},{8,9},{11,10... | collective-permute-start | bytes 786440 | tf_op jit(solution)/shard_map/ppermute | solution.py:365
  4.5 0.8 copy-start
  5.3 6.0 %copy-start.5 = (bf16[2,512,128]{2,1,0:T(8,128)(2,1)S(1)}, bf16[2,512,128]{2,1,0:T(8,128)(2,1)}, u32[]{:S(2)}) copy-start(bf16[2,512,128]{2,1,0:T(8,128)(2,1)} %param.9) | copy-start | bytes 786436
  11.2 11.5 %copy-start.2 = (bf16[256,2048]{1,0:T(8,128)(2,1)}, bf16[256,2048]{1,0:T(8,128)(2,1)S(1)}, u32[]{:S(2)}) copy-start(bf16[256,2048]{1,0:T(8,128)(2,1)S(1)} %get-tuple-element.45) | copy-start | bytes 3145732
  11.5 7.6 %collective-permute-start.2 = (bf16[2,2,256,128]{3,2,1,0:T(8,128)(2,1)S(1)}, bf16[2,2,256,128]{3,2,1,0:T(8,128)(2,1)S(1)}, u32[]{:S(2)}, u32[]{:S(2)}) collective-permute-start(bf16[2,2,256,128]{3,2,1,0:T(8,128)(2,1)S(1)} %get-tuple-element.90), channel_id=1, source_target_pairs={{32,0},{33,1},{34,2},{35,3},{36,4},{37,5},{38,6},{39,7},{104,8},{1... | collective-permute-start | bytes 786440 | tf_op jit(solution)/shard_map/ppermute | solution.py:57
  15.4 6.4 %collective-permute-start.3 = (bf16[2,2,256,128]{3,2,1,0:T(8,128)(2,1)S(1)}, bf16[2,2,256,128]{3,2,1,0:T(8,128)(2,1)S(1)}, u32[]{:S(2)}, u32[]{:S(2)}) collective-permute-start(bf16[2,2,256,128]{3,2,1,0:T(8,128)(2,1)S(1)} %get-tuple-element.89), channel_id=1, source_target_pairs={{2,0},{3,1},{0,2},{1,3},{6,4},{7,5},{4,6},{5,7},{14,8},{15,9},{12,... | collective-permute-start | bytes 786440 | tf_op jit(solution)/shard_map/ppermute | solution.py:57
  17.8 16.4 %collective-permute-start.10 = (bf16[256,2048]{1,0:T(8,128)(2,1)}, bf16[256,2048]{1,0:T(8,128)(2,1)}, u32[]{:S(2)}, u32[]{:S(2)}) collective-permute-start(bf16[256,2048]{1,0:T(8,128)(2,1)} %get-tuple-element.49), channel_id=1, source_target_pairs={{8,0},{9,1},{10,2},{11,3},{12,4},{13,5},{14,6},{15,7},{0,8},{1,9},... | collective-permute-start | bytes 3145736 | tf_op jit(solution)/shard_map/ppermute | solution.py:372
  19.1 12.4 %copy-start.4 = (bf16[2,2,256,128]{3,2,1,0:T(8,128)(2,1)}, bf16[2,2,256,128]{3,2,1,0:T(8,128)(2,1)S(1)}, u32[]{:S(2)}) copy-start(bf16[2,2,256,128]{3,2,1,0:T(8,128)(2,1)S(1)} %collective-permute-done.2) | copy-start | bytes 786436
  21.9 8.5 %collective-permute-start.7 = (bf16[2,2,2,256,128]{4,3,2,1,0:T(8,128)(2,1)S(1)}, bf16[2,2,2,256,128]{4,3,2,1,0:T(8,128)(2,1)}, u32[]{:S(2)}, u32[]{:S(2)}) collective-permute-start(bf16[2,2,2,256,128]{4,3,2,1,0:T(8,128)(2,1)S(1)} %pad_maximum_fusion.4), channel_id=1, source_target_pairs={{6,0},{7,1},{4,2},{5,3},{2,4},{3,5},{0,6},{1,7},{10,8},{11,9},{8,1... | collective-permute-start | bytes 1572872 | tf_op jit(solution)/shard_map/ppermute | solution.py:57
  22.8 9.0 %collective-permute-start.4 = (bf16[2,2,2,256,128]{4,3,2,1,0:T(8,128)(2,1)}, bf16[2,2,2,256,128]{4,3,2,1,0:T(8,128)(2,1)}, u32[]{:S(2)}, u32[]{:S(2)}) collective-permute-start(bf16[2,2,2,256,128]{4,3,2,1,0:T(8,128)(2,1)} %pad_maximum_fusion.3), channel_id=1, source_target_pairs={{96,0},{97,1},{98,2},{99,3},{100,4},{101,5},{102,6},{103,7},{40,8}... | collective-permute-start | bytes 1572872 | tf_op jit(solution)/shard_map/ppermute | solution.py:57
  22.8 20.6 %collective-permute-start.13 = (bf16[256,2048]{1,0:T(8,128)(2,1)}, bf16[256,2048]{1,0:T(8,128)(2,1)}, u32[]{:S(2)}, u32[]{:S(2)}) collective-permute-start(bf16[256,2048]{1,0:T(8,128)(2,1)} %get-tuple-element.51), channel_id=1, source_target_pairs={{16,0},{17,1},{18,2},{19,3},{20,4},{21,5},{22,6},{23,7},{24,8},{25... | collective-permute-start | bytes 3145736 | tf_op jit(solution)/shard_map/ppermute | solution.py:370
  23.5 13.1 %copy-start.1 = (s32[32]{0:T(128)S(1)}, s32[32]{0:T(128)}, u32[]{:S(2)}) copy-start(s32[32]{0:T(128)} %lengths.1) | copy-start | bytes 388
  23.5 13.1 %copy-start.7 = (s32[32]{0:T(128)S(1)}, s32[32]{0:T(128)}, u32[]{:S(2)}) copy-start(s32[32]{0:T(128)} %param.13) | copy-start | bytes 388
  31.5 6.5 %copy-start.6 = (bf16[2,4,32,128]{3,2,1,0:T(8,128)(2,1)S(1)}, bf16[2,4,32,128]{3,2,1,0:T(8,128)(2,1)}, u32[]{:S(2)}) copy-start(bf16[2,4,32,128]{3,2,1,0:T(8,128)(2,1)} %param.11) | copy-start | bytes 196612
  31.5 21.2 %collective-permute-start.12 = (bf16[4,2,2,256,128]{4,3,2,1,0:T(8,128)(2,1)S(1)}, bf16[4,2,2,256,128]{4,3,2,1,0:T(8,128)(2,1)}, u32[]{:S(2)}, u32[]{:S(2)}) collective-permute-start(bf16[4,2,2,256,128]{4,3,2,1,0:T(8,128)(2,1)S(1)} %pad_maximum_fusion.1.refs_3_), channel_id=1, source_target_pairs={{96,0},{97,1},{98,2},{99,3},{100,4},{101,5},{102,6},{103,7},{40,8}... | collective-permute-start | bytes 3145736 | tf_op jit(solution)/shard_map/ppermute | solution.py:57
  31.6 25.0 %collective-permute-start.8 = (bf16[4,2,2,256,128]{4,3,2,1,0:T(8,128)(2,1)S(1)}, bf16[4,2,2,256,128]{4,3,2,1,0:T(8,128)(2,1)}, u32[]{:S(2)}, u32[]{:S(2)}) collective-permute-start(bf16[4,2,2,256,128]{4,3,2,1,0:T(8,128)(2,1)S(1)} %pad_maximum_fusion.1.refs_3_), channel_id=1, source_target_pairs={{32,0},{33,1},{34,2},{35,3},{36,4},{37,5},{38,6},{39,7},{104,8},{1... | collective-permute-start | bytes 3145736 | tf_op jit(solution)/shard_map/ppermute | solution.py:57
  33.1 23.6 %collective-permute-start.11 = (bf16[4,2,2,256,128]{4,3,2,1,0:T(8,128)(2,1)S(1)}, bf16[4,2,2,256,128]{4,3,2,1,0:T(8,128)(2,1)}, u32[]{:S(2)}, u32[]{:S(2)}) collective-permute-start(bf16[4,2,2,256,128]{4,3,2,1,0:T(8,128)(2,1)S(1)} %pad_maximum_fusion.refs_2_), channel_id=1, source_target_pairs={{6,0},{7,1},{4,2},{5,3},{2,4},{3,5},{0,6},{1,7},{10,8},{11,9},{8,1... | collective-permute-start | bytes 3145736 | tf_op jit(solution)/shard_map/ppermute | solution.py:57
  34.2 22.6 %collective-permute-start.5 = (bf16[4,2,2,256,128]{4,3,2,1,0:T(8,128)(2,1)S(1)}, bf16[4,2,2,256,128]{4,3,2,1,0:T(8,128)(2,1)}, u32[]{:S(2)}, u32[]{:S(2)}) collective-permute-start(bf16[4,2,2,256,128]{4,3,2,1,0:T(8,128)(2,1)S(1)} %pad_maximum_fusion.refs_2_), channel_id=1, source_target_pairs={{2,0},{3,1},{0,2},{1,3},{6,4},{7,5},{4,6},{5,7},{14,8},{15,9},{12,... | collective-permute-start | bytes 3145736 | tf_op jit(solution)/shard_map/ppermute | solution.py:57
  42.9 1.2 copy-start.3
  44.2 22.8 %collective-permute-start.1 = (bf16[256,2048]{1,0:T(8,128)(2,1)S(1)}, bf16[256,2048]{1,0:T(8,128)(2,1)S(1)}, u32[]{:S(2)}, u32[]{:S(2)}) collective-permute-start(bf16[256,2048]{1,0:T(8,128)(2,1)S(1)} %copy-done.3), channel_id=1, source_target_pairs={{16,0},{17,1},{18,2},{19,3},{20,4},{21,5},{22,6},{23,7},{24,8},{25... | collective-permute-start | bytes 3145736 | tf_op jit(solution)/shard_map/ppermute | solution.py:371
  56.8 10.2 %collective-permute-start.14 = (bf16[256,2048]{1,0:T(8,128)(2,1)}, bf16[256,2048]{1,0:T(8,128)(2,1)S(1)}, u32[]{:S(2)}, u32[]{:S(2)}) collective-permute-start(bf16[256,2048]{1,0:T(8,128)(2,1)} %collective-permute-done.13), channel_id=1, source_target_pairs={{8,0},{9,1},{10,2},{11,3},{12,4},{13,5},{14,6},{15,7},{0,8},{1,9},... | collective-permute-start | bytes 3145736 | tf_op jit(solution)/shard_map/ppermute | solution.py:402
  61.1 14.2 %collective-permute-start.9 = (bf16[4,2,2,256,128]{4,3,2,1,0:T(8,128)(2,1)}, bf16[4,2,2,256,128]{4,3,2,1,0:T(8,128)(2,1)S(1)}, u32[]{:S(2)}, u32[]{:S(2)}) collective-permute-start(bf16[4,2,2,256,128]{4,3,2,1,0:T(8,128)(2,1)} %collective-permute-done.8.refs_3_.refs_5_), channel_id=1, source_target_pairs={{96,0},{97,1},{98,2},{99,3},{100,4},{101,5},{102,6},{103,7},{40,8}... | collective-permute-start | bytes 3145736 | tf_op jit(solution)/shard_map/ppermute | solution.py:57
  61.9 14.2 %collective-permute-start.6 = (bf16[4,2,2,256,128]{4,3,2,1,0:T(8,128)(2,1)}, bf16[4,2,2,256,128]{4,3,2,1,0:T(8,128)(2,1)S(1)}, u32[]{:S(2)}, u32[]{:S(2)}) collective-permute-start(bf16[4,2,2,256,128]{4,3,2,1,0:T(8,128)(2,1)} %collective-permute-done.5.refs_2_.refs_4_), channel_id=1, source_target_pairs={{6,0},{7,1},{4,2},{5,3},{2,4},{3,5},{0,6},{1,7},{10,8},{11,9},{8,1... | collective-permute-start | bytes 3145736 | tf_op jit(solution)/shard_map/ppermute | solution.py:57
  78.6 7.0 %collective-permute-start.15 = (bf16[2,2,8,256,128]{4,3,2,1,0:T(8,128)(2,1)S(1)}, bf16[2,2,8,256,128]{4,3,2,1,0:T(8,128)(2,1)S(1)}, u32[]{:S(2)}, u32[]{:S(2)}) collective-permute-start(bf16[2,2,8,256,128]{4,3,2,1,0:T(8,128)(2,1)S(1)} %shard_map.99), channel_id=1, source_target_pairs={{8,0},{9,1},{10,2},{11,3},{12,4},{13,5},{14,6},{15,7},{0,8},{1,9},... | collective-permute-start | bytes 6291464 | tf_op jit(solution)/shard_map/ppermute | solution.py:408

commit v4 on v3

--- a/solution.py
+++ b/solution.py
@@ -20,7 +20,7 @@
 SEQ, HEAD = AXES[:3], AXES[3:]
 X, Y, Z = 0, 1, 2
 MIB = 1024 * 1024
-LIMIT = 8
+LIMIT = 12
 VMEM = pl.BlockSpec(memory_space=pltpu.VMEM)
 SMEM = pl.BlockSpec(memory_space=pltpu.SMEM)
 
@@ -396,12 +396,14 @@
     fresh_values = jnp.pad(new_kv[1].transpose(1, 0, 2), padding)
     own, side = product(spot, [own_rows, side_rows], blocks, (0,))
     far = [swap(block, dim, 1) for block, dim in zip(one, last)]
-    one, two, corner_rows, own, side, query, fresh_keys, fresh_values, angles = together(
-        one, two, corner_rows, own, side, query, fresh_keys, fresh_values, angles
+    one, corner_rows, own, side, query, fresh_keys, fresh_values, angles = together(
+        one, corner_rows, own, side, query, fresh_keys, fresh_values, angles
     )
     corner_rows = lax.ppermute(corner_rows, AXES, flipped(core=1))
 
-    own, side = product(spot, [own_rows, side_rows], [*one, *two], (1, 2), [own, side])
+    own, side = product(spot, [own_rows, side_rows], one, (1,), [own, side])
+    spot_two, own, side = together(spot, own, side)
+    own, side = product(spot_two, [own_rows, side_rows], two, (2,), [own, side])
     spot_later, own, side = together(spot, own, side)
     corner, across = product(spot_later, [corner_rows, across_rows], [*blocks, *one, *two], (0, 1, 2))
     (sent,) = product(spot, [side_rows, corner_rows], far, (3,), [side, corner], narrow=True)

time: 137 us -> 137 us (level)
  waiting for transfers between devices: 28.2 us -> 25.2 us
  starting transfers between devices: 23.6 us -> 26.4 us
  blocking collectives: 45.5 us -> 43.4 us
    ppermute x10, waiting for transfers between devices: 26.4 us -> 23.5 us  [swap(): return lax.ppermute(value, AXES, exchange(dim, step))]
    ppermute x1, starting transfers between devices: 4.28 us -> 6.7 us  [shards(): corner_rows = lax.ppermute(corner_rows, AXES, flipped(core=1))]
    all_to_all x1, blocking collectives: 32.6 us -> 30.4 us  [shards(): received = lax.all_to_all(rows, ('ylo', 'x', 'yhi'), 0, 0)]
    pallas_call x5 -> x6, Pallas kernels: 17.8 us -> 18.4 us  [product(): pl.pallas_call(functools.partial(product_kernel, slots, count, carried, n...]
  transfers between devices with their start and end apart: 16 -> 16, of which waited for: 9 -> 7; matrix products, arithmetic and copies ran while one was open for 5% -> 6% of each run, Pallas kernels for 15% -> 16%
where the time goes in v4:
time: 137 us; the launch traced here: 136 us
  blocking collectives  43.4 us (32%)
  Pallas kernels  30.2 us (22%)
  starting transfers between devices  26.4 us (19%)
  waiting for transfers between devices  25.2 us (18%)
  other arithmetic  6.87 us (5%)
  local copies, waits for them, and re-layouts  3.37 us (2%)
    all_to_all x1, blocking collectives, shards(): received = lax.all_to_all(rows, ('ylo', 'x', 'yhi'), 0, 0)  30.4 us
    ppermute x10, waiting for transfers between devices, swap(): return lax.ppermute(value, AXES, exchange(dim, step))  23.5 us
    pallas_call x6, Pallas kernels, product(): pl.pallas_call(functools.partial(product_kernel, slots, count, carried, n...  18.4 us
    all_to_all x1, blocking collectives, shards(): parts = lax.all_to_all(packed, SEQ, 0, 0)  12.9 us
    ppermute x10, starting transfers between devices, swap(): return lax.ppermute(value, AXES, exchange(dim, step))  10.9 us
    ppermute x1, starting transfers between devices, shards(): corner_rows = lax.ppermute(corner_rows, AXES, flipped(core=1))  6.7 us
    pallas_call x1, Pallas kernels, prep(): pl.pallas_call(prep_kernel, out_shape=[jax.ShapeDtypeStruct((256, 2048),...  5.89 us
    ppermute x1, starting transfers between devices, shards(): weight = jnp.stack([kv_weight, lax.ppermute(kv_weight, AXES, flipped(y=2))])  3.82 us
  transfers between devices with their start and end apart: 16, of which 7 were waited for; matrix products, arithmetic and copies ran while one was open for 6% of the time, Pallas kernels for 16%

profile of v4, /device:TPU:1, one launch (start us, length us, event | category | flops | bytes accessed | tf_op | source)
XLA Modules:
  0.0 136.4 jit_solution(14005799757166650572)
XLA Ops:
  0.6 3.8 %collective-permute-start = (bf16[2,512,128]{2,1,0:T(8,128)(2,1)}, bf16[2,512,128]{2,1,0:T(8,128)(2,1)S(1)}, u32[]{:S(2)}, u32[]{:S(2)}) collective-permute-start(bf16[2,512,128]{2,1,0:T(8,128)(2,1)} %param.9), channel_id=1, source_target_pairs={{1,0},{0,1},{3,2},{2,3},{5,4},{4,5},{7,6},{6,7},{9,8},{8,9},{11,10... | collective-permute-start | bytes 786440 | tf_op jit(solution)/shard_map/ppermute | solution.py:365
  5.3 5.9 %shard_map.94 = (bf16[256,2048]{1,0:T(8,128)(2,1)S(1)}, bf16[256,2048]{1,0:T(8,128)(2,1)}, bf16[256,2048]{1,0:T(8,128)(2,1)S(1)}, bf16[256,2048]{1,0:T(8,128)(2,1)}) custom-call(s32[5]{0:T(128)S(1)} %stack.50.spot, bf16[256,8192]{1,0:T(8,128)(2,1)} %bitcast.52, f32[1,8192]{1,0:T(1,128)S(1)} %bitcast.49), custom_call_target="tpu_custom_call" | custom-call | flops 1000000 | bytes 262144 | tf_op jit(solution)/shard_map/pallas_call | solution.py:135
  11.5 3.8 %collective-permute-start.2 = (bf16[2,2,256,128]{3,2,1,0:T(8,128)(2,1)S(1)}, bf16[2,2,256,128]{3,2,1,0:T(8,128)(2,1)S(1)}, u32[]{:S(2)}, u32[]{:S(2)}) collective-permute-start(bf16[2,2,256,128]{3,2,1,0:T(8,128)(2,1)S(1)} %get-tuple-element.96), channel_id=1, source_target_pairs={{32,0},{33,1},{34,2},{35,3},{36,4},{37,5},{38,6},{39,7},{104,8},{1... | collective-permute-start | bytes 786440 | tf_op jit(solution)/shard_map/ppermute | solution.py:57
  15.3 2.5 %collective-permute-start.3 = (bf16[2,2,256,128]{3,2,1,0:T(8,128)(2,1)S(1)}, bf16[2,2,256,128]{3,2,1,0:T(8,128)(2,1)S(1)}, u32[]{:S(2)}, u32[]{:S(2)}) collective-permute-start(bf16[2,2,256,128]{3,2,1,0:T(8,128)(2,1)S(1)} %get-tuple-element.95), channel_id=1, source_target_pairs={{2,0},{3,1},{0,2},{1,3},{6,4},{7,5},{4,6},{5,7},{14,8},{15,9},{12,... | collective-permute-start | bytes 786440 | tf_op jit(solution)/shard_map/ppermute | solution.py:57
  19.1 2.7 %collective-permute-done.3 = bf16[2,2,256,128]{3,2,1,0:T(8,128)(2,1)S(1)} collective-permute-done((bf16[2,2,256,128]{3,2,1,0:T(8,128)(2,1)S(1)}, bf16[2,2,256,128]{3,2,1,0:T(8,128)(2,1)S(1)}, u32[]{:S(2)}, u32[]{:S(2)}) %collective-permute-start.3) | collective-permute-done | bytes 262176 | tf_op jit(solution)/shard_map/ppermute | solution.py:57
  23.7 6.7 %collective-permute-done.7 = bf16[2,2,2,256,128]{4,3,2,1,0:T(8,128)(2,1)} collective-permute-done((bf16[2,2,2,256,128]{4,3,2,1,0:T(8,128)(2,1)S(1)}, bf16[2,2,2,256,128]{4,3,2,1,0:T(8,128)(2,1)}, u32[]{:S(2)}, u32[]{:S(2)}) %collective-permute-start.7) | collective-permute-done | bytes 524320 | tf_op jit(solution)/shard_map/ppermute | solution.py:57
  31.9 2.1 %pad_maximum_fusion.refs_2_ = bf16[4,2,2,256,128]{4,3,2,1,0:T(8,128)(2,1)} fusion(bf16[2,2,2,256,128]{4,3,2,1,0:T(8,128)(2,1)} %collective-permute-done.4, bf16[1,2,2,256,128]{4,3,2,1,0:T(8,128)(2,1)S(1)} %bitcast.54, bf16[1,2,2,256,128]{4,3,2,1,0:T(8,128)(2,1)S(1)} %get-tuple-element.94), kind=kLoop, calls=%fused_computation | loop fusion | flops 1048576 | bytes 2097152 | tf_op jit(solution)/shard_map/concatenate | solution.py:379
  34.0 2.5 %collective-permute-start.5 = (bf16[4,2,2,256,128]{4,3,2,1,0:T(8,128)(2,1)}, bf16[4,2,2,256,128]{4,3,2,1,0:T(8,128)(2,1)}, u32[]{:S(2)}, u32[]{:S(2)}) collective-permute-start(bf16[4,2,2,256,128]{4,3,2,1,0:T(8,128)(2,1)} %pad_maximum_fusion.refs_2_), channel_id=1, source_target_pairs={{2,0},{3,1},{0,2},{1,3},{6,4},{7,5},{4,6},{5,7},{14,8},{15,9},{12,... | collective-permute-start | bytes 3145736 | tf_op jit(solution)/shard_map/ppermute | solution.py:57
  40.3 2.6 %shard_map.95 = (f32[2,8,256,128]{3,2,1,0:T(8,128)S(1)}, f32[2,8,256,128]{3,2,1,0:T(8,128)S(1)}) custom-call(s32[5]{0:T(128)S(1)} %stack.50.spot, bf16[256,2048]{1,0:T(8,128)(2,1)S(1)} %get-tuple-element.47.refs_0_, bf16[256,2048]{1,0:T(8,128)(2,1)S(1)} %collective-permute-done.10.refs_1_.refs_0_, bf16[4,2,2,256,128]{4,3,2,1,0:T(8,128)(2,1)} %pad_maximum_fusion.refs_2_, ...), custom_call_target="tpu_custom_call" | custom-call | flops 1000000 | bytes 262144 | tf_op jit(solution)/shard_map/pallas_call | solution.py:203
  44.9 10.8 %collective-permute-done.8.refs_3_.refs_5_ = bf16[4,2,2,256,128]{4,3,2,1,0:T(8,128)(2,1)} collective-permute-done((bf16[4,2,2,256,128]{4,3,2,1,0:T(8,128)(2,1)S(1)}, bf16[4,2,2,256,128]{4,3,2,1,0:T(8,128)(2,1)}, u32[]{:S(2)}, u32[]{:S(2)}) %collective-permute-start.8) | collective-permute-done | bytes 1048608 | tf_op jit(solution)/shard_map/ppermute | solution.py:57
  55.7 6.7 %collective-permute-start.14 = (bf16[256,2048]{1,0:T(8,128)(2,1)}, bf16[256,2048]{1,0:T(8,128)(2,1)S(1)}, u32[]{:S(2)}, u32[]{:S(2)}) collective-permute-start(bf16[256,2048]{1,0:T(8,128)(2,1)} %collective-permute-done.11), channel_id=1, source_target_pairs={{8,0},{9,1},{10,2},{11,3},{12,4},{13,5},{14,6},{15,7},{0,8},{1,9},... | collective-permute-start | bytes 3145736 | tf_op jit(solution)/shard_map/ppermute | solution.py:402
  63.8 3.0 %shard_map.96 = (f32[2,8,256,128]{3,2,1,0:T(8,128)S(1)}, f32[2,8,256,128]{3,2,1,0:T(8,128)S(1)}) custom-call(s32[5]{0:T(128)S(1)} %stack.50.spot, bf16[256,2048]{1,0:T(8,128)(2,1)S(1)} %get-tuple-element.47.refs_0_, bf16[256,2048]{1,0:T(8,128)(2,1)S(1)} %collective-permute-done.10.refs_1_.refs_0_, ...), custom_call_target="tpu_custom_call" | custom-call | flops 1000000 | bytes 262144 | tf_op jit(solution)/shard_map/pallas_call | solution.py:203
  66.8 3.0 %shard_map.97 = (f32[2,8,256,128]{3,2,1,0:T(8,128)S(1)}, f32[2,8,256,128]{3,2,1,0:T(8,128)S(1)}) custom-call(s32[5]{0:T(128)S(1)} %stack.50.spot, bf16[256,2048]{1,0:T(8,128)(2,1)S(1)} %get-tuple-element.47.refs_0_, bf16[256,2048]{1,0:T(8,128)(2,1)S(1)} %collective-permute-done.10.refs_1_.refs_0_, ...), custom_call_target="tpu_custom_call" | custom-call | flops 1000000 | bytes 262144 | tf_op jit(solution)/shard_map/pallas_call | solution.py:203
  69.9 6.0 %shard_map.98 = (f32[2,8,256,128]{3,2,1,0:T(8,128)S(1)}, f32[2,8,256,128]{3,2,1,0:T(8,128)S(1)}) custom-call(s32[5]{0:T(128)S(1)} %stack.50.spot, bf16[256,2048]{1,0:T(8,128)(2,1)S(1)} %collective-permute-done.14.refs_0_.refs_1_, bf16[256,2048]{1,0:T(8,128)(2,1)S(1)} %collective-permute-done.1.refs_1_, bf16[4,2,2,256,128]{4,3,2,1,0:T(8,128)(2,1)} %pad_maximum_fusion.refs_2_, ...), custom_call_target="tpu_custom_call" | custom-call | flops 1000000 | bytes 262144 | tf_op jit(solution)/shard_map/pallas_call | solution.py:203
  76.5 1.4 %collective-permute-done.6.refs_2_ = bf16[4,2,2,256,128]{4,3,2,1,0:T(8,128)(2,1)S(1)} collective-permute-done((bf16[4,2,2,256,128]{4,3,2,1,0:T(8,128)(2,1)}, bf16[4,2,2,256,128]{4,3,2,1,0:T(8,128)(2,1)S(1)}, u32[]{:S(2)}, u32[]{:S(2)}) %collective-permute-start.6) | collective-permute-done | bytes 1048608 | tf_op jit(solution)/shard_map/ppermute | solution.py:57
  78.0 1.9 %shard_map.100 = bf16[2,2,8,256,128]{4,3,2,1,0:T(8,128)(2,1)S(1)} custom-call(s32[5]{0:T(128)S(1)} %stack.50.spot, bf16[256,2048]{1,0:T(8,128)(2,1)S(1)} %collective-permute-done.10.refs_1_.refs_0_, bf16[256,2048]{1,0:T(8,128)(2,1)S(1)} %collective-permute-done.14.refs_0_.refs_1_, bf16[4,2,2,256,128]{4,3,2,1,0:T(8,128)(2,1)S(1)} %collective-permute-done.6.refs_2_, ...), custom_call_target="tpu_custom_call" | custom-call | flops 1000000 | bytes 262144 | tf_op jit(solution)/shard_map/pallas_call | solution.py:203
  79.8 3.6 %collective-permute-start.15 = (bf16[2,2,8,256,128]{4,3,2,1,0:T(8,128)(2,1)S(1)}, bf16[2,2,8,256,128]{4,3,2,1,0:T(8,128)(2,1)S(1)}, u32[]{:S(2)}, u32[]{:S(2)}) collective-permute-start(bf16[2,2,8,256,128]{4,3,2,1,0:T(8,128)(2,1)S(1)} %shard_map.100), channel_id=1, source_target_pairs={{8,0},{9,1},{10,2},{11,3},{12,4},{13,5},{14,6},{15,7},{0,8},{1,9},... | collective-permute-start | bytes 6291464 | tf_op jit(solution)/shard_map/ppermute | solution.py:410
  83.4 2.0 %shard_map.99 = (f32[2,8,256,128]{3,2,1,0:T(8,128)S(1)}, f32[2,8,256,128]{3,2,1,0:T(8,128)S(1)}) custom-call(s32[5]{0:T(128)S(1)} %stack.50.spot, bf16[256,2048]{1,0:T(8,128)(2,1)S(1)} %get-tuple-element.47.refs_0_, bf16[256,2048]{1,0:T(8,128)(2,1)S(1)} %collective-permute-done.1.refs_1_, bf16[4,2,2,256,128]{4,3,2,1,0:T(8,128)(2,1)S(1)} %collective-permute-done.6.refs_2_, ...), custom_call_target="tpu_custom_call" | custom-call | flops 1000000 | bytes 262144 | tf_op jit(solution)/shard_map/pallas_call | solution.py:203
  85.4 1.8 %collective-permute-done.15.side = bf16[2,2,8,256,128]{4,3,2,1,0:T(8,128)(2,1)S(1)} collective-permute-done((bf16[2,2,8,256,128]{4,3,2,1,0:T(8,128)(2,1)S(1)}, bf16[2,2,8,256,128]{4,3,2,1,0:T(8,128)(2,1)S(1)}, u32[]{:S(2)}, u32[]{:S(2)}) %collective-permute-start.15) | collective-permute-done | bytes 2097184 | tf_op jit(solution)/shard_map/ppermute | solution.py:410
  87.2 1.5 %shard_map.101 = bf16[2,8,2,256,128]{4,3,2,1,0:T(8,128)(2,1)S(1)} custom-call(s32[5]{0:T(128)S(1)} %stack.50.spot, f32[2,8,256,128]{3,2,1,0:T(8,128)S(1)} %get-tuple-element.75.own, f32[2,8,256,128]{3,2,1,0:T(8,128)S(1)} %get-tuple-element.76.across, bf16[2,2,8,256,128]{4,3,2,1,0:T(8,128)(2,1)S(1)} %collective-permute-done.15.side, ...), custom_call_target="tpu_custom_call" | custom-call | flops 4000000 | bytes 1048576 | tf_op jit(solution)/shard_map/pallas_call | solution.py:226
  88.6 30.4 %all_to_all.10.received = bf16[16,2,256,128]{3,2,1,0:T(8,128)(2,1)S(1)} all-to-all(bf16[16,2,256,128]{3,2,1,0:T(8,128)(2,1)S(1)} %bitcast.48), channel_id=1, replica_groups=mesh['z'=4,'ylo'=2,'core'=2,'x'=4,'yhi'=2] {'ylo','x','yhi'}, dimensions={0} | all-to-all | bytes 4194304 | tf_op jit(solution)/shard_map/all_to_all | solution.py:413
  119.1 2.4 %shard_map.102 = (bf16[32,64,128]{2,1,0:T(8,128)(2,1)}, bf16[32,64,128]{2,1,0:T(8,128)(2,1)}, bf16[16,80,128]{2,1,0:T(8,128)(2,1)S(1)}) custom-call(s32[5]{0:T(128)S(1)} %stack.50.spot, s32[32]{0:T(128)S(1)} %copy-done.1, bf16[16,2,256,128]{3,2,1,0:T(8,128)(2,1)S(1)} %all_to_all.10.received, f32[32,32,128]{2,1,0:T(8,128)S(1)} %fusion.1.query, ...), custom_call_target="tpu_custom_call" | custom-call | flops 60000000 | bytes 4194304 | tf_op jit(solution)/shard_map/pallas_call | solution.py:314
  121.4 12.9 %all_to_all.11.parts = bf16[16,80,128]{2,1,0:T(8,128)(2,1)} all-to-all(bf16[16,80,128]{2,1,0:T(8,128)(2,1)S(1)} %get-tuple-element.88), channel_id=1, replica_groups=mesh['z'=4,'ylo'=2,'core'=2,'x'=4,'yhi'=2] {'z','ylo','core'}, dimensions={0} | all-to-all | bytes 655360 | tf_op jit(solution)/shard_map/all_to_all | solution.py:415
  134.4 2.0 %shard_map.103 = bf16[4,2,1024]{2,1,0:T(2,128)(2,1)} custom-call(bf16[16,80,128]{2,1,0:T(8,128)(2,1)} %all_to_all.11.parts), custom_call_target="tpu_custom_call" | custom-call | flops 300000 | bytes 1048576 | tf_op jit(solution)/shard_map/pallas_call | solution.py:350
  (71 shorter events, 13.5 us)
Async XLA Ops:
  0.6 10.6 %collective-permute-start = (bf16[2,512,128]{2,1,0:T(8,128)(2,1)}, bf16[2,512,128]{2,1,0:T(8,128)(2,1)S(1)}, u32[]{:S(2)}, u32[]{:S(2)}) collective-permute-start(bf16[2,512,128]{2,1,0:T(8,128)(2,1)} %param.9), channel_id=1, source_target_pairs={{1,0},{0,1},{3,2},{2,3},{5,4},{4,5},{7,6},{6,7},{9,8},{8,9},{11,10... | collective-permute-start | bytes 786440 | tf_op jit(solution)/shard_map/ppermute | solution.py:365
  5.3 5.9 %copy-start.8 = (bf16[2,512,128]{2,1,0:T(8,128)(2,1)S(1)}, bf16[2,512,128]{2,1,0:T(8,128)(2,1)}, u32[]{:S(2)}) copy-start(bf16[2,512,128]{2,1,0:T(8,128)(2,1)} %param.9) | copy-start | bytes 786436
  11.2 11.6 %copy-start.2 = (bf16[256,2048]{1,0:T(8,128)(2,1)}, bf16[256,2048]{1,0:T(8,128)(2,1)S(1)}, u32[]{:S(2)}) copy-start(bf16[256,2048]{1,0:T(8,128)(2,1)S(1)} %get-tuple-element.48) | copy-start | bytes 3145732
  11.5 11.3 %copy-start.4 = (bf16[1,2,2,256,128]{4,3,2,1,0:T(8,128)(2,1)}, bf16[1,2,2,256,128]{4,3,2,1,0:T(8,128)(2,1)S(1)}, u32[]{:S(2)}) copy-start(bf16[1,2,2,256,128]{4,3,2,1,0:T(8,128)(2,1)S(1)} %get-tuple-element.93) | copy-start | bytes 786436
  11.5 7.6 %collective-permute-start.2 = (bf16[2,2,256,128]{3,2,1,0:T(8,128)(2,1)S(1)}, bf16[2,2,256,128]{3,2,1,0:T(8,128)(2,1)S(1)}, u32[]{:S(2)}, u32[]{:S(2)}) collective-permute-start(bf16[2,2,256,128]{3,2,1,0:T(8,128)(2,1)S(1)} %get-tuple-element.96), channel_id=1, source_target_pairs={{32,0},{33,1},{34,2},{35,3},{36,4},{37,5},{38,6},{39,7},{104,8},{1... | collective-permute-start | bytes 786440 | tf_op jit(solution)/shard_map/ppermute | solution.py:57
  15.3 6.4 %collective-permute-start.3 = (bf16[2,2,256,128]{3,2,1,0:T(8,128)(2,1)S(1)}, bf16[2,2,256,128]{3,2,1,0:T(8,128)(2,1)S(1)}, u32[]{:S(2)}, u32[]{:S(2)}) collective-permute-start(bf16[2,2,256,128]{3,2,1,0:T(8,128)(2,1)S(1)} %get-tuple-element.95), channel_id=1, source_target_pairs={{2,0},{3,1},{0,2},{1,3},{6,4},{7,5},{4,6},{5,7},{14,8},{15,9},{12,... | collective-permute-start | bytes 786440 | tf_op jit(solution)/shard_map/ppermute | solution.py:57
  17.8 18.6 %collective-permute-start.10 = (bf16[256,2048]{1,0:T(8,128)(2,1)}, bf16[256,2048]{1,0:T(8,128)(2,1)S(1)}, u32[]{:S(2)}, u32[]{:S(2)}) collective-permute-start(bf16[256,2048]{1,0:T(8,128)(2,1)} %get-tuple-element.52), channel_id=1, source_target_pairs={{8,0},{9,1},{10,2},{11,3},{12,4},{13,5},{14,6},{15,7},{0,8},{1,9},... | collective-permute-start | bytes 3145736 | tf_op jit(solution)/shard_map/ppermute | solution.py:372
  19.1 3.7 %copy-start.5 = (bf16[2,2,256,128]{3,2,1,0:T(8,128)(2,1)}, bf16[2,2,256,128]{3,2,1,0:T(8,128)(2,1)S(1)}, u32[]{:S(2)}) copy-start(bf16[2,2,256,128]{3,2,1,0:T(8,128)(2,1)S(1)} %collective-permute-done.2) | copy-start | bytes 786436
  21.8 8.5 %collective-permute-start.7 = (bf16[2,2,2,256,128]{4,3,2,1,0:T(8,128)(2,1)S(1)}, bf16[2,2,2,256,128]{4,3,2,1,0:T(8,128)(2,1)}, u32[]{:S(2)}, u32[]{:S(2)}) collective-permute-start(bf16[2,2,2,256,128]{4,3,2,1,0:T(8,128)(2,1)S(1)} %pad_maximum_fusion.4), channel_id=1, source_target_pairs={{6,0},{7,1},{4,2},{5,3},{2,4},{3,5},{0,6},{1,7},{10,8},{11,9},{8,1... | collective-permute-start | bytes 1572872 | tf_op jit(solution)/shard_map/ppermute | solution.py:57
  22.8 9.1 %collective-permute-start.4 = (bf16[2,2,2,256,128]{4,3,2,1,0:T(8,128)(2,1)}, bf16[2,2,2,256,128]{4,3,2,1,0:T(8,128)(2,1)}, u32[]{:S(2)}, u32[]{:S(2)}) collective-permute-start(bf16[2,2,2,256,128]{4,3,2,1,0:T(8,128)(2,1)} %pad_maximum_fusion.3), channel_id=1, source_target_pairs={{96,0},{97,1},{98,2},{99,3},{100,4},{101,5},{102,6},{103,7},{40,8}... | collective-permute-start | bytes 1572872 | tf_op jit(solution)/shard_map/ppermute | solution.py:57
  22.8 20.8 %collective-permute-start.11 = (bf16[256,2048]{1,0:T(8,128)(2,1)}, bf16[256,2048]{1,0:T(8,128)(2,1)}, u32[]{:S(2)}, u32[]{:S(2)}) collective-permute-start(bf16[256,2048]{1,0:T(8,128)(2,1)} %get-tuple-element.54), channel_id=1, source_target_pairs={{16,0},{17,1},{18,2},{19,3},{20,4},{21,5},{22,6},{23,7},{24,8},{25... | collective-permute-start | bytes 3145736 | tf_op jit(solution)/shard_map/ppermute | solution.py:370
  23.6 8.2 %copy-start.6 = (bf16[2,2,256,128]{3,2,1,0:T(8,128)(2,1)S(1)}, bf16[2,2,256,128]{3,2,1,0:T(8,128)(2,1)}, u32[]{:S(2)}) copy-start(bf16[2,2,256,128]{3,2,1,0:T(8,128)(2,1)} %copy-done.5) | copy-start | bytes 786436
  23.7 13.2 %copy-start.1 = (s32[32]{0:T(128)S(1)}, s32[32]{0:T(128)}, u32[]{:S(2)}) copy-start(s32[32]{0:T(128)} %lengths.1) | copy-start | bytes 388
  23.7 13.2 %copy-start.10 = (s32[32]{0:T(128)S(1)}, s32[32]{0:T(128)}, u32[]{:S(2)}) copy-start(s32[32]{0:T(128)} %param.13) | copy-start | bytes 388
  31.6 6.6 %copy-start.9 = (bf16[2,4,32,128]{3,2,1,0:T(8,128)(2,1)S(1)}, bf16[2,4,32,128]{3,2,1,0:T(8,128)(2,1)}, u32[]{:S(2)}) copy-start(bf16[2,4,32,128]{3,2,1,0:T(8,128)(2,1)} %param.11) | copy-start | bytes 196612
  31.6 24.0 %collective-permute-start.8 = (bf16[4,2,2,256,128]{4,3,2,1,0:T(8,128)(2,1)S(1)}, bf16[4,2,2,256,128]{4,3,2,1,0:T(8,128)(2,1)}, u32[]{:S(2)}, u32[]{:S(2)}) collective-permute-start(bf16[4,2,2,256,128]{4,3,2,1,0:T(8,128)(2,1)S(1)} %pad_maximum_fusion.1.refs_3_), channel_id=1, source_target_pairs={{32,0},{33,1},{34,2},{35,3},{36,4},{37,5},{38,6},{39,7},{104,8},{1... | collective-permute-start | bytes 3145736 | tf_op jit(solution)/shard_map/ppermute | solution.py:57
  31.8 32.0 %collective-permute-start.13 = (bf16[4,2,2,256,128]{4,3,2,1,0:T(8,128)(2,1)S(1)}, bf16[4,2,2,256,128]{4,3,2,1,0:T(8,128)(2,1)}, u32[]{:S(2)}, u32[]{:S(2)}) collective-permute-start(bf16[4,2,2,256,128]{4,3,2,1,0:T(8,128)(2,1)S(1)} %pad_maximum_fusion.1.refs_3_), channel_id=1, source_target_pairs={{96,0},{97,1},{98,2},{99,3},{100,4},{101,5},{102,6},{103,7},{40,8}... | collective-permute-start | bytes 3145736 | tf_op jit(solution)/shard_map/ppermute | solution.py:57
  34.0 21.7 %collective-permute-start.5 = (bf16[4,2,2,256,128]{4,3,2,1,0:T(8,128)(2,1)}, bf16[4,2,2,256,128]{4,3,2,1,0:T(8,128)(2,1)}, u32[]{:S(2)}, u32[]{:S(2)}) collective-permute-start(bf16[4,2,2,256,128]{4,3,2,1,0:T(8,128)(2,1)} %pad_maximum_fusion.refs_2_), channel_id=1, source_target_pairs={{2,0},{3,1},{0,2},{1,3},{6,4},{7,5},{4,6},{5,7},{14,8},{15,9},{12,... | collective-permute-start | bytes 3145736 | tf_op jit(solution)/shard_map/ppermute | solution.py:57
  36.5 30.4 %collective-permute-start.12 = (bf16[4,2,2,256,128]{4,3,2,1,0:T(8,128)(2,1)}, bf16[4,2,2,256,128]{4,3,2,1,0:T(8,128)(2,1)}, u32[]{:S(2)}, u32[]{:S(2)}) collective-permute-start(bf16[4,2,2,256,128]{4,3,2,1,0:T(8,128)(2,1)} %pad_maximum_fusion.refs_2_), channel_id=1, source_target_pairs={{6,0},{7,1},{4,2},{5,3},{2,4},{3,5},{0,6},{1,7},{10,8},{11,9},{8,1... | collective-permute-start | bytes 3145736 | tf_op jit(solution)/shard_map/ppermute | solution.py:57
  44.4 25.5 %collective-permute-start.1 = (bf16[256,2048]{1,0:T(8,128)(2,1)S(1)}, bf16[256,2048]{1,0:T(8,128)(2,1)S(1)}, u32[]{:S(2)}, u32[]{:S(2)}) collective-permute-start(bf16[256,2048]{1,0:T(8,128)(2,1)S(1)} %copy-done.3), channel_id=1, source_target_pairs={{16,0},{17,1},{18,2},{19,3},{20,4},{21,5},{22,6},{23,7},{24,8},{25... | collective-permute-start | bytes 3145736 | tf_op jit(solution)/shard_map/ppermute | solution.py:371
  55.7 14.2 %collective-permute-start.14 = (bf16[256,2048]{1,0:T(8,128)(2,1)}, bf16[256,2048]{1,0:T(8,128)(2,1)S(1)}, u32[]{:S(2)}, u32[]{:S(2)}) collective-permute-start(bf16[256,2048]{1,0:T(8,128)(2,1)} %collective-permute-done.11), channel_id=1, source_target_pairs={{8,0},{9,1},{10,2},{11,3},{12,4},{13,5},{14,6},{15,7},{0,8},{1,9},... | collective-permute-start | bytes 3145736 | tf_op jit(solution)/shard_map/ppermute | solution.py:402
  62.4 14.2 %collective-permute-start.9 = (bf16[4,2,2,256,128]{4,3,2,1,0:T(8,128)(2,1)}, bf16[4,2,2,256,128]{4,3,2,1,0:T(8,128)(2,1)S(1)}, u32[]{:S(2)}, u32[]{:S(2)}) collective-permute-start(bf16[4,2,2,256,128]{4,3,2,1,0:T(8,128)(2,1)} %collective-permute-done.8.refs_3_.refs_5_), channel_id=1, source_target_pairs={{96,0},{97,1},{98,2},{99,3},{100,4},{101,5},{102,6},{103,7},{40,8}... | collective-permute-start | bytes 3145736 | tf_op jit(solution)/shard_map/ppermute | solution.py:57
  63.8 14.2 %collective-permute-start.6 = (bf16[4,2,2,256,128]{4,3,2,1,0:T(8,128)(2,1)}, bf16[4,2,2,256,128]{4,3,2,1,0:T(8,128)(2,1)S(1)}, u32[]{:S(2)}, u32[]{:S(2)}) collective-permute-start(bf16[4,2,2,256,128]{4,3,2,1,0:T(8,128)(2,1)} %collective-permute-done.5.refs_2_.refs_4_), channel_id=1, source_target_pairs={{6,0},{7,1},{4,2},{5,3},{2,4},{3,5},{0,6},{1,7},{10,8},{11,9},{8,1... | collective-permute-start | bytes 3145736 | tf_op jit(solution)/shard_map/ppermute | solution.py:57
  79.8 7.3 %collective-permute-start.15 = (bf16[2,2,8,256,128]{4,3,2,1,0:T(8,128)(2,1)S(1)}, bf16[2,2,8,256,128]{4,3,2,1,0:T(8,128)(2,1)S(1)}, u32[]{:S(2)}, u32[]{:S(2)}) collective-permute-start(bf16[2,2,8,256,128]{4,3,2,1,0:T(8,128)(2,1)S(1)} %shard_map.100), channel_id=1, source_target_pairs={{8,0},{9,1},{10,2},{11,3},{12,4},{13,5},{14,6},{15,7},{0,8},{1,9},... | collective-permute-start | bytes 6291464 | tf_op jit(solution)/shard_map/ppermute | solution.py:410
  (3 other events, 3.0 us)

commit v5 on v4

--- a/solution.py
+++ b/solution.py
@@ -368,6 +368,7 @@
     )
     weight, own_rows = together(weight, own_rows)
     corner_rows = lax.ppermute(to_corner, AXES, flipped(y=1))
+    corner_rows, to_across = together(corner_rows, to_across)
     across_rows = lax.ppermute(to_across, AXES, flipped(y=1))
     side_rows = lax.ppermute(to_side, AXES, flipped(core=1))
     middle, last = (Z, X), (X, Z)
@@ -394,12 +395,12 @@
     padding = ((0, 0), (0, 8 - STEPS), (0, 0))
     fresh_keys = jnp.pad(rotated(fresh[0], step_cos, step_sin), padding)
     fresh_values = jnp.pad(new_kv[1].transpose(1, 0, 2), padding)
+    corner_rows = lax.ppermute(corner_rows, AXES, flipped(core=1))
     own, side = product(spot, [own_rows, side_rows], blocks, (0,))
     far = [swap(block, dim, 1) for block, dim in zip(one, last)]
     one, corner_rows, own, side, query, fresh_keys, fresh_values, angles = together(
         one, corner_rows, own, side, query, fresh_keys, fresh_values, angles
     )
-    corner_rows = lax.ppermute(corner_rows, AXES, flipped(core=1))
 
     own, side = product(spot, [own_rows, side_rows], one, (1,), [own, side])
     spot_two, own, side = together(spot, own, side)

time: 137 us -> 144 us (1.051)
  waiting for transfers between devices: 25.2 us -> 34.1 us
  starting transfers between devices: 26.4 us -> 24.1 us
  blocking collectives: 43.4 us -> 45.1 us
    ppermute x1, waiting for transfers between devices: 0.01 us -> 10.4 us  [shards(): across_rows = lax.ppermute(to_across, AXES, flipped(y=1))]
    ppermute x10, waiting for transfers between devices: 23.5 us -> 15.5 us  [swap(): return lax.ppermute(value, AXES, exchange(dim, step))]
    ppermute x1, waiting for transfers between devices: 0.01 us -> 6.39 us  [shards(): corner_rows = lax.ppermute(to_corner, AXES, flipped(y=1))]
    all_to_all x1, blocking collectives: 30.4 us -> 32.2 us  [shards(): received = lax.all_to_all(rows, ('ylo', 'x', 'yhi'), 0, 0)]
    ppermute x1, starting transfers between devices: 6.7 us -> 5.23 us  [shards(): corner_rows = lax.ppermute(corner_rows, AXES, flipped(core=1))]
where the time goes in v5:
time: 144 us
  blocking collectives  45.1 us (31%)
  waiting for transfers between devices  34.1 us (24%)
  Pallas kernels  30.2 us (21%)
  starting transfers between devices  24.1 us (17%)
  other arithmetic  6.86 us (5%)
  local copies, waits for them, and re-layouts  2.6 us (2%)
    all_to_all x1, blocking collectives, shards(): received = lax.all_to_all(rows, ('ylo', 'x', 'yhi'), 0, 0)  32.2 us
    pallas_call x6, Pallas kernels, product(): pl.pallas_call(functools.partial(product_kernel, slots, count, carried, n...  18.4 us
    ppermute x10, waiting for transfers between devices, swap(): return lax.ppermute(value, AXES, exchange(dim, step))  15.5 us
    all_to_all x1, blocking collectives, shards(): parts = lax.all_to_all(packed, SEQ, 0, 0)  12.9 us
    ppermute x10, starting transfers between devices, swap(): return lax.ppermute(value, AXES, exchange(dim, step))  11.4 us
    ppermute x1, waiting for transfers between devices, shards(): across_rows = lax.ppermute(to_across, AXES, flipped(y=1))  10.4 us
    ppermute x1, waiting for transfers between devices, shards(): corner_rows = lax.ppermute(to_corner, AXES, flipped(y=1))  6.39 us
    pallas_call x1, Pallas kernels, prep(): pl.pallas_call(prep_kernel, out_shape=[jax.ShapeDtypeStruct((256, 2048),...  5.89 us
  transfers between devices with their start and end apart: 16, of which 7 were waited for; matrix products, arithmetic and copies ran while one was open for 6% of the time, Pallas kernels for 16%

profile of v5, /device:TPU:1, one launch (start us, length us, event | category | flops | bytes accessed | tf_op | source)
XLA Modules:
  0.0 144.0 jit_solution(604951514740533594)
XLA Ops:
  0.6 3.8 %collective-permute-start = (bf16[2,512,128]{2,1,0:T(8,128)(2,1)}, bf16[2,512,128]{2,1,0:T(8,128)(2,1)S(1)}, u32[]{:S(2)}, u32[]{:S(2)}) collective-permute-start(bf16[2,512,128]{2,1,0:T(8,128)(2,1)} %param.9), channel_id=1, source_target_pairs={{1,0},{0,1},{3,2},{2,3},{5,4},{4,5},{7,6},{6,7},{9,8},{8,9},{11,10... | collective-permute-start | bytes 786440 | tf_op jit(solution)/shard_map/ppermute | solution.py:365
  5.3 5.9 %shard_map.94 = (bf16[256,2048]{1,0:T(8,128)(2,1)S(1)}, bf16[256,2048]{1,0:T(8,128)(2,1)}, bf16[256,2048]{1,0:T(8,128)(2,1)S(1)}, bf16[256,2048]{1,0:T(8,128)(2,1)}) custom-call(s32[5]{0:T(128)S(1)} %stack.50.spot, bf16[256,8192]{1,0:T(8,128)(2,1)} %bitcast.52, f32[1,8192]{1,0:T(1,128)S(1)} %bitcast.49), custom_call_target="tpu_custom_call" | custom-call | flops 1000000 | bytes 262144 | tf_op jit(solution)/shard_map/pallas_call | solution.py:135
  11.5 3.8 %collective-permute-start.3 = (bf16[2,2,256,128]{3,2,1,0:T(8,128)(2,1)S(1)}, bf16[2,2,256,128]{3,2,1,0:T(8,128)(2,1)S(1)}, u32[]{:S(2)}, u32[]{:S(2)}) collective-permute-start(bf16[2,2,256,128]{3,2,1,0:T(8,128)(2,1)S(1)} %get-tuple-element.100), channel_id=1, source_target_pairs={{32,0},{33,1},{34,2},{35,3},{36,4},{37,5},{38,6},{39,7},{104,8},{1... | collective-permute-start | bytes 786440 | tf_op jit(solution)/shard_map/ppermute | solution.py:57
  15.3 2.5 %collective-permute-start.4 = (bf16[2,2,256,128]{3,2,1,0:T(8,128)(2,1)S(1)}, bf16[2,2,256,128]{3,2,1,0:T(8,128)(2,1)S(1)}, u32[]{:S(2)}, u32[]{:S(2)}) collective-permute-start(bf16[2,2,256,128]{3,2,1,0:T(8,128)(2,1)S(1)} %get-tuple-element.99), channel_id=1, source_target_pairs={{2,0},{3,1},{0,2},{1,3},{6,4},{7,5},{4,6},{5,7},{14,8},{15,9},{12,... | collective-permute-start | bytes 786440 | tf_op jit(solution)/shard_map/ppermute | solution.py:57
  19.1 2.7 %collective-permute-done.4 = bf16[2,2,256,128]{3,2,1,0:T(8,128)(2,1)S(1)} collective-permute-done((bf16[2,2,256,128]{3,2,1,0:T(8,128)(2,1)S(1)}, bf16[2,2,256,128]{3,2,1,0:T(8,128)(2,1)S(1)}, u32[]{:S(2)}, u32[]{:S(2)}) %collective-permute-start.4) | collective-permute-done | bytes 262176 | tf_op jit(solution)/shard_map/ppermute | solution.py:57
  23.7 6.6 %collective-permute-done.8 = bf16[2,2,2,256,128]{4,3,2,1,0:T(8,128)(2,1)} collective-permute-done((bf16[2,2,2,256,128]{4,3,2,1,0:T(8,128)(2,1)S(1)}, bf16[2,2,2,256,128]{4,3,2,1,0:T(8,128)(2,1)}, u32[]{:S(2)}, u32[]{:S(2)}) %collective-permute-start.8) | collective-permute-done | bytes 524320 | tf_op jit(solution)/shard_map/ppermute | solution.py:57
  31.8 2.1 %pad_maximum_fusion.refs_2_ = bf16[4,2,2,256,128]{4,3,2,1,0:T(8,128)(2,1)} fusion(bf16[2,2,2,256,128]{4,3,2,1,0:T(8,128)(2,1)} %collective-permute-done.5, bf16[1,2,2,256,128]{4,3,2,1,0:T(8,128)(2,1)S(1)} %bitcast.54, bf16[1,2,2,256,128]{4,3,2,1,0:T(8,128)(2,1)S(1)} %get-tuple-element.98), kind=kLoop, calls=%fused_computation | loop fusion | flops 1048576 | bytes 2097152 | tf_op jit(solution)/shard_map/concatenate | solution.py:380
  34.0 2.5 %collective-permute-start.6 = (bf16[4,2,2,256,128]{4,3,2,1,0:T(8,128)(2,1)}, bf16[4,2,2,256,128]{4,3,2,1,0:T(8,128)(2,1)}, u32[]{:S(2)}, u32[]{:S(2)}) collective-permute-start(bf16[4,2,2,256,128]{4,3,2,1,0:T(8,128)(2,1)} %pad_maximum_fusion.refs_2_), channel_id=1, source_target_pairs={{2,0},{3,1},{0,2},{1,3},{6,4},{7,5},{4,6},{5,7},{14,8},{15,9},{12,... | collective-permute-start | bytes 3145736 | tf_op jit(solution)/shard_map/ppermute | solution.py:57
  37.1 6.4 %collective-permute-done.1 = bf16[256,2048]{1,0:T(8,128)(2,1)} collective-permute-done((bf16[256,2048]{1,0:T(8,128)(2,1)}, bf16[256,2048]{1,0:T(8,128)(2,1)}, u32[]{:S(2)}, u32[]{:S(2)}) %collective-permute-start.1) | collective-permute-done | bytes 1048608 | tf_op jit(solution)/shard_map/ppermute | solution.py:370
  43.5 5.2 %collective-permute-start.12 = (bf16[256,2048]{1,0:T(8,128)(2,1)}, bf16[256,2048]{1,0:T(8,128)(2,1)S(1)}, u32[]{:S(2)}, u32[]{:S(2)}) collective-permute-start(bf16[256,2048]{1,0:T(8,128)(2,1)} %collective-permute-done.1), channel_id=1, source_target_pairs={{8,0},{9,1},{10,2},{11,3},{12,4},{13,5},{14,6},{15,7},{0,8},{1,9},... | collective-permute-start | bytes 3145736 | tf_op jit(solution)/shard_map/ppermute | solution.py:398
  50.8 4.9 %collective-permute-done.9.refs_3_.refs_5_ = bf16[4,2,2,256,128]{4,3,2,1,0:T(8,128)(2,1)} collective-permute-done((bf16[4,2,2,256,128]{4,3,2,1,0:T(8,128)(2,1)S(1)}, bf16[4,2,2,256,128]{4,3,2,1,0:T(8,128)(2,1)}, u32[]{:S(2)}, u32[]{:S(2)}) %collective-permute-start.9) | collective-permute-done | bytes 1048608 | tf_op jit(solution)/shard_map/ppermute | solution.py:57
  55.7 1.9 %collective-permute-start.10 = (bf16[4,2,2,256,128]{4,3,2,1,0:T(8,128)(2,1)}, bf16[4,2,2,256,128]{4,3,2,1,0:T(8,128)(2,1)S(1)}, u32[]{:S(2)}, u32[]{:S(2)}) collective-permute-start(bf16[4,2,2,256,128]{4,3,2,1,0:T(8,128)(2,1)} %collective-permute-done.9.refs_3_.refs_5_), channel_id=1, source_target_pairs={{96,0},{97,1},{98,2},{99,3},{100,4},{101,5},{102,6},{103,7},{40,8}... | collective-permute-start | bytes 3145736 | tf_op jit(solution)/shard_map/ppermute | solution.py:57
  58.7 2.6 %shard_map.95 = (f32[2,8,256,128]{3,2,1,0:T(8,128)S(1)}, f32[2,8,256,128]{3,2,1,0:T(8,128)S(1)}) custom-call(s32[5]{0:T(128)S(1)} %stack.50.spot, bf16[256,2048]{1,0:T(8,128)(2,1)S(1)} %get-tuple-element.49.refs_0_, bf16[256,2048]{1,0:T(8,128)(2,1)S(1)} %collective-permute-done.11.refs_1_.refs_0_, bf16[4,2,2,256,128]{4,3,2,1,0:T(8,128)(2,1)} %pad_maximum_fusion.refs_2_, ...), custom_call_target="tpu_custom_call" | custom-call | flops 1000000 | bytes 262144 | tf_op jit(solution)/shard_map/pallas_call | solution.py:203
  62.0 3.0 %shard_map.96 = (f32[2,8,256,128]{3,2,1,0:T(8,128)S(1)}, f32[2,8,256,128]{3,2,1,0:T(8,128)S(1)}) custom-call(s32[5]{0:T(128)S(1)} %stack.50.spot, bf16[256,2048]{1,0:T(8,128)(2,1)S(1)} %get-tuple-element.49.refs_0_, bf16[256,2048]{1,0:T(8,128)(2,1)S(1)} %collective-permute-done.11.refs_1_.refs_0_, ...), custom_call_target="tpu_custom_call" | custom-call | flops 1000000 | bytes 262144 | tf_op jit(solution)/shard_map/pallas_call | solution.py:203
  65.0 3.0 %shard_map.97 = (f32[2,8,256,128]{3,2,1,0:T(8,128)S(1)}, f32[2,8,256,128]{3,2,1,0:T(8,128)S(1)}) custom-call(s32[5]{0:T(128)S(1)} %stack.50.spot, bf16[256,2048]{1,0:T(8,128)(2,1)S(1)} %get-tuple-element.49.refs_0_, bf16[256,2048]{1,0:T(8,128)(2,1)S(1)} %collective-permute-done.11.refs_1_.refs_0_, ...), custom_call_target="tpu_custom_call" | custom-call | flops 1000000 | bytes 262144 | tf_op jit(solution)/shard_map/pallas_call | solution.py:203
  68.0 10.4 %collective-permute-done.2.refs_1_ = bf16[256,2048]{1,0:T(8,128)(2,1)S(1)} collective-permute-done((bf16[256,2048]{1,0:T(8,128)(2,1)S(1)}, bf16[256,2048]{1,0:T(8,128)(2,1)S(1)}, u32[]{:S(2)}, u32[]{:S(2)}) %collective-permute-start.2) | collective-permute-done | bytes 1048608 | tf_op jit(solution)/shard_map/ppermute | solution.py:372
  78.5 6.0 %shard_map.98 = (f32[2,8,256,128]{3,2,1,0:T(8,128)S(1)}, f32[2,8,256,128]{3,2,1,0:T(8,128)S(1)}) custom-call(s32[5]{0:T(128)S(1)} %stack.50.spot, bf16[256,2048]{1,0:T(8,128)(2,1)S(1)} %collective-permute-done.12.refs_0_.refs_1_, bf16[256,2048]{1,0:T(8,128)(2,1)S(1)} %collective-permute-done.2.refs_1_, bf16[4,2,2,256,128]{4,3,2,1,0:T(8,128)(2,1)} %pad_maximum_fusion.refs_2_, ...), custom_call_target="tpu_custom_call" | custom-call | flops 1000000 | bytes 262144 | tf_op jit(solution)/shard_map/pallas_call | solution.py:203
  84.5 1.9 %shard_map.100 = bf16[2,2,8,256,128]{4,3,2,1,0:T(8,128)(2,1)S(1)} custom-call(s32[5]{0:T(128)S(1)} %stack.50.spot, bf16[256,2048]{1,0:T(8,128)(2,1)S(1)} %collective-permute-done.11.refs_1_.refs_0_, bf16[256,2048]{1,0:T(8,128)(2,1)S(1)} %collective-permute-done.12.refs_0_.refs_1_, bf16[4,2,2,256,128]{4,3,2,1,0:T(8,128)(2,1)S(1)} %collective-permute-done.7.refs_2_, ...), custom_call_target="tpu_custom_call" | custom-call | flops 1000000 | bytes 262144 | tf_op jit(solution)/shard_map/pallas_call | solution.py:203
  86.3 2.8 %collective-permute-start.15 = (bf16[2,2,8,256,128]{4,3,2,1,0:T(8,128)(2,1)S(1)}, bf16[2,2,8,256,128]{4,3,2,1,0:T(8,128)(2,1)S(1)}, u32[]{:S(2)}, u32[]{:S(2)}) collective-permute-start(bf16[2,2,8,256,128]{4,3,2,1,0:T(8,128)(2,1)S(1)} %shard_map.100), channel_id=1, source_target_pairs={{8,0},{9,1},{10,2},{11,3},{12,4},{13,5},{14,6},{15,7},{0,8},{1,9},... | collective-permute-start | bytes 6291464 | tf_op jit(solution)/shard_map/ppermute | solution.py:411
  89.2 2.0 %shard_map.99 = (f32[2,8,256,128]{3,2,1,0:T(8,128)S(1)}, f32[2,8,256,128]{3,2,1,0:T(8,128)S(1)}) custom-call(s32[5]{0:T(128)S(1)} %stack.50.spot, bf16[256,2048]{1,0:T(8,128)(2,1)S(1)} %get-tuple-element.49.refs_0_, bf16[256,2048]{1,0:T(8,128)(2,1)S(1)} %collective-permute-done.2.refs_1_, bf16[4,2,2,256,128]{4,3,2,1,0:T(8,128)(2,1)S(1)} %collective-permute-done.7.refs_2_, ...), custom_call_target="tpu_custom_call" | custom-call | flops 1000000 | bytes 262144 | tf_op jit(solution)/shard_map/pallas_call | solution.py:203
  94.4 32.2 %all_to_all.10.received = bf16[16,2,256,128]{3,2,1,0:T(8,128)(2,1)S(1)} all-to-all(bf16[16,2,256,128]{3,2,1,0:T(8,128)(2,1)S(1)} %bitcast.48), channel_id=1, replica_groups=mesh['z'=4,'ylo'=2,'core'=2,'x'=4,'yhi'=2] {'ylo','x','yhi'}, dimensions={0} | all-to-all | bytes 4194304 | tf_op jit(solution)/shard_map/all_to_all | solution.py:414
  126.6 2.4 %shard_map.102 = (bf16[32,64,128]{2,1,0:T(8,128)(2,1)}, bf16[32,64,128]{2,1,0:T(8,128)(2,1)}, bf16[16,80,128]{2,1,0:T(8,128)(2,1)S(1)}) custom-call(s32[5]{0:T(128)S(1)} %stack.50.spot, s32[32]{0:T(128)S(1)} %copy-done.1, bf16[16,2,256,128]{3,2,1,0:T(8,128)(2,1)S(1)} %all_to_all.10.received, f32[32,32,128]{2,1,0:T(8,128)S(1)} %fusion.1.query, ...), custom_call_target="tpu_custom_call" | custom-call | flops 60000000 | bytes 4194304 | tf_op jit(solution)/shard_map/pallas_call | solution.py:314
  129.0 12.9 %all_to_all.11.parts = bf16[16,80,128]{2,1,0:T(8,128)(2,1)} all-to-all(bf16[16,80,128]{2,1,0:T(8,128)(2,1)S(1)} %get-tuple-element.92), channel_id=1, replica_groups=mesh['z'=4,'ylo'=2,'core'=2,'x'=4,'yhi'=2] {'z','ylo','core'}, dimensions={0} | all-to-all | bytes 655360 | tf_op jit(solution)/shard_map/all_to_all | solution.py:416
  142.0 2.0 %shard_map.103 = bf16[4,2,1024]{2,1,0:T(2,128)(2,1)} custom-call(bf16[16,80,128]{2,1,0:T(8,128)(2,1)} %all_to_all.11.parts), custom_call_target="tpu_custom_call" | custom-call | flops 300000 | bytes 1048576 | tf_op jit(solution)/shard_map/pallas_call | solution.py:350
  (71 shorter events, 13.4 us)
Async XLA Ops:
  0.6 10.6 %collective-permute-start = (bf16[2,512,128]{2,1,0:T(8,128)(2,1)}, bf16[2,512,128]{2,1,0:T(8,128)(2,1)S(1)}, u32[]{:S(2)}, u32[]{:S(2)}) collective-permute-start(bf16[2,512,128]{2,1,0:T(8,128)(2,1)} %param.9), channel_id=1, source_target_pairs={{1,0},{0,1},{3,2},{2,3},{5,4},{4,5},{7,6},{6,7},{9,8},{8,9},{11,10... | collective-permute-start | bytes 786440 | tf_op jit(solution)/shard_map/ppermute | solution.py:365
  5.3 5.9 %copy-start.8 = (bf16[2,512,128]{2,1,0:T(8,128)(2,1)S(1)}, bf16[2,512,128]{2,1,0:T(8,128)(2,1)}, u32[]{:S(2)}) copy-start(bf16[2,512,128]{2,1,0:T(8,128)(2,1)} %param.9) | copy-start | bytes 786436
  11.2 11.6 %copy-start.2 = (bf16[256,2048]{1,0:T(8,128)(2,1)}, bf16[256,2048]{1,0:T(8,128)(2,1)S(1)}, u32[]{:S(2)}) copy-start(bf16[256,2048]{1,0:T(8,128)(2,1)S(1)} %get-tuple-element.52) | copy-start | bytes 3145732
  11.5 11.3 %copy-start.4 = (bf16[1,2,2,256,128]{4,3,2,1,0:T(8,128)(2,1)}, bf16[1,2,2,256,128]{4,3,2,1,0:T(8,128)(2,1)S(1)}, u32[]{:S(2)}) copy-start(bf16[1,2,2,256,128]{4,3,2,1,0:T(8,128)(2,1)S(1)} %get-tuple-element.97) | copy-start | bytes 786436
  11.5 7.6 %collective-permute-start.3 = (bf16[2,2,256,128]{3,2,1,0:T(8,128)(2,1)S(1)}, bf16[2,2,256,128]{3,2,1,0:T(8,128)(2,1)S(1)}, u32[]{:S(2)}, u32[]{:S(2)}) collective-permute-start(bf16[2,2,256,128]{3,2,1,0:T(8,128)(2,1)S(1)} %get-tuple-element.100), channel_id=1, source_target_pairs={{32,0},{33,1},{34,2},{35,3},{36,4},{37,5},{38,6},{39,7},{104,8},{1... | collective-permute-start | bytes 786440 | tf_op jit(solution)/shard_map/ppermute | solution.py:57
  15.3 6.4 %collective-permute-start.4 = (bf16[2,2,256,128]{3,2,1,0:T(8,128)(2,1)S(1)}, bf16[2,2,256,128]{3,2,1,0:T(8,128)(2,1)S(1)}, u32[]{:S(2)}, u32[]{:S(2)}) collective-permute-start(bf16[2,2,256,128]{3,2,1,0:T(8,128)(2,1)S(1)} %get-tuple-element.99), channel_id=1, source_target_pairs={{2,0},{3,1},{0,2},{1,3},{6,4},{7,5},{4,6},{5,7},{14,8},{15,9},{12,... | collective-permute-start | bytes 786440 | tf_op jit(solution)/shard_map/ppermute | solution.py:57
  17.8 18.6 %collective-permute-start.11 = (bf16[256,2048]{1,0:T(8,128)(2,1)}, bf16[256,2048]{1,0:T(8,128)(2,1)S(1)}, u32[]{:S(2)}, u32[]{:S(2)}) collective-permute-start(bf16[256,2048]{1,0:T(8,128)(2,1)} %get-tuple-element.56), channel_id=1, source_target_pairs={{8,0},{9,1},{10,2},{11,3},{12,4},{13,5},{14,6},{15,7},{0,8},{1,9},... | collective-permute-start | bytes 3145736 | tf_op jit(solution)/shard_map/ppermute | solution.py:373
  21.8 8.5 %collective-permute-start.8 = (bf16[2,2,2,256,128]{4,3,2,1,0:T(8,128)(2,1)S(1)}, bf16[2,2,2,256,128]{4,3,2,1,0:T(8,128)(2,1)}, u32[]{:S(2)}, u32[]{:S(2)}) collective-permute-start(bf16[2,2,2,256,128]{4,3,2,1,0:T(8,128)(2,1)S(1)} %pad_maximum_fusion.4), channel_id=1, source_target_pairs={{6,0},{7,1},{4,2},{5,3},{2,4},{3,5},{0,6},{1,7},{10,8},{11,9},{8,1... | collective-permute-start | bytes 1572872 | tf_op jit(solution)/shard_map/ppermute | solution.py:57
  22.8 9.1 %collective-permute-start.5 = (bf16[2,2,2,256,128]{4,3,2,1,0:T(8,128)(2,1)}, bf16[2,2,2,256,128]{4,3,2,1,0:T(8,128)(2,1)}, u32[]{:S(2)}, u32[]{:S(2)}) collective-permute-start(bf16[2,2,2,256,128]{4,3,2,1,0:T(8,128)(2,1)} %pad_maximum_fusion.3), channel_id=1, source_target_pairs={{96,0},{97,1},{98,2},{99,3},{100,4},{101,5},{102,6},{103,7},{40,8}... | collective-permute-start | bytes 1572872 | tf_op jit(solution)/shard_map/ppermute | solution.py:57
  22.8 20.7 %collective-permute-start.1 = (bf16[256,2048]{1,0:T(8,128)(2,1)}, bf16[256,2048]{1,0:T(8,128)(2,1)}, u32[]{:S(2)}, u32[]{:S(2)}) collective-permute-start(bf16[256,2048]{1,0:T(8,128)(2,1)} %get-tuple-element.50), channel_id=1, source_target_pairs={{16,0},{17,1},{18,2},{19,3},{20,4},{21,5},{22,6},{23,7},{24,8},{25... | collective-permute-start | bytes 3145736 | tf_op jit(solution)/shard_map/ppermute | solution.py:370
  23.6 8.2 %copy-start.6 = (bf16[2,2,256,128]{3,2,1,0:T(8,128)(2,1)S(1)}, bf16[2,2,256,128]{3,2,1,0:T(8,128)(2,1)}, u32[]{:S(2)}) copy-start(bf16[2,2,256,128]{3,2,1,0:T(8,128)(2,1)} %copy-done.5) | copy-start | bytes 786436
  23.7 13.2 %copy-start.1 = (s32[32]{0:T(128)S(1)}, s32[32]{0:T(128)}, u32[]{:S(2)}) copy-start(s32[32]{0:T(128)} %lengths.1) | copy-start | bytes 388
  23.7 13.2 %copy-start.10 = (s32[32]{0:T(128)S(1)}, s32[32]{0:T(128)}, u32[]{:S(2)}) copy-start(s32[32]{0:T(128)} %param.13) | copy-start | bytes 388
  23.7 26.1 %copy-start.9 = (bf16[2,4,32,128]{3,2,1,0:T(8,128)(2,1)S(1)}, bf16[2,4,32,128]{3,2,1,0:T(8,128)(2,1)}, u32[]{:S(2)}) copy-start(bf16[2,4,32,128]{3,2,1,0:T(8,128)(2,1)} %param.11) | copy-start | bytes 196612
  31.6 24.0 %collective-permute-start.9 = (bf16[4,2,2,256,128]{4,3,2,1,0:T(8,128)(2,1)S(1)}, bf16[4,2,2,256,128]{4,3,2,1,0:T(8,128)(2,1)}, u32[]{:S(2)}, u32[]{:S(2)}) collective-permute-start(bf16[4,2,2,256,128]{4,3,2,1,0:T(8,128)(2,1)S(1)} %pad_maximum_fusion.1.refs_3_), channel_id=1, source_target_pairs={{32,0},{33,1},{34,2},{35,3},{36,4},{37,5},{38,6},{39,7},{104,8},{1... | collective-permute-start | bytes 3145736 | tf_op jit(solution)/shard_map/ppermute | solution.py:57
  31.8 33.2 %collective-permute-start.14 = (bf16[4,2,2,256,128]{4,3,2,1,0:T(8,128)(2,1)S(1)}, bf16[4,2,2,256,128]{4,3,2,1,0:T(8,128)(2,1)}, u32[]{:S(2)}, u32[]{:S(2)}) collective-permute-start(bf16[4,2,2,256,128]{4,3,2,1,0:T(8,128)(2,1)S(1)} %pad_maximum_fusion.1.refs_3_), channel_id=1, source_target_pairs={{96,0},{97,1},{98,2},{99,3},{100,4},{101,5},{102,6},{103,7},{40,8}... | collective-permute-start | bytes 3145736 | tf_op jit(solution)/shard_map/ppermute | solution.py:57
  34.0 21.7 %collective-permute-start.6 = (bf16[4,2,2,256,128]{4,3,2,1,0:T(8,128)(2,1)}, bf16[4,2,2,256,128]{4,3,2,1,0:T(8,128)(2,1)}, u32[]{:S(2)}, u32[]{:S(2)}) collective-permute-start(bf16[4,2,2,256,128]{4,3,2,1,0:T(8,128)(2,1)} %pad_maximum_fusion.refs_2_), channel_id=1, source_target_pairs={{2,0},{3,1},{0,2},{1,3},{6,4},{7,5},{4,6},{5,7},{14,8},{15,9},{12,... | collective-permute-start | bytes 3145736 | tf_op jit(solution)/shard_map/ppermute | solution.py:57
  36.5 28.6 %collective-permute-start.13 = (bf16[4,2,2,256,128]{4,3,2,1,0:T(8,128)(2,1)}, bf16[4,2,2,256,128]{4,3,2,1,0:T(8,128)(2,1)}, u32[]{:S(2)}, u32[]{:S(2)}) collective-permute-start(bf16[4,2,2,256,128]{4,3,2,1,0:T(8,128)(2,1)} %pad_maximum_fusion.refs_2_), channel_id=1, source_target_pairs={{6,0},{7,1},{4,2},{5,3},{2,4},{3,5},{0,6},{1,7},{10,8},{11,9},{8,1... | collective-permute-start | bytes 3145736 | tf_op jit(solution)/shard_map/ppermute | solution.py:57
  37.1 18.5 %copy-start.3 = (bf16[256,2048]{1,0:T(8,128)(2,1)S(1)}, bf16[256,2048]{1,0:T(8,128)(2,1)}, u32[]{:S(2)}) copy-start(bf16[256,2048]{1,0:T(8,128)(2,1)} %copy-done.2) | copy-start | bytes 3145732
  43.5 14.0 %collective-permute-start.12 = (bf16[256,2048]{1,0:T(8,128)(2,1)}, bf16[256,2048]{1,0:T(8,128)(2,1)S(1)}, u32[]{:S(2)}, u32[]{:S(2)}) collective-permute-start(bf16[256,2048]{1,0:T(8,128)(2,1)} %collective-permute-done.1), channel_id=1, source_target_pairs={{8,0},{9,1},{10,2},{11,3},{12,4},{13,5},{14,6},{15,7},{0,8},{1,9},... | collective-permute-start | bytes 3145736 | tf_op jit(solution)/shard_map/ppermute | solution.py:398
  55.6 22.8 %collective-permute-start.2 = (bf16[256,2048]{1,0:T(8,128)(2,1)S(1)}, bf16[256,2048]{1,0:T(8,128)(2,1)S(1)}, u32[]{:S(2)}, u32[]{:S(2)}) collective-permute-start(bf16[256,2048]{1,0:T(8,128)(2,1)S(1)} %copy-done.3), channel_id=1, source_target_pairs={{16,0},{17,1},{18,2},{19,3},{20,4},{21,5},{22,6},{23,7},{24,8},{25... | collective-permute-start | bytes 3145736 | tf_op jit(solution)/shard_map/ppermute | solution.py:372
  55.7 28.8 %collective-permute-start.10 = (bf16[4,2,2,256,128]{4,3,2,1,0:T(8,128)(2,1)}, bf16[4,2,2,256,128]{4,3,2,1,0:T(8,128)(2,1)S(1)}, u32[]{:S(2)}, u32[]{:S(2)}) collective-permute-start(bf16[4,2,2,256,128]{4,3,2,1,0:T(8,128)(2,1)} %collective-permute-done.9.refs_3_.refs_5_), channel_id=1, source_target_pairs={{96,0},{97,1},{98,2},{99,3},{100,4},{101,5},{102,6},{103,7},{40,8}... | collective-permute-start | bytes 3145736 | tf_op jit(solution)/shard_map/ppermute | solution.py:57
  57.6 26.9 %collective-permute-start.7 = (bf16[4,2,2,256,128]{4,3,2,1,0:T(8,128)(2,1)}, bf16[4,2,2,256,128]{4,3,2,1,0:T(8,128)(2,1)S(1)}, u32[]{:S(2)}, u32[]{:S(2)}) collective-permute-start(bf16[4,2,2,256,128]{4,3,2,1,0:T(8,128)(2,1)} %collective-permute-done.6.refs_2_.refs_4_), channel_id=1, source_target_pairs={{6,0},{7,1},{4,2},{5,3},{2,4},{3,5},{0,6},{1,7},{10,8},{11,9},{8,1... | collective-permute-start | bytes 3145736 | tf_op jit(solution)/shard_map/ppermute | solution.py:57
  86.3 6.6 %collective-permute-start.15 = (bf16[2,2,8,256,128]{4,3,2,1,0:T(8,128)(2,1)S(1)}, bf16[2,2,8,256,128]{4,3,2,1,0:T(8,128)(2,1)S(1)}, u32[]{:S(2)}, u32[]{:S(2)}) collective-permute-start(bf16[2,2,8,256,128]{4,3,2,1,0:T(8,128)(2,1)S(1)} %shard_map.100), channel_id=1, source_target_pairs={{8,0},{9,1},{10,2},{11,3},{12,4},{13,5},{14,6},{15,7},{0,8},{1,9},... | collective-permute-start | bytes 6291464 | tf_op jit(solution)/shard_map/ppermute | solution.py:411
  (3 other events, 5.4 us)
